TPU v7x, 32 devices: a whole 2x2x4 slice. The times are simulated.
32 devices in a mesh: groups: 2 (over x), seq: 16 (over z, y, core).
Axes of the slice: x: 2, y: 2, z: 4, core: 2. Of those that a mesh axis runs over, the one named last changes fastest.
Arguments:
- ssm_inputs: bfloat16 [4096, 2048], P(('groups', 'seq')), parts along dimension 0, may hold values from -6 to 6
- state_write: bfloat16 [4096, 128], P(('groups', 'seq')), parts along dimension 0, may hold values from -6 to 6
- state_read: bfloat16 [4096, 128], P(('groups', 'seq')), parts along dimension 0, may hold values from -6 to 6
- decay_codes: int32 [4096, 32], P(('groups', 'seq')), parts along dimension 0, may hold values from 0 to 4095, as said below
- decay_rate: float32 [32], replicated, as said below
- queries: bfloat16 [2, 4096, 2048], P(None, ('groups', 'seq')), parts along dimension 1, may hold values from -6 to 6
- keys_values: bfloat16 [2, 4096, 512], P(None, ('groups', 'seq')), parts along dimension 1, may hold values from -6 to 6
- segment_ids: int32 [4096], P(('groups', 'seq')), parts along dimension 0, may hold values from 0 to 3, never falling along the last dimension, each value on 1 to 1024 neighbouring positions
Outputs:
- ssm_output: bfloat16 [4096, 2048], P(('groups', 'seq')), parts along dimension 0
- attn_output: bfloat16 [2, 4096, 2048], P(None, ('groups', 'seq')), parts along dimension 1
There are 2 independent parts, one for each index of `groups`. A program takes and returns all parts, laid end to end along the dimension named above; an argument that names none is the same for every part. Nothing has to cross between parts.
Inputs may be any that keep to these rules, and one draw needn't show every extreme that they name: `decay_codes`: the low ten bits of a code scale a head's rate, the higher bits mark rare positions at which every head loses part of its state. `decay_rate`: every rate is positive.
All inputs are finite; a program needn't handle non-finite values.
Results may differ from a plain program's by a relative error of at most 0.0047.
Values may be sent and summed in bfloat16 or wider, within the bound.
No kernel may reach another device: no remote copies, remote signals or barrier semaphores. Data moves between devices by JAX's collectives and lax.ppermute only.
A program may use at most 192 MiB of HBM per device.

v0:
```python
import jax
import jax.numpy as jnp
from jax import lax
from jax.sharding import PartitionSpec as P

Q_HEADS = 16
KV_HEADS = 4
HEAD = 128
WINDOW = 1024


def entering(value, axis, join, neutral):
    count, mine = (lax.axis_size(axis), lax.axis_index(axis))
    pieces = jax.tree.map(lambda part: lax.all_gather(part, axis), value)
    running = jax.tree.map(
        lambda part, zero: jnp.full_like(part, 0) + jnp.asarray(zero, part.dtype), value, neutral
    )

    def lap(position, running):
        longer = join(running, jax.tree.map(lambda part: part[position], pieces))
        return jax.tree.map(lambda new, old: jnp.where(position < mine, new, old), longer, running)

    return lax.fori_loop(0, count - 1, lap, running)


def from_behind(block, axis, distance):
    devices = range(lax.axis_size(axis))
    route = [(i - distance, i) for i in devices if i - distance in devices]
    return lax.ppermute(block, axis, route)


def log_decay(codes, rates):
    lower = (codes % 1024).astype(jnp.float32)
    level = (codes // 1024).astype(jnp.float32)
    return -rates[None, :] * (1.0 + lower / 128.0) - 0.125 * level


def chain_combine(earlier, later):
    return (earlier[0] * later[0], later[0][:, None, None] * earlier[1] + later[1])


def shards(
    ssm_inputs, state_write, state_read, decay_codes, decay_rate, queries, keys_values, segment_ids
):
    row_count = ssm_inputs.shape[0]
    head_count = decay_rate.shape[0]
    head_width = ssm_inputs.shape[1] // head_count
    steps_log = log_decay(decay_codes, decay_rate)
    running = jnp.cumsum(steps_log, axis=0)
    trailing = running.T
    spread_log = trailing[:, :, None] - trailing[:, None, :]
    causal_pairs = lax.broadcasted_iota(
        jnp.int32, (row_count, row_count), 0
    ) >= lax.broadcasted_iota(jnp.int32, (row_count, row_count), 1)
    damping = jnp.where(causal_pairs[None], jnp.exp(jnp.minimum(spread_log, 0.0)), 0.0)
    inner_products = jnp.dot(state_read, state_write.T, preferred_element_type=jnp.float32)
    mixing = (inner_products[None] * damping).astype(jnp.bfloat16)
    inputs = ssm_inputs.reshape(row_count, head_count, head_width)
    local_part = jnp.einsum("hts,shp->thp", mixing, inputs, preferred_element_type=jnp.float32)
    to_block_end = jnp.exp(running[-1][None, :] - running)
    scaled = (to_block_end[:, :, None] * inputs).astype(jnp.bfloat16)
    contribution = jnp.einsum(
        "shp,sn->hpn", scaled, state_write, preferred_element_type=jnp.float32
    )
    total_decay = jnp.exp(running[-1])
    identity = (jnp.ones_like(total_decay), jnp.zeros_like(contribution))
    chained = entering((total_decay, contribution), "seq", chain_combine, identity)
    incoming = chained[1]
    carried = jnp.einsum(
        "tn,hpn->thp", state_read.astype(jnp.float32), incoming, precision=lax.Precision.HIGHEST
    )
    mixed = local_part + carried * jnp.exp(running)[:, :, None]
    mean_square = jnp.mean(mixed * mixed, axis=-1, keepdims=True)
    ssm_output = (
        (mixed * lax.rsqrt(mean_square + 1e-05))
        .reshape(row_count, head_count * head_width)
        .astype(jnp.bfloat16)
    )
    device_rank = lax.axis_index("seq")
    reach = WINDOW // row_count
    group_size = Q_HEADS // KV_HEADS
    own_segments = segment_ids.astype(jnp.bfloat16)[None, :]
    earlier = []
    moving = (keys_values, own_segments)
    for step in range(reach):
        moving = from_behind((moving[0], moving[1]), "seq", 1)
        earlier.append(moving)
    pieces = earlier[::-1] + [(keys_values, own_segments)]
    window_pairs = jnp.concatenate([piece[0] for piece in pieces], axis=1)
    window_segments = jnp.concatenate([piece[1][0] for piece in pieces], axis=0).astype(jnp.int32)
    span = window_pairs.shape[1]
    key_pos = (device_rank - reach) * row_count + lax.broadcasted_iota(jnp.int32, (span,), 0)
    query_pos = device_rank * row_count + lax.broadcasted_iota(jnp.int32, (row_count,), 0)
    allowed = (key_pos[None, :] <= query_pos[:, None]) & (
        key_pos[None, :] > query_pos[:, None] - WINDOW
    )
    allowed = allowed & (key_pos[None, :] >= 0) & (window_segments[None, :] == segment_ids[:, None])
    key_heads = jnp.transpose(window_pairs[0].reshape(span, KV_HEADS, HEAD), (1, 0, 2))
    value_heads = jnp.transpose(window_pairs[1].reshape(span, KV_HEADS, HEAD), (1, 0, 2))
    query_heads = jnp.transpose(
        queries.reshape(2, row_count, KV_HEADS, group_size, HEAD), (0, 2, 3, 1, 4)
    )
    query_heads = query_heads.reshape(2 * KV_HEADS, group_size, row_count, HEAD)

    def attend_item(item):
        item_queries, item_index = item
        head_keys = key_heads[item_index % KV_HEADS]
        head_values = value_heads[item_index % KV_HEADS]
        scores = jnp.einsum(
            "gqd,kd->gqk", item_queries, head_keys, preferred_element_type=jnp.float32
        ) * HEAD ** (-0.5)
        masked = jnp.where(allowed[None], scores, -1e30)
        peak = jnp.max(masked, axis=-1, keepdims=True)
        probs = jnp.where(allowed[None], jnp.exp(masked - peak), 0.0)
        totals = jnp.sum(probs, axis=-1)
        weighted = jnp.einsum(
            "gqk,kd->gqd",
            probs.astype(jnp.bfloat16),
            head_values,
            preferred_element_type=jnp.float32,
        )
        return weighted / totals[..., None]

    results = lax.map(attend_item, (query_heads, jnp.arange(2 * KV_HEADS, dtype=jnp.int32)))
    results = jnp.transpose(
        results.reshape(2, KV_HEADS, group_size, row_count, HEAD), (0, 3, 1, 2, 4)
    )
    attn_output = results.reshape(2, row_count, Q_HEADS * HEAD).astype(jnp.bfloat16)
    return (ssm_output, attn_output)


def solution(mesh):
    return jax.shard_map(
        shards,
        mesh=mesh,
        in_specs=(
            P(("groups", "seq"), None),
            P(("groups", "seq"), None),
            P(("groups", "seq"), None),
            P(("groups", "seq"), None),
            P(),
            P(None, ("groups", "seq"), None),
            P(None, ("groups", "seq"), None),
            P(("groups", "seq")),
        ),
        out_specs=(P(("groups", "seq"), None), P(None, ("groups", "seq"), None)),
        check_vma=False,
    )
```

profile of v0, /device:TPU:1, one launch (start us, length us, event | category | flops | bytes accessed | tf_op | source)
XLA Modules:
  0.0 288.0 jit_solution(11623118376654881412)
XLA Ops:
  7.3 1.3 copy.36
  10.4 2.1 fusion.67
  12.7 4.5 %collective-permute-start.8 = (bf16[2,128,512]{1,2,0:T(8,128)(2,1)S(1)}, bf16[2,128,512]{1,2,0:T(8,128)(2,1)S(1)}, u32[]{:S(2)}, u32[]{:S(2)}) collective-permute-start(bf16[2,128,512]{1,2,0:T(8,128)(2,1)S(1)} %copy.40), channel_id=1, source_target_pairs={{0,1},{1,2},{2,3},{3,4},{4,5},{5,6},{6,7},{7,8},{8,9},{9,10},{10,1... | collective-permute-start | bytes 786440 | tf_op jit(solution)/shard_map/ppermute | solution.py:29
  17.3 3.3 %collective-permute-done.8 = bf16[2,128,512]{1,2,0:T(8,128)(2,1)S(1)} collective-permute-done((bf16[2,128,512]{1,2,0:T(8,128)(2,1)S(1)}, bf16[2,128,512]{1,2,0:T(8,128)(2,1)S(1)}, u32[]{:S(2)}, u32[]{:S(2)}) %collective-permute-start.8) | collective-permute-done | bytes 262176 | tf_op jit(solution)/shard_map/ppermute | solution.py:29
  20.6 4.4 %collective-permute-start.9 = (bf16[2,128,512]{1,2,0:T(8,128)(2,1)S(1)}, bf16[2,128,512]{1,2,0:T(8,128)(2,1)S(1)}, u32[]{:S(2)}, u32[]{:S(2)}) collective-permute-start(bf16[2,128,512]{1,2,0:T(8,128)(2,1)S(1)} %collective-permute-done.8), channel_id=1, source_target_pairs={{0,1},{1,2},{2,3},{3,4},{4,5},{5,6},{6,7},{7,8},{8,9},{9,10},{10,1... | collective-permute-start | bytes 786440 | tf_op jit(solution)/shard_map/ppermute | solution.py:29
  24.9 8.8 %collective-permute-done.9 = bf16[2,128,512]{1,2,0:T(8,128)(2,1)S(1)} collective-permute-done((bf16[2,128,512]{1,2,0:T(8,128)(2,1)S(1)}, bf16[2,128,512]{1,2,0:T(8,128)(2,1)S(1)}, u32[]{:S(2)}, u32[]{:S(2)}) %collective-permute-start.9) | collective-permute-done | bytes 262176 | tf_op jit(solution)/shard_map/ppermute | solution.py:29
  33.7 4.4 %collective-permute-start.10 = (bf16[2,128,512]{1,2,0:T(8,128)(2,1)S(1)}, bf16[2,128,512]{1,2,0:T(8,128)(2,1)S(1)}, u32[]{:S(2)}, u32[]{:S(2)}) collective-permute-start(bf16[2,128,512]{1,2,0:T(8,128)(2,1)S(1)} %collective-permute-done.9), channel_id=1, source_target_pairs={{0,1},{1,2},{2,3},{3,4},{4,5},{5,6},{6,7},{7,8},{8,9},{9,10},{10,1... | collective-permute-start | bytes 786440 | tf_op jit(solution)/shard_map/ppermute | solution.py:29
  38.1 3.3 %collective-permute-done.10 = bf16[2,128,512]{1,2,0:T(8,128)(2,1)S(1)} collective-permute-done((bf16[2,128,512]{1,2,0:T(8,128)(2,1)S(1)}, bf16[2,128,512]{1,2,0:T(8,128)(2,1)S(1)}, u32[]{:S(2)}, u32[]{:S(2)}) %collective-permute-start.10) | collective-permute-done | bytes 262176 | tf_op jit(solution)/shard_map/ppermute | solution.py:29
  41.4 4.4 %collective-permute-start.11 = (bf16[2,128,512]{1,2,0:T(8,128)(2,1)S(1)}, bf16[2,128,512]{1,2,0:T(8,128)(2,1)S(1)}, u32[]{:S(2)}, u32[]{:S(2)}) collective-permute-start(bf16[2,128,512]{1,2,0:T(8,128)(2,1)S(1)} %collective-permute-done.10), channel_id=1, source_target_pairs={{0,1},{1,2},{2,3},{3,4},{4,5},{5,6},{6,7},{7,8},{8,9},{9,10},{10,1... | collective-permute-start | bytes 786440 | tf_op jit(solution)/shard_map/ppermute | solution.py:29
  45.8 3.3 %collective-permute-done.11 = bf16[2,128,512]{1,2,0:T(8,128)(2,1)S(1)} collective-permute-done((bf16[2,128,512]{1,2,0:T(8,128)(2,1)S(1)}, bf16[2,128,512]{1,2,0:T(8,128)(2,1)S(1)}, u32[]{:S(2)}, u32[]{:S(2)}) %collective-permute-start.11) | collective-permute-done | bytes 262176 | tf_op jit(solution)/shard_map/ppermute | solution.py:29
  49.1 6.3 %collective-permute-start.12 = (bf16[2,128,512]{1,2,0:T(8,128)(2,1)S(1)}, bf16[2,128,512]{1,2,0:T(8,128)(2,1)S(1)}, u32[]{:S(2)}, u32[]{:S(2)}) collective-permute-start(bf16[2,128,512]{1,2,0:T(8,128)(2,1)S(1)} %collective-permute-done.11), channel_id=1, source_target_pairs={{0,1},{1,2},{2,3},{3,4},{4,5},{5,6},{6,7},{7,8},{8,9},{9,10},{10,1... | collective-permute-start | bytes 786440 | tf_op jit(solution)/shard_map/ppermute | solution.py:29
  55.4 13.0 %collective-permute-start = (bf16[1,128]{1,0:T(2,128)(2,1)S(1)}, bf16[1,128]{1,0:T(2,128)(2,1)S(1)}, u32[]{:S(2)}, u32[]{:S(2)}) collective-permute-start(bf16[1,128]{1,0:T(2,128)(2,1)S(1)} %convert_bitcast_fusion), channel_id=1, source_target_pairs={{0,1},{1,2},{2,3},{3,4},{4,5},{5,6},{6,7},{7,8},{8,9},{9,10},{10,1... | collective-permute-start | bytes 776 | tf_op jit(solution)/shard_map/ppermute | solution.py:29
  68.5 5.3 %collective-permute-start.13 = (bf16[2,128,512]{1,2,0:T(8,128)(2,1)S(1)}, bf16[2,128,512]{1,2,0:T(8,128)(2,1)}, u32[]{:S(2)}, u32[]{:S(2)}) collective-permute-start(bf16[2,128,512]{1,2,0:T(8,128)(2,1)S(1)} %collective-permute-done.12), channel_id=1, source_target_pairs={{0,1},{1,2},{2,3},{3,4},{4,5},{5,6},{6,7},{7,8},{8,9},{9,10},{10,1... | collective-permute-start | bytes 786440 | tf_op jit(solution)/shard_map/ppermute | solution.py:29
  74.0 8.6 %collective-permute-done.13 = bf16[2,128,512]{1,2,0:T(8,128)(2,1)} collective-permute-done((bf16[2,128,512]{1,2,0:T(8,128)(2,1)S(1)}, bf16[2,128,512]{1,2,0:T(8,128)(2,1)}, u32[]{:S(2)}, u32[]{:S(2)}) %collective-permute-start.13) | collective-permute-done | bytes 262176 | tf_op jit(solution)/shard_map/ppermute | solution.py:29
  82.5 4.5 %collective-permute-start.14 = (bf16[2,128,512]{1,2,0:T(8,128)(2,1)}, bf16[2,128,512]{1,2,0:T(8,128)(2,1)}, u32[]{:S(2)}, u32[]{:S(2)}) collective-permute-start(bf16[2,128,512]{1,2,0:T(8,128)(2,1)} %collective-permute-done.13), channel_id=1, source_target_pairs={{0,1},{1,2},{2,3},{3,4},{4,5},{5,6},{6,7},{7,8},{8,9},{9,10},{10,1... | collective-permute-start | bytes 786440 | tf_op jit(solution)/shard_map/ppermute | solution.py:29
  88.0 4.1 %collective-permute-start.1 = (bf16[1,128]{1,0:T(2,128)(2,1)S(1)}, bf16[1,128]{1,0:T(2,128)(2,1)S(1)}, u32[]{:S(2)}, u32[]{:S(2)}) collective-permute-start(bf16[1,128]{1,0:T(2,128)(2,1)S(1)} %collective-permute-done), channel_id=1, source_target_pairs={{0,1},{1,2},{2,3},{3,4},{4,5},{5,6},{6,7},{7,8},{8,9},{9,10},{10,1... | collective-permute-start | bytes 776 | tf_op jit(solution)/shard_map/ppermute | solution.py:29
  92.1 4.1 %collective-permute-done.1 = bf16[1,128]{1,0:T(2,128)(2,1)S(1)} collective-permute-done((bf16[1,128]{1,0:T(2,128)(2,1)S(1)}, bf16[1,128]{1,0:T(2,128)(2,1)S(1)}, u32[]{:S(2)}, u32[]{:S(2)}) %collective-permute-start.1) | collective-permute-done | bytes 288 | tf_op jit(solution)/shard_map/ppermute | solution.py:29
  96.2 4.4 %collective-permute-start.2 = (bf16[1,128]{1,0:T(2,128)(2,1)S(1)}, bf16[1,128]{1,0:T(2,128)(2,1)S(1)}, u32[]{:S(2)}, u32[]{:S(2)}) collective-permute-start(bf16[1,128]{1,0:T(2,128)(2,1)S(1)} %collective-permute-done.1), channel_id=1, source_target_pairs={{0,1},{1,2},{2,3},{3,4},{4,5},{5,6},{6,7},{7,8},{8,9},{9,10},{10,1... | collective-permute-start | bytes 776 | tf_op jit(solution)/shard_map/ppermute | solution.py:29
  101.3 5.2 %collective-permute-start.3 = (bf16[1,128]{1,0:T(2,128)(2,1)S(1)}, bf16[1,128]{1,0:T(2,128)(2,1)S(1)}, u32[]{:S(2)}, u32[]{:S(2)}) collective-permute-start(bf16[1,128]{1,0:T(2,128)(2,1)S(1)} %collective-permute-done.2), channel_id=1, source_target_pairs={{0,1},{1,2},{2,3},{3,4},{4,5},{5,6},{6,7},{7,8},{8,9},{9,10},{10,1... | collective-permute-start | bytes 776 | tf_op jit(solution)/shard_map/ppermute | solution.py:29
  107.2 5.3 %collective-permute-start.4 = (bf16[1,128]{1,0:T(2,128)(2,1)S(1)}, bf16[1,128]{1,0:T(2,128)(2,1)S(1)}, u32[]{:S(2)}, u32[]{:S(2)}) collective-permute-start(bf16[1,128]{1,0:T(2,128)(2,1)S(1)} %collective-permute-done.3), channel_id=1, source_target_pairs={{0,1},{1,2},{2,3},{3,4},{4,5},{5,6},{6,7},{7,8},{8,9},{9,10},{10,1... | collective-permute-start | bytes 776 | tf_op jit(solution)/shard_map/ppermute | solution.py:29
  112.5 13.6 %collective-permute-start.15 = (bf16[2,128,512]{1,2,0:T(8,128)(2,1)}, bf16[2,128,512]{1,2,0:T(8,128)(2,1)}, u32[]{:S(2)}, u32[]{:S(2)}) collective-permute-start(bf16[2,128,512]{1,2,0:T(8,128)(2,1)} %collective-permute-done.14), channel_id=1, source_target_pairs={{0,1},{1,2},{2,3},{3,4},{4,5},{5,6},{6,7},{7,8},{8,9},{9,10},{10,1... | collective-permute-start | bytes 786440 | tf_op jit(solution)/shard_map/ppermute | solution.py:29
  126.1 8.3 %collective-permute-start.5 = (bf16[1,128]{1,0:T(2,128)(2,1)S(1)}, bf16[1,128]{1,0:T(2,128)(2,1)S(1)}, u32[]{:S(2)}, u32[]{:S(2)}) collective-permute-start(bf16[1,128]{1,0:T(2,128)(2,1)S(1)} %collective-permute-done.4), channel_id=1, source_target_pairs={{0,1},{1,2},{2,3},{3,4},{4,5},{5,6},{6,7},{7,8},{8,9},{9,10},{10,1... | collective-permute-start | bytes 776 | tf_op jit(solution)/shard_map/ppermute | solution.py:29
  134.4 33.1 %all-gather.1 = f32[16,1,32]{2,1,0:T(1,128)S(1)} all-gather(f32[1,1,32]{2,1,0:T(1,128)S(1)} %get-tuple-element.307), channel_id=1, replica_groups=mesh['groups'=2,'seq'=16] {'seq'}, dimensions={0}, use_global_device_ids=true | all-gather | bytes 2176 | tf_op jit(solution)/shard_map/all_gather | solution.py:14
  167.5 1.9 collective-permute-start.6
  169.5 1.1 collective-permute-done.6
  170.5 3.9 %collective-permute-start.7 = (bf16[1,128]{1,0:T(2,128)(2,1)S(1)}, bf16[1,128]{1,0:T(2,128)(2,1)S(1)}, u32[]{:S(2)}, u32[]{:S(2)}) collective-permute-start(bf16[1,128]{1,0:T(2,128)(2,1)S(1)} %collective-permute-done.6), channel_id=1, source_target_pairs={{0,1},{1,2},{2,3},{3,4},{4,5},{5,6},{6,7},{7,8},{8,9},{9,10},{10,1... | collective-permute-start | bytes 776 | tf_op jit(solution)/shard_map/ppermute | solution.py:29
  174.6 1.8 reshape.145
  176.4 1.2 copy.39
  184.7 1.2 fusion.88
  186.0 67.1 %while.27 = (s32[]{:T(128)}, bf16[8,4,128,128]{3,2,1,0:T(8,128)(2,1)}, bf16[8,4,128,128]{3,2,1,0:T(8,128)(2,1)}, s32[8]{0:T(128)S(1)}, bf16[4,1152,128]{1,2,0:T(...) while((s32[]{:T(128)}, ...), condition=%wide.region_7.8_spmd.clone, body=%wide.region_4.7_spmd.clone.sunk | while | flops 459836160 | bytes 2164672 | solution.py:124
  188.8 2.3 fusion.110
  191.1 3.2 %fusion.111 = bf16[8,4,128,128]{3,2,1,0:T(8,128)(2,1)} fusion(bf16[8,4,128,128]{3,2,1,0:T(8,128)(2,1)} %get-tuple-element.454, s32[]{:T(128)S(6)} %copy.76, bf16[4,1152,128]{1,2,0:T(8,128)(2,1)S(1)} %get-tuple-element.474, s32[]{:T(128)S(6)} %select_n.129, pred[128,1152]{1,0:T(8,128)(4,1)S(1)} %compare_and_fusion.2, ...), kind=kOutput, calls=%fused_computation.11.clone.1 | convolution fusion | flops 305006208 | bytes 1282048 | tf_op jit(solution)/shard_map/while/body/eval_jaxpr/gqk,kd->gqd/dot_general | solution.py:116
  197.2 2.3 fusion.110
  199.5 3.2 %fusion.111 = bf16[8,4,128,128]{3,2,1,0:T(8,128)(2,1)} fusion(bf16[8,4,128,128]{3,2,1,0:T(8,128)(2,1)} %get-tuple-element.454, s32[]{:T(128)S(6)} %copy.76, bf16[4,1152,128]{1,2,0:T(8,128)(2,1)S(1)} %get-tuple-element.474, s32[]{:T(128)S(6)} %select_n.129, pred[128,1152]{1,0:T(8,128)(4,1)S(1)} %compare_and_fusion.2, ...), kind=kOutput, calls=%fused_computation.11.clone.1 | convolution fusion | flops 305006208 | bytes 1282048 | tf_op jit(solution)/shard_map/while/body/eval_jaxpr/gqk,kd->gqd/dot_general | solution.py:116
  205.5 2.3 fusion.110
  207.9 3.2 %fusion.111 = bf16[8,4,128,128]{3,2,1,0:T(8,128)(2,1)} fusion(bf16[8,4,128,128]{3,2,1,0:T(8,128)(2,1)} %get-tuple-element.454, s32[]{:T(128)S(6)} %copy.76, bf16[4,1152,128]{1,2,0:T(8,128)(2,1)S(1)} %get-tuple-element.474, s32[]{:T(128)S(6)} %select_n.129, pred[128,1152]{1,0:T(8,128)(4,1)S(1)} %compare_and_fusion.2, ...), kind=kOutput, calls=%fused_computation.11.clone.1 | convolution fusion | flops 305006208 | bytes 1282048 | tf_op jit(solution)/shard_map/while/body/eval_jaxpr/gqk,kd->gqd/dot_general | solution.py:116
  213.9 2.3 fusion.110
  216.3 3.2 %fusion.111 = bf16[8,4,128,128]{3,2,1,0:T(8,128)(2,1)} fusion(bf16[8,4,128,128]{3,2,1,0:T(8,128)(2,1)} %get-tuple-element.454, s32[]{:T(128)S(6)} %copy.76, bf16[4,1152,128]{1,2,0:T(8,128)(2,1)S(1)} %get-tuple-element.474, s32[]{:T(128)S(6)} %select_n.129, pred[128,1152]{1,0:T(8,128)(4,1)S(1)} %compare_and_fusion.2, ...), kind=kOutput, calls=%fused_computation.11.clone.1 | convolution fusion | flops 305006208 | bytes 1282048 | tf_op jit(solution)/shard_map/while/body/eval_jaxpr/gqk,kd->gqd/dot_general | solution.py:116
  222.3 2.3 fusion.110
  224.7 3.2 %fusion.111 = bf16[8,4,128,128]{3,2,1,0:T(8,128)(2,1)} fusion(bf16[8,4,128,128]{3,2,1,0:T(8,128)(2,1)} %get-tuple-element.454, s32[]{:T(128)S(6)} %copy.76, bf16[4,1152,128]{1,2,0:T(8,128)(2,1)S(1)} %get-tuple-element.474, s32[]{:T(128)S(6)} %select_n.129, pred[128,1152]{1,0:T(8,128)(4,1)S(1)} %compare_and_fusion.2, ...), kind=kOutput, calls=%fused_computation.11.clone.1 | convolution fusion | flops 305006208 | bytes 1282048 | tf_op jit(solution)/shard_map/while/body/eval_jaxpr/gqk,kd->gqd/dot_general | solution.py:116
  230.7 2.3 fusion.110
  233.0 3.2 %fusion.111 = bf16[8,4,128,128]{3,2,1,0:T(8,128)(2,1)} fusion(bf16[8,4,128,128]{3,2,1,0:T(8,128)(2,1)} %get-tuple-element.454, s32[]{:T(128)S(6)} %copy.76, bf16[4,1152,128]{1,2,0:T(8,128)(2,1)S(1)} %get-tuple-element.474, s32[]{:T(128)S(6)} %select_n.129, pred[128,1152]{1,0:T(8,128)(4,1)S(1)} %compare_and_fusion.2, ...), kind=kOutput, calls=%fused_computation.11.clone.1 | convolution fusion | flops 305006208 | bytes 1282048 | tf_op jit(solution)/shard_map/while/body/eval_jaxpr/gqk,kd->gqd/dot_general | solution.py:116
  239.1 2.3 fusion.110
  241.4 3.2 %fusion.111 = bf16[8,4,128,128]{3,2,1,0:T(8,128)(2,1)} fusion(bf16[8,4,128,128]{3,2,1,0:T(8,128)(2,1)} %get-tuple-element.454, s32[]{:T(128)S(6)} %copy.76, bf16[4,1152,128]{1,2,0:T(8,128)(2,1)S(1)} %get-tuple-element.474, s32[]{:T(128)S(6)} %select_n.129, pred[128,1152]{1,0:T(8,128)(4,1)S(1)} %compare_and_fusion.2, ...), kind=kOutput, calls=%fused_computation.11.clone.1 | convolution fusion | flops 305006208 | bytes 1282048 | tf_op jit(solution)/shard_map/while/body/eval_jaxpr/gqk,kd->gqd/dot_general | solution.py:116
  247.5 2.3 fusion.110
  249.8 3.2 %fusion.111 = bf16[8,4,128,128]{3,2,1,0:T(8,128)(2,1)} fusion(bf16[8,4,128,128]{3,2,1,0:T(8,128)(2,1)} %get-tuple-element.454, s32[]{:T(128)S(6)} %copy.76, bf16[4,1152,128]{1,2,0:T(8,128)(2,1)S(1)} %get-tuple-element.474, s32[]{:T(128)S(6)} %select_n.129, pred[128,1152]{1,0:T(8,128)(4,1)S(1)} %compare_and_fusion.2, ...), kind=kOutput, calls=%fused_computation.11.clone.1 | convolution fusion | flops 305006208 | bytes 1282048 | tf_op jit(solution)/shard_map/while/body/eval_jaxpr/gqk,kd->gqd/dot_general | solution.py:116
  253.1 2.0 copy.49
  255.1 1.6 convert_element_type.62
  256.7 22.6 %while.28 = (s32[]{:T(128)}, f32[32,64,128]{2,1,0:T(8,128)S(1)}, s32[]{:T(128)}, f32[16,32]{1,0:T(8,128)S(1)}, f32[16,32,64,128]{3,2,1,0:T(8,128)}, /*index=5*/s32[]{:T(128)}, s32[]{:T(128)}) while((s32[]{:T(128)}, f32[32,64,128]{2,1,0:T(8,128)S(1)}, s32[]{:T(128)}, f32[16,32]{1,0:T(8,128)S(1)}, f32[16,32,64,128]{3,2,1,0:T(8,128)}, ...), condition=%wide.region_2.3_spmd.clone, body=%wide.region_1.2_spmd.clone.sunk | while | flops 1048580 | bytes 3146225 | solution.py:23
  256.7 1.5 fusion.112
  258.2 1.5 fusion.112
  259.7 1.5 fusion.112
  261.2 1.5 fusion.112
  262.7 1.5 fusion.112
  264.3 1.5 fusion.112
  265.8 1.5 fusion.112
  267.3 1.5 fusion.112
  268.8 1.5 fusion.112
  270.3 1.5 fusion.112
  271.8 1.5 fusion.112
  273.3 1.5 fusion.112
  274.8 1.5 fusion.112
  276.3 1.5 fusion.112
  277.8 1.5 fusion.112
  (111 shorter events, 20.4 us)
Async XLA Ops:
  7.2 66.7 %copy-start = (bf16[128,128]{1,0:T(8,128)(2,1)S(1)}, bf16[128,128]{1,0:T(8,128)(2,1)}, u32[]{:S(2)}) copy-start(bf16[128,128]{1,0:T(8,128)(2,1)} %param.14) | copy-start | bytes 98308
  7.2 66.7 %copy-start.10 = (bf16[128,128]{1,0:T(8,128)(2,1)S(1)}, bf16[128,128]{1,0:T(8,128)(2,1)}, u32[]{:S(2)}) copy-start(bf16[128,128]{1,0:T(8,128)(2,1)} %param.13) | copy-start | bytes 98308
  7.2 5.3 %copy-start.1 = (bf16[2,128,512]{2,1,0:T(8,128)(2,1)S(1)}, bf16[2,128,512]{2,1,0:T(8,128)(2,1)}, u32[]{:S(2)}) copy-start(bf16[2,128,512]{2,1,0:T(8,128)(2,1)} %param.18) | copy-start | bytes 786436
  7.2 48.2 %copy-start.11 = (s32[128]{0:T(128)S(1)}, s32[128]{0:T(128)}, u32[]{:S(2)}) copy-start(s32[128]{0:T(128)} %param.19) | copy-start | bytes 1540
  7.2 249.5 %all-gather.4.cloned.1.call-start = ((), (), s32[]{:S(2)}) async-start(), calls=%async_computation | async-start | bytes 17825792 | tf_op jit(solution)/shard_map/all_gather | solution.py:14
  12.7 7.8 %collective-permute-start.8 = (bf16[2,128,512]{1,2,0:T(8,128)(2,1)S(1)}, bf16[2,128,512]{1,2,0:T(8,128)(2,1)S(1)}, u32[]{:S(2)}, u32[]{:S(2)}) collective-permute-start(bf16[2,128,512]{1,2,0:T(8,128)(2,1)S(1)} %copy.40), channel_id=1, source_target_pairs={{0,1},{1,2},{2,3},{3,4},{4,5},{5,6},{6,7},{7,8},{8,9},{9,10},{10,1... | collective-permute-start | bytes 786440 | tf_op jit(solution)/shard_map/ppermute | solution.py:29
  20.6 113.9 %copy-start.2 = (bf16[2,128,512]{1,2,0:T(8,128)(2,1)}, bf16[2,128,512]{1,2,0:T(8,128)(2,1)S(1)}, u32[]{:S(2)}) copy-start(bf16[2,128,512]{1,2,0:T(8,128)(2,1)S(1)} %collective-permute-done.8) | copy-start | bytes 786436
  20.6 13.2 %collective-permute-start.9 = (bf16[2,128,512]{1,2,0:T(8,128)(2,1)S(1)}, bf16[2,128,512]{1,2,0:T(8,128)(2,1)S(1)}, u32[]{:S(2)}, u32[]{:S(2)}) collective-permute-start(bf16[2,128,512]{1,2,0:T(8,128)(2,1)S(1)} %collective-permute-done.8), channel_id=1, source_target_pairs={{0,1},{1,2},{2,3},{3,4},{4,5},{5,6},{6,7},{7,8},{8,9},{9,10},{10,1... | collective-permute-start | bytes 786440 | tf_op jit(solution)/shard_map/ppermute | solution.py:29
  33.7 140.8 %copy-start.4 = (bf16[2,128,512]{1,2,0:T(8,128)(2,1)}, bf16[2,128,512]{1,2,0:T(8,128)(2,1)S(1)}, u32[]{:S(2)}) copy-start(bf16[2,128,512]{1,2,0:T(8,128)(2,1)S(1)} %collective-permute-done.9) | copy-start | bytes 786436
  33.7 7.7 %collective-permute-start.10 = (bf16[2,128,512]{1,2,0:T(8,128)(2,1)S(1)}, bf16[2,128,512]{1,2,0:T(8,128)(2,1)S(1)}, u32[]{:S(2)}, u32[]{:S(2)}) collective-permute-start(bf16[2,128,512]{1,2,0:T(8,128)(2,1)S(1)} %collective-permute-done.9), channel_id=1, source_target_pairs={{0,1},{1,2},{2,3},{3,4},{4,5},{5,6},{6,7},{7,8},{8,9},{9,10},{10,1... | collective-permute-start | bytes 786440 | tf_op jit(solution)/shard_map/ppermute | solution.py:29
  41.4 133.1 %copy-start.6 = (bf16[2,128,512]{1,2,0:T(8,128)(2,1)}, bf16[2,128,512]{1,2,0:T(8,128)(2,1)S(1)}, u32[]{:S(2)}) copy-start(bf16[2,128,512]{1,2,0:T(8,128)(2,1)S(1)} %collective-permute-done.10) | copy-start | bytes 786436
  41.4 7.7 %collective-permute-start.11 = (bf16[2,128,512]{1,2,0:T(8,128)(2,1)S(1)}, bf16[2,128,512]{1,2,0:T(8,128)(2,1)S(1)}, u32[]{:S(2)}, u32[]{:S(2)}) collective-permute-start(bf16[2,128,512]{1,2,0:T(8,128)(2,1)S(1)} %collective-permute-done.10), channel_id=1, source_target_pairs={{0,1},{1,2},{2,3},{3,4},{4,5},{5,6},{6,7},{7,8},{8,9},{9,10},{10,1... | collective-permute-start | bytes 786440 | tf_op jit(solution)/shard_map/ppermute | solution.py:29
  49.1 125.4 %copy-start.8 = (bf16[2,128,512]{1,2,0:T(8,128)(2,1)}, bf16[2,128,512]{1,2,0:T(8,128)(2,1)S(1)}, u32[]{:S(2)}) copy-start(bf16[2,128,512]{1,2,0:T(8,128)(2,1)S(1)} %collective-permute-done.11) | copy-start | bytes 786436
  49.1 19.4 %collective-permute-start.12 = (bf16[2,128,512]{1,2,0:T(8,128)(2,1)S(1)}, bf16[2,128,512]{1,2,0:T(8,128)(2,1)S(1)}, u32[]{:S(2)}, u32[]{:S(2)}) collective-permute-start(bf16[2,128,512]{1,2,0:T(8,128)(2,1)S(1)} %collective-permute-done.11), channel_id=1, source_target_pairs={{0,1},{1,2},{2,3},{3,4},{4,5},{5,6},{6,7},{7,8},{8,9},{9,10},{10,1... | collective-permute-start | bytes 786440 | tf_op jit(solution)/shard_map/ppermute | solution.py:29
  55.4 32.5 %collective-permute-start = (bf16[1,128]{1,0:T(2,128)(2,1)S(1)}, bf16[1,128]{1,0:T(2,128)(2,1)S(1)}, u32[]{:S(2)}, u32[]{:S(2)}) collective-permute-start(bf16[1,128]{1,0:T(2,128)(2,1)S(1)} %convert_bitcast_fusion), channel_id=1, source_target_pairs={{0,1},{1,2},{2,3},{3,4},{4,5},{5,6},{6,7},{7,8},{8,9},{9,10},{10,1... | collective-permute-start | bytes 776 | tf_op jit(solution)/shard_map/ppermute | solution.py:29
  68.5 14.1 %copy-start.9 = (bf16[2,128,512]{1,2,0:T(8,128)(2,1)}, bf16[2,128,512]{1,2,0:T(8,128)(2,1)S(1)}, u32[]{:S(2)}) copy-start(bf16[2,128,512]{1,2,0:T(8,128)(2,1)S(1)} %collective-permute-done.12) | copy-start | bytes 786436
  68.5 14.1 %collective-permute-start.13 = (bf16[2,128,512]{1,2,0:T(8,128)(2,1)S(1)}, bf16[2,128,512]{1,2,0:T(8,128)(2,1)}, u32[]{:S(2)}, u32[]{:S(2)}) collective-permute-start(bf16[2,128,512]{1,2,0:T(8,128)(2,1)S(1)} %collective-permute-done.12), channel_id=1, source_target_pairs={{0,1},{1,2},{2,3},{3,4},{4,5},{5,6},{6,7},{7,8},{8,9},{9,10},{10,1... | collective-permute-start | bytes 786440 | tf_op jit(solution)/shard_map/ppermute | solution.py:29
  82.5 30.0 %collective-permute-start.14 = (bf16[2,128,512]{1,2,0:T(8,128)(2,1)}, bf16[2,128,512]{1,2,0:T(8,128)(2,1)}, u32[]{:S(2)}, u32[]{:S(2)}) collective-permute-start(bf16[2,128,512]{1,2,0:T(8,128)(2,1)} %collective-permute-done.13), channel_id=1, source_target_pairs={{0,1},{1,2},{2,3},{3,4},{4,5},{5,6},{6,7},{7,8},{8,9},{9,10},{10,1... | collective-permute-start | bytes 786440 | tf_op jit(solution)/shard_map/ppermute | solution.py:29
  88.0 8.3 %collective-permute-start.1 = (bf16[1,128]{1,0:T(2,128)(2,1)S(1)}, bf16[1,128]{1,0:T(2,128)(2,1)S(1)}, u32[]{:S(2)}, u32[]{:S(2)}) collective-permute-start(bf16[1,128]{1,0:T(2,128)(2,1)S(1)} %collective-permute-done), channel_id=1, source_target_pairs={{0,1},{1,2},{2,3},{3,4},{4,5},{5,6},{6,7},{7,8},{8,9},{9,10},{10,1... | collective-permute-start | bytes 776 | tf_op jit(solution)/shard_map/ppermute | solution.py:29
  96.2 5.1 %collective-permute-start.2 = (bf16[1,128]{1,0:T(2,128)(2,1)S(1)}, bf16[1,128]{1,0:T(2,128)(2,1)S(1)}, u32[]{:S(2)}, u32[]{:S(2)}) collective-permute-start(bf16[1,128]{1,0:T(2,128)(2,1)S(1)} %collective-permute-done.1), channel_id=1, source_target_pairs={{0,1},{1,2},{2,3},{3,4},{4,5},{5,6},{6,7},{7,8},{8,9},{9,10},{10,1... | collective-permute-start | bytes 776 | tf_op jit(solution)/shard_map/ppermute | solution.py:29
  101.3 5.9 %collective-permute-start.3 = (bf16[1,128]{1,0:T(2,128)(2,1)S(1)}, bf16[1,128]{1,0:T(2,128)(2,1)S(1)}, u32[]{:S(2)}, u32[]{:S(2)}) collective-permute-start(bf16[1,128]{1,0:T(2,128)(2,1)S(1)} %collective-permute-done.2), channel_id=1, source_target_pairs={{0,1},{1,2},{2,3},{3,4},{4,5},{5,6},{6,7},{7,8},{8,9},{9,10},{10,1... | collective-permute-start | bytes 776 | tf_op jit(solution)/shard_map/ppermute | solution.py:29
  107.2 18.9 %collective-permute-start.4 = (bf16[1,128]{1,0:T(2,128)(2,1)S(1)}, bf16[1,128]{1,0:T(2,128)(2,1)S(1)}, u32[]{:S(2)}, u32[]{:S(2)}) collective-permute-start(bf16[1,128]{1,0:T(2,128)(2,1)S(1)} %collective-permute-done.3), channel_id=1, source_target_pairs={{0,1},{1,2},{2,3},{3,4},{4,5},{5,6},{6,7},{7,8},{8,9},{9,10},{10,1... | collective-permute-start | bytes 776 | tf_op jit(solution)/shard_map/ppermute | solution.py:29
  112.5 66.8 %collective-permute-start.15 = (bf16[2,128,512]{1,2,0:T(8,128)(2,1)}, bf16[2,128,512]{1,2,0:T(8,128)(2,1)}, u32[]{:S(2)}, u32[]{:S(2)}) collective-permute-start(bf16[2,128,512]{1,2,0:T(8,128)(2,1)} %collective-permute-done.14), channel_id=1, source_target_pairs={{0,1},{1,2},{2,3},{3,4},{4,5},{5,6},{6,7},{7,8},{8,9},{9,10},{10,1... | collective-permute-start | bytes 786440 | tf_op jit(solution)/shard_map/ppermute | solution.py:29
  126.1 41.4 %collective-permute-start.5 = (bf16[1,128]{1,0:T(2,128)(2,1)S(1)}, bf16[1,128]{1,0:T(2,128)(2,1)S(1)}, u32[]{:S(2)}, u32[]{:S(2)}) collective-permute-start(bf16[1,128]{1,0:T(2,128)(2,1)S(1)} %collective-permute-done.4), channel_id=1, source_target_pairs={{0,1},{1,2},{2,3},{3,4},{4,5},{5,6},{6,7},{7,8},{8,9},{9,10},{10,1... | collective-permute-start | bytes 776 | tf_op jit(solution)/shard_map/ppermute | solution.py:29
  167.5 3.0 %collective-permute-start.6 = (bf16[1,128]{1,0:T(2,128)(2,1)S(1)}, bf16[1,128]{1,0:T(2,128)(2,1)S(1)}, u32[]{:S(2)}, u32[]{:S(2)}) collective-permute-start(bf16[1,128]{1,0:T(2,128)(2,1)S(1)} %collective-permute-done.5), channel_id=1, source_target_pairs={{0,1},{1,2},{2,3},{3,4},{4,5},{5,6},{6,7},{7,8},{8,9},{9,10},{10,1... | collective-permute-start | bytes 776 | tf_op jit(solution)/shard_map/ppermute | solution.py:29
  170.5 7.1 %collective-permute-start.7 = (bf16[1,128]{1,0:T(2,128)(2,1)S(1)}, bf16[1,128]{1,0:T(2,128)(2,1)S(1)}, u32[]{:S(2)}, u32[]{:S(2)}) collective-permute-start(bf16[1,128]{1,0:T(2,128)(2,1)S(1)} %collective-permute-done.6), channel_id=1, source_target_pairs={{0,1},{1,2},{2,3},{3,4},{4,5},{5,6},{6,7},{7,8},{8,9},{9,10},{10,1... | collective-permute-start | bytes 776 | tf_op jit(solution)/shard_map/ppermute | solution.py:29
  177.6 6.8 %copy-start.7 = (bf16[2,128,512]{1,2,0:T(8,128)(2,1)S(1)}, bf16[2,128,512]{1,2,0:T(8,128)(2,1)}, u32[]{:S(2)}) copy-start(bf16[2,128,512]{1,2,0:T(8,128)(2,1)} %copy-done.6) | copy-start | bytes 786436
  177.6 6.9 %copy-start.5 = (bf16[2,128,512]{1,2,0:T(8,128)(2,1)S(1)}, bf16[2,128,512]{1,2,0:T(8,128)(2,1)}, u32[]{:S(2)}) copy-start(bf16[2,128,512]{1,2,0:T(8,128)(2,1)} %copy-done.4) | copy-start | bytes 786436
  177.6 7.0 %copy-start.3 = (bf16[2,128,512]{1,2,0:T(8,128)(2,1)S(1)}, bf16[2,128,512]{1,2,0:T(8,128)(2,1)}, u32[]{:S(2)}) copy-start(bf16[2,128,512]{1,2,0:T(8,128)(2,1)} %copy-done.2) | copy-start | bytes 786436
Sparse Core Ops, SparseCore 0:
  12.7 143.8 all-gather.3
where the time goes:
time: 290 us; the launch traced here: 288 us
  starting transfers between devices  93.5 us (32%)
  matrix products  48.4 us (17%)
  waiting for transfers between devices  33.8 us (12%)
  blocking collectives  33.1 us (11%)
  other arithmetic  25.9 us (9%)
  local copies, waits for them, and re-layouts  22.5 us (8%)
  loops' own time  16.3 us (6%)
  between operations  14.5 us (5%)
    ppermute x16, starting transfers between devices, from_behind(): return lax.ppermute(block, axis, route)  93.5 us
    ppermute x16, waiting for transfers between devices, from_behind(): return lax.ppermute(block, axis, route)  33.8 us
    all_gather x1, blocking collectives, entering(): pieces = jax.tree.map(lambda part: lax.all_gather(part, axis), value)  33.1 us
    dot_general x8, matrix products, attend_item(): jnp.einsum('gqk,kd->gqd', probs.astype(jnp.bfloat16), head_values, prefer...  26 us
    select_n x15, other arithmetic, lap(): jnp.where(position < mine, new, old)  21.9 us
    sub x8, matrix products, attend_item(): probs = jnp.where(allowed[None], jnp.exp(masked - peak), 0.0)  18.6 us
    another operation x1, loops' own time, shards(): lax.map(attend_item, (query_heads, jnp.arange(2 * KV_HEADS, dtype=jnp.int...  15.7 us
    unnamed x43, local copies, waits for them, and re-layouts  9.51 us
  transfers between devices with their start and end apart: 17, of which 9 were waited for; matrix products, arithmetic and copies ran while one was open for 23% of the time, Pallas kernels for 0%

commit v1 on v0

v1 whole, which is shorter than its diff:
```python
import functools
import math

import jax
import jax.numpy as jnp
from jax import lax
from jax.experimental import pallas as pl
from jax.experimental.pallas import tpu as pltpu
from jax.sharding import PartitionSpec as P

KV_HEADS = 4
HEAD = 128
WINDOW = 1024
ROW = 4
FAR = -1e30
SCALE = HEAD ** (-0.5) * math.log2(math.e)
F32 = jnp.float32
BF16 = jnp.bfloat16
VMEM = pltpu.VMEM


def nt_dot(a, b):
    return lax.dot_general(a, b, (((1,), (1,)), ((), ())), preferred_element_type=F32)


def tn_dot(a, b, precision=None):
    return lax.dot_general(
        a, b, (((0,), (0,)), ((), ())), preferred_element_type=F32, precision=precision
    )


def call(kernel, name, outs, flops, moved, trans, **rest):
    return pl.pallas_call(
        kernel,
        name=name,
        out_shape=outs,
        cost_estimate=pl.CostEstimate(
            flops=int(flops), bytes_accessed=int(moved), transcendentals=int(trans)
        ),
        compiler_params=pltpu.CompilerParams(vmem_limit_bytes=48 * 1024 * 1024),
        **rest,
    )


def attend_kernel(kinds, first, last, tokens, *refs):
    count = len(kinds)
    q_ref, seg_ref = refs[0], refs[1]
    pieces = refs[2 : 2 + count]
    at = 2 + count
    if not first:
        acc_in, stat_in = refs[at : at + 2]
        at += 2
    if last:
        out_ref = refs[at]
        at += 1
    else:
        acc_out, stat_out = refs[at : at + 2]
        at += 2
    k_all, v_all, bias = refs[at : at + 3]
    head = pl.program_id(0)
    rows = tokens

    @pl.when(head == 0)
    def _():
        mine = seg_ref[...]
        i = lax.broadcasted_iota(jnp.int32, (rows, rows), 0)
        j = lax.broadcasted_iota(jnp.int32, (rows, rows), 1)
        for n, kind in enumerate(kinds):
            theirs = pieces[n][2 * rows : 2 * rows + 1, 0:rows].astype(F32)
            same = theirs == mine
            if kind == "own":
                same = same & (j <= i)
            if kind == "edge":
                same = same & (j > i)
            bias[:, n * rows : (n + 1) * rows] = jnp.where(same, 0.0, FAR)
        v_all[:, HEAD:] = jnp.ones((count * rows, HEAD), BF16)

    lanes = pl.ds(pl.multiple_of(head * HEAD, HEAD), HEAD)
    for n in range(count):
        k_all[n * rows : (n + 1) * rows, :] = pieces[n][0:rows, lanes]
        v_all[n * rows : (n + 1) * rows, 0:HEAD] = pieces[n][rows : 2 * rows, lanes]
    keys = k_all[...]
    values = v_all[...]
    group = q_ref.shape[2] // HEAD
    for layer in range(2):
        for r in range(group):
            slot = layer * group + r
            cols = slice(r * HEAD, (r + 1) * HEAD)
            scores = nt_dot(q_ref[layer, :, cols], keys) * SCALE + bias[...]
            peak = jnp.max(scores, axis=1, keepdims=True)
            if not first:
                old_peak = stat_in[0, :, slot : slot + 1]
                peak = jnp.maximum(peak, old_peak)
            probs = jnp.exp2(scores - peak)
            both = jnp.dot(probs.astype(BF16), values, preferred_element_type=F32)
            total = both[:, HEAD:]
            acc = both[:, :HEAD]
            if not first:
                fade = jnp.exp2(old_peak - peak)
                acc = acc + fade * acc_in[layer, :, cols]
                total = total + fade * stat_in[0, :, 8 + slot : 9 + slot]
            if last:
                out_ref[layer, :, cols] = (acc / total).astype(BF16)
            else:
                acc_out[layer, :, cols] = acc
                stat_out[0, :, slot : slot + 1] = peak
                stat_out[0, :, 8 + slot : 9 + slot] = total[:, 0:1]


def attend(queries, segs, pieces, kinds, carry, last):
    layers, tokens, width = queries.shape
    block = width // KV_HEADS
    count = len(kinds)
    wide = pl.BlockSpec((layers, tokens, block), lambda h: (0, 0, h))
    stat = pl.BlockSpec((1, tokens, HEAD), lambda h: (h, 0, 0))
    whole = lambda x: pl.BlockSpec(x.shape, lambda h: (0,) * x.ndim)
    in_specs = [wide, whole(segs)] + [whole(p) for p in pieces]
    args = [queries, segs] + list(pieces)
    if carry is not None:
        in_specs += [wide, stat]
        args += list(carry)
    if last:
        outs = jax.ShapeDtypeStruct(queries.shape, BF16)
        out_specs = wide
    else:
        outs = (
            jax.ShapeDtypeStruct(queries.shape, F32),
            jax.ShapeDtypeStruct((KV_HEADS, tokens, HEAD), F32),
        )
        out_specs = (wide, stat)
    work = layers * tokens * width * tokens * count
    return call(
        functools.partial(attend_kernel, kinds, carry is None, last, tokens),
        "attend",
        outs,
        4 * work,
        4 * queries.size * 2,
        work // HEAD,
        grid=(KV_HEADS,),
        in_specs=in_specs,
        out_specs=out_specs,
        scratch_shapes=[
            VMEM((count * tokens, HEAD), BF16),
            VMEM((count * tokens, 2 * HEAD), BF16),
            VMEM((tokens, count * tokens), F32),
        ],
    )(*args)


def spread(columns, first, pairs, width):
    lane = lax.broadcasted_iota(jnp.int32, (1, 2 * width), 1)
    parts = [
        jnp.where(
            lane < width,
            columns[:, first + 2 * k : first + 2 * k + 1],
            columns[:, first + 2 * k + 1 : first + 2 * k + 2],
        )
        for k in range(pairs)
    ]
    return jnp.concatenate(parts, axis=1)


def local_kernel(
    heads, state, place, x_ref, own_ref, y_ref, c_ref, rate_ref, mixed_ref, tail_ref, run_ref,
    read_ref, xs, sm
):
    tokens = x_ref.shape[0]
    cols = xs.shape[2]
    width = cols // heads
    q = place[0]
    core = lax.rem(q, 2)
    lanes = lambda n: pl.ds(pl.multiple_of(n * cols, cols), cols)
    xs[q] = x_ref[:, lanes(q)]
    sm[q] = own_ref[...]
    xs[q ^ 2] = y_ref[:, lanes(core)]
    sm[q ^ 2] = y_ref[:, 2 * cols :]
    xs[q ^ 1] = c_ref[0:tokens, 0:cols]
    sm[q ^ 1] = c_ref[0:tokens, cols:]
    xs[q ^ 3] = c_ref[tokens:, 0:cols]
    sm[q ^ 3] = c_ref[tokens:, cols:]

    i = lax.broadcasted_iota(jnp.int32, (tokens, tokens), 0)
    j = lax.broadcasted_iota(jnp.int32, (tokens, tokens), 1)
    causal = j <= i
    lower_ones = causal.astype(F32)
    upper_ones = (i <= j).astype(F32)
    lane = lax.broadcasted_iota(jnp.int32, (1, 2 * width), 1)
    low = lane < width
    rates = rate_ref[0:1, :]
    shift = lax.rem(128 - q * heads, 128)
    carried_state = jnp.zeros((state, cols), F32)
    offset = jnp.zeros((1, 128), F32)
    for b in range(ROW):
        write = sm[b, :, 0:state]
        read = sm[b, :, state : 2 * state]
        read_ref[b] = read
        codes = sm[b, :, 2 * state :].astype(F32)
        high = codes
        little = pltpu.roll(codes, 64, 1)
        level = jnp.floor(high * 0.0625)
        lower = high * 64.0 + little - 1024.0 * level
        step = -rates * (1.0 + lower * (1.0 / 128.0)) - 0.125 * level
        step = pltpu.roll(step, shift, 1)
        step = jnp.where(j < heads, step, 0.0)
        run = jnp.dot(
            lower_ones, step, preferred_element_type=F32, precision=lax.Precision.HIGHEST
        )
        run_t = tn_dot(step, upper_ones, lax.Precision.HIGHEST)
        end = run[tokens - 1 : tokens, :]
        run_ref[b] = run + offset
        offset = offset + end
        inner = nt_dot(read, write)
        inner = jnp.where(causal, inner, 0.0)
        to_end = jnp.exp(end - run)
        locals_ = []
        scaled = []
        for pair in range(heads // 2):
            tile = xs[b, :, pair * 2 * width : (pair + 1) * 2 * width]
            mixes = []
            for h in (2 * pair, 2 * pair + 1):
                gap = jnp.minimum(run[:, h : h + 1] - run_t[h : h + 1, :], 0.0)
                mixes.append((inner * jnp.exp(gap)).astype(BF16))
            zero = jnp.zeros_like(tile)
            stacked = jnp.concatenate(
                [jnp.where(low, tile, zero), jnp.where(low, zero, tile)], axis=0
            )
            locals_.append(
                jnp.dot(jnp.concatenate(mixes, axis=1), stacked, preferred_element_type=F32)
            )
            weight = jnp.where(
                low, to_end[:, 2 * pair : 2 * pair + 1], to_end[:, 2 * pair + 1 : 2 * pair + 2]
            )
            scaled.append((weight * tile.astype(F32)).astype(BF16))
        mixed = jnp.concatenate(locals_, axis=1)
        if b > 0:
            seen = jnp.dot(read, carried_state.astype(BF16), preferred_element_type=F32)
            mixed = mixed + spread(jnp.exp(run), 0, heads // 2, width) * seen
        mixed_ref[b] = mixed
        added = tn_dot(write, jnp.concatenate(scaled, axis=1))
        if b > 0:
            added = spread(jnp.exp(end), 0, heads // 2, width) * carried_state + added
        carried_state = added
    tail_ref[0:state, :] = carried_state.astype(BF16)
    log_total = spread(offset, 0, heads // 2, width)
    one = log_total.astype(BF16)
    rest = log_total - one.astype(F32)
    two = rest.astype(BF16)
    three = (rest - two.astype(F32)).astype(BF16)
    row = lax.broadcasted_iota(jnp.int32, (16, cols), 0)
    tail_ref[state:, :] = jnp.where(row == 0, one, jnp.where(row == 1, two, three))


def finish_kernel(
    heads, state, rows, place, mixed_ref, tails_ref, run_ref, read_ref, self_ref, c_ref, y_ref
):
    q = place[0]
    z = place[1]
    cols = mixed_ref.shape[2]
    width = cols // heads
    entering = jnp.zeros((state, cols), F32)
    for n in range(rows - 1):
        logs = tails_ref[n, state:, :].astype(F32)
        decay = jnp.exp(logs[0:1] + logs[1:2] + logs[2:3])
        later = decay * entering + tails_ref[n, 0:state, :].astype(F32)
        entering = jnp.where(n < z, later, entering)
    entering = entering.astype(BF16)
    a = lax.broadcasted_iota(jnp.int32, (4 * width, 2 * width), 0)
    b = lax.broadcasted_iota(jnp.int32, (4 * width, 2 * width), 1)
    same = (lax.rem(a, 2 * width) < width) == (b < width)
    average = jnp.where(same, 1.0 / width, 0.0).astype(BF16)
    for near in range(ROW):
        at = q ^ near
        seen = jnp.dot(read_ref[at], entering, preferred_element_type=F32)
        fade = spread(jnp.exp(run_ref[at]), 0, heads // 2, width)
        mixed = mixed_ref[at] + fade * seen
        for pair in range(heads // 2):
            part = slice(pair * 2 * width, (pair + 1) * 2 * width)
            tile = mixed[:, part]
            square = tile * tile
            big = square.astype(BF16)
            small = (square - big.astype(F32)).astype(BF16)
            mean = jnp.dot(
                jnp.concatenate([big, small], axis=1), average, preferred_element_type=F32
            )
            result = (tile * lax.rsqrt(mean + 1e-05)).astype(BF16)
            if near == 0:
                self_ref[:, part] = result
            elif near == 1:
                c_ref[:, part] = result
            else:
                y_ref[near - 2, :, part] = result


def gather_kernel(place, self_ref, y_ref, c_ref, out_ref):
    q = place[0]
    cols = self_ref.shape[1]
    lanes = lambda n: pl.ds(pl.multiple_of(n * cols, cols), cols)
    out_ref[:, lanes(q)] = self_ref[...]
    out_ref[:, lanes(q ^ 2)] = y_ref[0]
    out_ref[:, lanes(q ^ 1)] = c_ref[0]
    out_ref[:, lanes(q ^ 3)] = c_ref[1]


def shards(
    ssm_inputs, state_write, state_read, decay_codes, decay_rate, queries, keys_values, segment_ids
):
    tokens, channels = ssm_inputs.shape
    heads = decay_rate.shape[0]
    state = state_write.shape[1]
    own_heads = heads // ROW
    cols = channels // ROW
    devices = lax.axis_size("seq")
    rows = devices // ROW
    rank = lax.axis_index("seq")
    q = rank % ROW
    core, y = q % 2, q // 2
    place = jnp.stack([q, rank // ROW]).astype(jnp.int32)
    swap_c = [(i, i ^ 1) for i in range(devices)]
    swap_y = [(i, i ^ 2) for i in range(devices)]
    up_z = [(i, i + ROW) for i in range(devices - ROW)]
    c_up = [(i, i + 1) for i in range(0, devices, 2)]
    c_down = [(i + 1, i) for i in range(0, devices, 2)]
    send = lambda x, route: lax.ppermute(x, "seq", route)
    smem = pl.BlockSpec(memory_space=pltpu.SMEM)
    vmem = pl.BlockSpec(memory_space=pltpu.VMEM)

    seg_codes = (segment_ids + 1).astype(BF16)
    kv_width = keys_values.shape[2]
    seg_rows = jnp.broadcast_to(
        jnp.pad(seg_codes, (0, kv_width - tokens))[None, :], (16, kv_width)
    )
    own = jnp.concatenate([keys_values[0], keys_values[1], seg_rows], axis=0)
    segs = jnp.broadcast_to(seg_codes.astype(F32)[:, None], (tokens, tokens))

    codes = jnp.concatenate(
        [
            jnp.pad((decay_codes // 64).astype(BF16), ((0, 0), (0, 64 - heads))),
            jnp.pad((decay_codes % 64).astype(BF16), ((0, 0), (0, 64 - heads))),
        ],
        axis=1,
    )
    small = jnp.concatenate([state_write, state_read, codes], axis=1)
    to_y = jnp.concatenate(
        [lax.dynamic_slice_in_dim(ssm_inputs, (1 - y) * 2 * cols, 2 * cols, 1), small], axis=1
    )
    from_y = send(to_y, swap_y)
    behind2 = send(own, up_z)
    partner = send(own, c_up)
    to_c = jnp.concatenate(
        [
            jnp.concatenate(
                [lax.dynamic_slice_in_dim(ssm_inputs, (q ^ 1) * cols, cols, 1), small], axis=1
            ),
            jnp.concatenate(
                [
                    lax.dynamic_slice_in_dim(from_y, (1 - core) * cols, cols, 1),
                    from_y[:, 2 * cols :],
                ],
                axis=1,
            ),
        ],
        axis=0,
    )
    from_c = send(to_c, swap_c)

    carry = attend(queries, segs, [own, partner], ("own", "any"), None, False)

    rates = jnp.broadcast_to(jnp.pad(decay_rate, (0, 128 - heads))[None, :], (8, 128))
    mixed, tail, run, reads = call(
        functools.partial(local_kernel, own_heads, state),
        "local",
        (
            jax.ShapeDtypeStruct((ROW, tokens, cols), F32),
            jax.ShapeDtypeStruct((state + 16, cols), BF16),
            jax.ShapeDtypeStruct((ROW, tokens, 128), F32),
            jax.ShapeDtypeStruct((ROW, tokens, state), BF16),
        ),
        ROW * tokens * cols * tokens * 8,
        4 * 1024 * 1024,
        ROW * own_heads * tokens * tokens,
        in_specs=[smem] + [vmem] * 5,
        out_specs=(vmem,) * 4,
        scratch_shapes=[
            VMEM((ROW, tokens, cols), BF16),
            VMEM((ROW, tokens, 2 * state + 128), BF16),
        ],
    )(place, ssm_inputs, small, from_y, from_c, rates)
    groups = [[i + ROW * n for n in range(rows)] for i in range(ROW)]
    tails = lax.all_gather(tail, "seq", axis_index_groups=groups)

    behind1 = send(jnp.where(y == 0, own, behind2), swap_y)
    behind4 = send(behind2, up_z)
    behind2c = send(behind2, swap_c)
    behind1c = send(behind1, swap_c)
    carry = attend(
        queries, segs, [behind2, behind2c, behind1, behind1c], ("any",) * 4, carry, False
    )
    behind3 = send(jnp.where(y == 0, behind2, behind4), swap_y)
    behind4c = send(behind4, c_down)
    behind3c = send(behind3, swap_c)

    mine, for_c, for_y = call(
        functools.partial(finish_kernel, own_heads, state, rows),
        "finish",
        (
            jax.ShapeDtypeStruct((tokens, cols), BF16),
            jax.ShapeDtypeStruct((tokens, cols), BF16),
            jax.ShapeDtypeStruct((2, tokens, cols), BF16),
        ),
        ROW * tokens * cols * tokens * 6,
        4 * 1024 * 1024,
        ROW * tokens * cols,
        in_specs=[smem] + [vmem] * 4,
        out_specs=(vmem,) * 3,
    )(place, mixed, tails, run, reads)
    back_y = send(for_y, swap_y)
    back_c = send(jnp.stack([for_c, back_y[1]]), swap_c)

    attn_output = attend(
        queries, segs, [behind4, behind4c, behind3, behind3c], ("edge",) + ("any",) * 3, carry, True
    )
    ssm_output = call(
        gather_kernel,
        "collect",
        jax.ShapeDtypeStruct((tokens, channels), BF16),
        0,
        1024 * 1024,
        0,
        in_specs=[smem] + [vmem] * 3,
        out_specs=vmem,
    )(place, mine, back_y, back_c)
    return (ssm_output, attn_output)


def solution(mesh):
    return jax.shard_map(
        shards,
        mesh=mesh,
        in_specs=(
            P(("groups", "seq"), None),
            P(("groups", "seq"), None),
            P(("groups", "seq"), None),
            P(("groups", "seq"), None),
            P(),
            P(None, ("groups", "seq"), None),
            P(None, ("groups", "seq"), None),
            P(("groups", "seq")),
        ),
        out_specs=(P(("groups", "seq"), None), P(None, ("groups", "seq"), None)),
        check_vma=False,
    )
```

time: 290 us -> 85.7 us (0.30)
  starting transfers between devices: 93.5 us -> 26 us
  matrix products: 48.4 us -> 0 us
  Pallas kernels: 0 us -> 31.1 us
  waiting for transfers between devices: 33.8 us -> 6.33 us
  other arithmetic: 25.9 us -> 0.44 us
  blocking collectives: 33.1 us -> 14.6 us
  local copies, waits for them, and re-layouts: 22.5 us -> 5.35 us
  loops' own time: 16.3 us -> 0 us
  between operations: 14.5 us -> 1.08 us
    ppermute x16 -> x13, starting transfers between devices: 93.5 us -> 26 us  [shards(): send = lambda x, route: lax.ppermute(x, 'seq', route)]
    pallas_call x0 -> x6, Pallas kernels: none -> 31.1 us  [the longest x3 23.6 us: attend(): call(functools.partial(attend_kernel, kinds, carry is None, last, tokens)...]
    dot_general x12 -> x0, matrix products: 29.7 us -> none  [the longest x8 26 us: attend_item(): jnp.einsum('gqk,kd->gqd', probs.astype(jnp.bfloat16), head_values, prefer...]
    ppermute x16 -> x13, waiting for transfers between devices: 33.8 us -> 6.33 us  [shards(): send = lambda x, route: lax.ppermute(x, 'seq', route)]
    select_n x15 -> x1, other arithmetic: 21.9 us -> 0.12 us  [shards(): behind1 = send(jnp.where(y == 0, own, behind2), swap_y)]
    sub x8 -> x0, matrix products: 18.6 us -> none  [attend_item(): probs = jnp.where(allowed[None], jnp.exp(masked - peak), 0.0)]
    all_gather x1, blocking collectives: 33.1 us -> 14.6 us  [shards(): tails = lax.all_gather(tail, 'seq', axis_index_groups=groups)]
    another operation x2 -> x0, loops' own time: 16.3 us -> none  [the longest x1 15.7 us: shards(): lax.map(attend_item, (query_heads, jnp.arange(2 * KV_HEADS, dtype=jnp.int...]
  transfers between devices with their start and end apart: 17 -> 13, of which waited for: 9 -> 2; matrix products, arithmetic and copies ran while one was open for 23% -> 2% of each run, Pallas kernels for 0% -> 35%
where the time goes in v1:
time: 85.7 us; the launch traced here: 84.9 us
  Pallas kernels  31.1 us (36%)
  starting transfers between devices  26 us (30%)
  blocking collectives  14.6 us (17%)
  waiting for transfers between devices  6.33 us (7%)
  local copies, waits for them, and re-layouts  5.35 us (6%)
  between operations  1.08 us (1%)
    ppermute x13, starting transfers between devices, shards(): send = lambda x, route: lax.ppermute(x, 'seq', route)  26 us
    pallas_call x3, Pallas kernels, attend(): call(functools.partial(attend_kernel, kinds, carry is None, last, tokens)...  23.6 us
    all_gather x1, blocking collectives, shards(): tails = lax.all_gather(tail, 'seq', axis_index_groups=groups)  14.6 us
    ppermute x13, waiting for transfers between devices, shards(): send = lambda x, route: lax.ppermute(x, 'seq', route)  6.33 us
    pallas_call x1, Pallas kernels, shards(): call(functools.partial(local_kernel, own_heads, state), 'local', (jax.Sha...  4.37 us
    unnamed x15, local copies, waits for them, and re-layouts  2.23 us
  transfers between devices with their start and end apart: 13, of which 2 were waited for; matrix products, arithmetic and copies ran while one was open for 2% of the time, Pallas kernels for 35%

profile of v1, /device:TPU:1, one launch (start us, length us, event | category | flops | bytes accessed | tf_op | source)
XLA Modules:
  0.0 84.9 jit_solution(7612956926088921389)
XLA Ops:
  0.6 0.0 copy-start.2
  0.6 0.0 copy-start.3
  0.7 0.0 copy-start.4
  0.7 0.0 copy-start.5
  0.7 0.0 copy-start.6
  0.7 0.9 %copy.10 = s32[128,32]{1,0:T(8,128)S(1)} copy(s32[128,32]{0,1:T(8,128)} %param.11) | data formatting | bytes 32768 | tf_op args[3]
  1.6 0.1 fusion
  1.7 1.0 %constant_dynamic-slice_fusion.2 = bf16[128,1024]{1,0:T(8,128)(2,1)S(1)} fusion(bf16[128,2048]{1,0:T(8,128)(2,1)} %x_ref.1, s32[]{:T(128)S(6)} %select_n.55), kind=kLoop, calls=%fused_computation.20 | loop fusion | bytes 524292 | tf_op jit(solution)/shard_map/dynamic_slice | solution.py:344
  2.7 0.9 %concatenate.21 = bf16[128,1408]{1,0:T(8,128)(2,1)S(1)} concatenate(bf16[128,1024]{1,0:T(8,128)(2,1)S(1)} %constant_dynamic-slice_fusion.2, bf16[128,128]{1,0:T(8,128)(2,1)} %param.9, bf16[128,128]{1,0:T(8,128)(2,1)} %param.10, bf16[128,64]{1,0:T(8,128)(2,1)S(1)} %pad.15, bf16[128,64]{1,0:T(8,128)(2,1)S(1)} %pad.16), dimensions={1} | concatenate | bytes 720896 | tf_op jit(solution)/shard_map/concatenate | solution.py:343
  3.6 2.1 %collective-permute-start = (bf16[128,1408]{1,0:T(8,128)(2,1)S(1)}, bf16[128,1408]{1,0:T(8,128)(2,1)S(1)}, u32[]{:S(2)}, u32[]{:S(2)}) collective-permute-start(bf16[128,1408]{1,0:T(8,128)(2,1)S(1)} %concatenate.21), channel_id=1, source_target_pairs={{0,2},{1,3},{2,0},{3,1},{4,6},{5,7},{6,4},{7,5},{8,10},{9,11},{10,... | collective-permute-start | bytes 1081352 | tf_op jit(solution)/shard_map/ppermute | solution.py:323
  5.7 1.0 %slice_bitcast_fusion.1 = (bf16[128,512]{1,0:T(8,128)(2,1)S(1)}, bf16[128,512]{1,0:T(8,128)(2,1)S(1)}) fusion(bf16[2,128,512]{2,1,0:T(8,128)(2,1)} %param.14), kind=kLoop, calls=%fused_computation.6 | loop fusion | bytes 524288 | tf_op jit(solution)/shard_map/squeeze | solution.py:332
  6.7 0.0 copy-done.5
  6.8 3.2 %collective-permute-start.4 = (bf16[272,512]{1,0:T(8,128)(2,1)S(1)}, bf16[272,512]{1,0:T(8,128)(2,1)S(1)}, u32[]{:S(2)}, u32[]{:S(2)}) collective-permute-start(bf16[272,512]{1,0:T(8,128)(2,1)S(1)} %pad_maximum_fusion.refs_2_), channel_id=1, source_target_pairs={{0,4},{1,5},{2,6},{3,7},{4,8},{5,9},{6,10},{7,11},{8,12},{9,13},{1... | collective-permute-start | bytes 835592 | tf_op jit(solution)/shard_map/ppermute | solution.py:323
  10.1 0.0 copy-done.2
  10.1 0.0 copy-done.3
  10.1 0.0 copy-done.4
  10.1 0.1 concatenate.22
  10.2 0.0 copy-done.6
  10.3 4.7 %collective-permute-done.4.refs_2_ = bf16[272,512]{1,0:T(8,128)(2,1)S(1)} collective-permute-done((bf16[272,512]{1,0:T(8,128)(2,1)S(1)}, bf16[272,512]{1,0:T(8,128)(2,1)S(1)}, u32[]{:S(2)}, u32[]{:S(2)}) %collective-permute-start.4) | collective-permute-done | bytes 278560 | tf_op jit(solution)/shard_map/ppermute | solution.py:323
  15.0 4.1 %collective-permute-start.5 = (bf16[272,512]{1,0:T(8,128)(2,1)S(1)}, bf16[272,512]{1,0:T(8,128)(2,1)S(1)}, u32[]{:S(2)}, u32[]{:S(2)}) collective-permute-start(bf16[272,512]{1,0:T(8,128)(2,1)S(1)} %collective-permute-done.4.refs_2_), channel_id=1, source_target_pairs={{0,4},{1,5},{2,6},{3,7},{4,8},{5,9},{6,10},{7,11},{8,12},{9,13},{1... | collective-permute-start | bytes 835592 | tf_op jit(solution)/shard_map/ppermute | solution.py:323
  19.1 0.0 collective-permute-done.y_ref
  19.2 2.2 %collective-permute-start.1 = (bf16[256,896]{1,0:T(8,128)(2,1)S(1)}, bf16[256,896]{1,0:T(8,128)(2,1)S(1)}, u32[]{:S(2)}, u32[]{:S(2)}) collective-permute-start(bf16[256,896]{1,0:T(8,128)(2,1)S(1)} %maximum_maximum_fusion), channel_id=1, source_target_pairs={{0,1},{1,0},{2,3},{3,2},{4,5},{5,4},{6,7},{7,6},{8,9},{9,8},{10,11... | collective-permute-start | bytes 1376264 | tf_op jit(solution)/shard_map/ppermute | solution.py:323
  21.4 0.1 pad_add_fusion.place
  21.5 0.1 pad_maximum_fusion.2.own_ref
  21.6 1.6 %collective-permute-done.5.refs_2_ = bf16[272,512]{1,0:T(8,128)(2,1)S(1)} collective-permute-done((bf16[272,512]{1,0:T(8,128)(2,1)S(1)}, bf16[272,512]{1,0:T(8,128)(2,1)S(1)}, u32[]{:S(2)}, u32[]{:S(2)}) %collective-permute-start.5) | collective-permute-done | bytes 278560 | tf_op jit(solution)/shard_map/ppermute | solution.py:323
  23.2 0.1 broadcast_select_fusion
  23.3 0.3 collective-permute-start.10
  23.6 1.2 %collective-permute-start.7 = (bf16[272,512]{1,0:T(8,128)(2,1)S(1)}, bf16[272,512]{1,0:T(8,128)(2,1)S(1)}, u32[]{:S(2)}, u32[]{:S(2)}) collective-permute-start(bf16[272,512]{1,0:T(8,128)(2,1)S(1)} %get-tuple-element.25), channel_id=1, source_target_pairs={{0,2},{1,3},{2,0},{3,1},{4,6},{5,7},{6,4},{7,5},{8,10},{9,11},{10,... | collective-permute-start | bytes 835592 | tf_op jit(solution)/shard_map/ppermute | solution.py:323
  24.8 0.0 collective-permute-done.1.c_ref
  24.8 4.4 %local.1 = (f32[4,128,512]{2,1,0:T(8,128)S(1)}, bf16[144,512]{1,0:T(8,128)(2,1)S(1)}, f32[4,128,128]{2,1,0:T(8,128)S(1)}, bf16[4,128,128]{2,1,0:T(8,128)(2,1)S(1)}) custom-call(s32[2]{0:T(128)S(1)} %pad_add_fusion.place, bf16[128,2048]{1,0:T(8,128)(2,1)S(1)} %copy-done.2, bf16[128,384]{1,0:T(8,128)(2,1)S(1)} %pad_maximum_fusion.2.own_ref, ...), custom_call_target="tpu_custom_call" | custom-call | flops 268435456 | bytes 4194304 | tf_op jit(solution)/shard_map/local/pallas_call | solution.py:369
  29.2 0.0 copy-start
  29.2 14.6 %all-gather = bf16[576,512]{1,0:T(8,128)(2,1)S(1)} all-gather(bf16[144,512]{1,0:T(8,128)(2,1)S(1)} %get-tuple-element.14), channel_id=2, replica_groups={{0,4,8,12},{1,5,9,13},{2,6,10,14},{3,7,11,15},{16,20,24,28},{17,21,25,2..., dimensions={0}, use_global_device_ids=true | all-gather | bytes 737280 | tf_op jit(solution)/shard_map/all_gather | solution.py:389
  43.8 1.7 %finish.1 = (bf16[128,512]{1,0:T(8,128)(2,1)S(1)}, bf16[128,512]{1,0:T(8,128)(2,1)S(1)}, bf16[2,128,512]{2,1,0:T(8,128)(2,1)S(1)}) custom-call(s32[2]{0:T(128)S(1)} %pad_add_fusion.place, f32[4,128,512]{2,1,0:T(8,128)S(1)} %get-tuple-element.13.mixed_ref, bf16[4,144,512]{2,1,0:T(8,128)(2,1)S(1)} %bitcast.8, f32[4,128,128]{2,1,0:T(8,128)S(1)} %get-tuple-element.15.run_ref, ...), custom_call_target="tpu_custom_call" | custom-call | flops 201326592 | bytes 4194304 | tf_op jit(solution)/shard_map/finish/pallas_call | solution.py:402
  45.5 0.3 collective-permute-start.2
  45.8 1.3 %collective-permute-start.12 = (bf16[272,512]{1,0:T(8,128)(2,1)S(1)}, bf16[272,512]{1,0:T(8,128)(2,1)S(1)}, u32[]{:S(2)}, u32[]{:S(2)}) collective-permute-start(bf16[272,512]{1,0:T(8,128)(2,1)S(1)} %pad_maximum_fusion.refs_2_), channel_id=1, source_target_pairs={{0,1},{2,3},{4,5},{6,7},{8,9},{10,11},{12,13},{14,15},{16,17},{18,... | collective-permute-start | bytes 835592 | tf_op jit(solution)/shard_map/ppermute | solution.py:323
  47.1 6.7 %collective-permute-start.9 = (bf16[272,512]{1,0:T(8,128)(2,1)S(1)}, bf16[272,512]{1,0:T(8,128)(2,1)S(1)}, u32[]{:S(2)}, u32[]{:S(2)}) collective-permute-start(bf16[272,512]{1,0:T(8,128)(2,1)S(1)} %collective-permute-done.4.refs_2_), channel_id=1, source_target_pairs={{0,1},{1,0},{2,3},{3,2},{4,5},{5,4},{6,7},{7,6},{8,9},{9,8},{10,11... | collective-permute-start | bytes 835592 | tf_op jit(solution)/shard_map/ppermute | solution.py:323
  53.8 0.0 collective-permute-done.10.refs_4_
  53.8 0.1 collective-permute-start.11
  53.9 0.0 collective-permute-done.7.refs_4_
  53.9 2.3 %collective-permute-start.6 = (bf16[272,512]{1,0:T(8,128)(2,1)S(1)}, bf16[272,512]{1,0:T(8,128)(2,1)S(1)}, u32[]{:S(2)}, u32[]{:S(2)}) collective-permute-start(bf16[272,512]{1,0:T(8,128)(2,1)S(1)} %collective-permute-done.5.refs_2_), channel_id=1, source_target_pairs={{1,0},{3,2},{5,4},{7,6},{9,8},{11,10},{13,12},{15,14},{17,16},{19,... | collective-permute-start | bytes 835592 | tf_op jit(solution)/shard_map/ppermute | solution.py:323
  56.2 0.0 collective-permute-done.2.y_ref
  56.2 2.1 %collective-permute-start.8 = (bf16[272,512]{1,0:T(8,128)(2,1)S(1)}, bf16[272,512]{1,0:T(8,128)(2,1)S(1)}, u32[]{:S(2)}, u32[]{:S(2)}) collective-permute-start(bf16[272,512]{1,0:T(8,128)(2,1)S(1)} %collective-permute-done.7.refs_4_), channel_id=1, source_target_pairs={{0,1},{1,0},{2,3},{3,2},{4,5},{5,4},{6,7},{7,6},{8,9},{9,8},{10,11... | collective-permute-start | bytes 835592 | tf_op jit(solution)/shard_map/ppermute | solution.py:323
  58.3 0.0 collective-permute-done.12.refs_3_
  58.4 0.1 collective-permute-start.3
  58.4 0.1 broadcast_in_dim.7.refs_1_
  58.5 0.0 copy-done
  58.5 3.3 %attend.3 = (f32[2,128,2048]{2,1,0:T(8,128)S(1)}, f32[4,128,128]{2,1,0:T(8,128)S(1)}) custom-call(bf16[2,128,2048]{2,1,0:T(8,128)(2,1)S(1)} %copy-done, f32[128,128]{1,0:T(8,128)S(1)} %broadcast_in_dim.7.refs_1_, bf16[272,512]{1,0:T(8,128)(2,1)S(1)} %pad_maximum_fusion.refs_2_, bf16[272,512]{1,0:T(8,128)(2,1)S(1)} %collective-permute-done.12.refs_3_), custom_call_target="tpu_custom_call" | custom-call | flops 536870912 | bytes 4194304 | tf_op jit(solution)/shard_map/attend/pallas_call | solution.py:132
  61.8 0.0 copy-start.1
  61.8 1.3 %copy-done.1 = f32[2,128,2048]{2,1,0:T(8,128)} copy-done((f32[2,128,2048]{2,1,0:T(8,128)}, f32[2,128,2048]{2,1,0:T(8,128)S(1)}, u32[]{:S(2)}) %copy-start.1) | copy-done | bytes 2097176
  63.1 0.0 collective-permute-done.9.refs_3_
  63.1 0.0 collective-permute-done.11.refs_5_
  63.1 11.0 %attend.4 = (f32[2,128,2048]{2,1,0:T(8,128)S(1)}, f32[4,128,128]{2,1,0:T(8,128)S(1)}) custom-call(bf16[2,128,2048]{2,1,0:T(8,128)(2,1)S(1)} %copy-done, f32[128,128]{1,0:T(8,128)S(1)} %broadcast_in_dim.7.refs_1_, bf16[272,512]{1,0:T(8,128)(2,1)S(1)} %collective-permute-done.4.refs_2_, bf16[272,512]{1,0:T(8,128)(2,1)S(1)} %collective-permute-done.9.refs_3_, ...), custom_call_target="tpu_custom_call" | custom-call | flops 1073741824 | bytes 4194304 | tf_op jit(solution)/shard_map/attend/pallas_call | solution.py:132
  74.1 0.0 collective-permute-done.6.refs_3_
  74.1 0.0 collective-permute-done.8.refs_5_
  74.1 9.4 %attend.5 = bf16[2,128,2048]{2,1,0:T(8,128)(2,1)} custom-call(bf16[2,128,2048]{2,1,0:T(8,128)(2,1)S(1)} %copy-done, f32[128,128]{1,0:T(8,128)S(1)} %broadcast_in_dim.7.refs_1_, bf16[272,512]{1,0:T(8,128)(2,1)S(1)} %collective-permute-done.5.refs_2_, bf16[272,512]{1,0:T(8,128)(2,1)S(1)} %collective-permute-done.6.refs_3_, ...), custom_call_target="tpu_custom_call" | custom-call | flops 1073741824 | bytes 4194304 | tf_op jit(solution)/shard_map/attend/pallas_call | solution.py:132
  83.5 0.0 collective-permute-done.3.c_ref
  83.5 1.4 %collect.1 = bf16[128,2048]{1,0:T(8,128)(2,1)} custom-call(s32[2]{0:T(128)S(1)} %pad_add_fusion.place, bf16[128,512]{1,0:T(8,128)(2,1)S(1)} %get-tuple-element.17.self_ref, bf16[2,128,512]{2,1,0:T(8,128)(2,1)S(1)} %collective-permute-done.2.y_ref, bf16[2,128,512]{2,1,0:T(8,128)(2,1)S(1)} %collective-permute-done.3.c_ref), custom_call_target="tpu_custom_call" | custom-call | bytes 1048576 | tf_op jit(solution)/shard_map/collect/pallas_call | solution.py:422
  (14 shorter events, 0.2 us)
Async XLA Ops:
  0.6 9.4 %copy-start.2 = (bf16[128,2048]{1,0:T(8,128)(2,1)S(1)}, bf16[128,2048]{1,0:T(8,128)(2,1)}, u32[]{:S(2)}) copy-start(bf16[128,2048]{1,0:T(8,128)(2,1)} %x_ref.1) | copy-start | bytes 1572868
  0.6 9.4 %copy-start.3 = (bf16[128,128]{1,0:T(8,128)(2,1)S(1)}, bf16[128,128]{1,0:T(8,128)(2,1)}, u32[]{:S(2)}) copy-start(bf16[128,128]{1,0:T(8,128)(2,1)} %param.10) | copy-start | bytes 98308
  0.7 9.4 %copy-start.4 = (bf16[128,128]{1,0:T(8,128)(2,1)S(1)}, bf16[128,128]{1,0:T(8,128)(2,1)}, u32[]{:S(2)}) copy-start(bf16[128,128]{1,0:T(8,128)(2,1)} %param.9) | copy-start | bytes 98308
  0.7 6.1 %copy-start.5 = (s32[128]{0:T(128)S(1)}, s32[128]{0:T(128)}, u32[]{:S(2)}) copy-start(s32[128]{0:T(128)} %param.15) | copy-start | bytes 1540
  0.7 9.6 %copy-start.6 = (f32[32]{0:T(128)S(1)}, f32[32]{0:T(128)}, u32[]{:S(2)}) copy-start(f32[32]{0:T(128)} %param.12) | copy-start | bytes 388
  3.6 15.5 %collective-permute-start = (bf16[128,1408]{1,0:T(8,128)(2,1)S(1)}, bf16[128,1408]{1,0:T(8,128)(2,1)S(1)}, u32[]{:S(2)}, u32[]{:S(2)}) collective-permute-start(bf16[128,1408]{1,0:T(8,128)(2,1)S(1)} %concatenate.21), channel_id=1, source_target_pairs={{0,2},{1,3},{2,0},{3,1},{4,6},{5,7},{6,4},{7,5},{8,10},{9,11},{10,... | collective-permute-start | bytes 1081352 | tf_op jit(solution)/shard_map/ppermute | solution.py:323
  6.8 8.2 %collective-permute-start.4 = (bf16[272,512]{1,0:T(8,128)(2,1)S(1)}, bf16[272,512]{1,0:T(8,128)(2,1)S(1)}, u32[]{:S(2)}, u32[]{:S(2)}) collective-permute-start(bf16[272,512]{1,0:T(8,128)(2,1)S(1)} %pad_maximum_fusion.refs_2_), channel_id=1, source_target_pairs={{0,4},{1,5},{2,6},{3,7},{4,8},{5,9},{6,10},{7,11},{8,12},{9,13},{1... | collective-permute-start | bytes 835592 | tf_op jit(solution)/shard_map/ppermute | solution.py:323
  15.0 8.2 %collective-permute-start.5 = (bf16[272,512]{1,0:T(8,128)(2,1)S(1)}, bf16[272,512]{1,0:T(8,128)(2,1)S(1)}, u32[]{:S(2)}, u32[]{:S(2)}) collective-permute-start(bf16[272,512]{1,0:T(8,128)(2,1)S(1)} %collective-permute-done.4.refs_2_), channel_id=1, source_target_pairs={{0,4},{1,5},{2,6},{3,7},{4,8},{5,9},{6,10},{7,11},{8,12},{9,13},{1... | collective-permute-start | bytes 835592 | tf_op jit(solution)/shard_map/ppermute | solution.py:323
  19.2 5.6 %collective-permute-start.1 = (bf16[256,896]{1,0:T(8,128)(2,1)S(1)}, bf16[256,896]{1,0:T(8,128)(2,1)S(1)}, u32[]{:S(2)}, u32[]{:S(2)}) collective-permute-start(bf16[256,896]{1,0:T(8,128)(2,1)S(1)} %maximum_maximum_fusion), channel_id=1, source_target_pairs={{0,1},{1,0},{2,3},{3,2},{4,5},{5,4},{6,7},{7,6},{8,9},{9,8},{10,11... | collective-permute-start | bytes 1376264 | tf_op jit(solution)/shard_map/ppermute | solution.py:323
  23.3 30.5 %collective-permute-start.10 = (bf16[272,512]{1,0:T(8,128)(2,1)S(1)}, bf16[272,512]{1,0:T(8,128)(2,1)S(1)}, u32[]{:S(2)}, u32[]{:S(2)}) collective-permute-start(bf16[272,512]{1,0:T(8,128)(2,1)S(1)} %get-tuple-element.24), channel_id=1, source_target_pairs={{0,2},{1,3},{2,0},{3,1},{4,6},{5,7},{6,4},{7,5},{8,10},{9,11},{10,... | collective-permute-start | bytes 835592 | tf_op jit(solution)/shard_map/ppermute | solution.py:323
  23.6 30.3 %collective-permute-start.7 = (bf16[272,512]{1,0:T(8,128)(2,1)S(1)}, bf16[272,512]{1,0:T(8,128)(2,1)S(1)}, u32[]{:S(2)}, u32[]{:S(2)}) collective-permute-start(bf16[272,512]{1,0:T(8,128)(2,1)S(1)} %get-tuple-element.25), channel_id=1, source_target_pairs={{0,2},{1,3},{2,0},{3,1},{4,6},{5,7},{6,4},{7,5},{8,10},{9,11},{10,... | collective-permute-start | bytes 835592 | tf_op jit(solution)/shard_map/ppermute | solution.py:323
  29.2 29.3 %copy-start = (bf16[2,128,2048]{2,1,0:T(8,128)(2,1)S(1)}, bf16[2,128,2048]{2,1,0:T(8,128)(2,1)}, u32[]{:S(2)}) copy-start(bf16[2,128,2048]{2,1,0:T(8,128)(2,1)} %refs_0_.5) | copy-start | bytes 3145732
  45.5 10.7 %collective-permute-start.2 = (bf16[2,128,512]{2,1,0:T(8,128)(2,1)S(1)}, bf16[2,128,512]{2,1,0:T(8,128)(2,1)S(1)}, u32[]{:S(2)}, u32[]{:S(2)}) collective-permute-start(bf16[2,128,512]{2,1,0:T(8,128)(2,1)S(1)} %get-tuple-element.18), channel_id=1, source_target_pairs={{0,2},{1,3},{2,0},{3,1},{4,6},{5,7},{6,4},{7,5},{8,10},{9,11},{10,... | collective-permute-start | bytes 786440 | tf_op jit(solution)/shard_map/ppermute | solution.py:323
  45.8 12.5 %collective-permute-start.12 = (bf16[272,512]{1,0:T(8,128)(2,1)S(1)}, bf16[272,512]{1,0:T(8,128)(2,1)S(1)}, u32[]{:S(2)}, u32[]{:S(2)}) collective-permute-start(bf16[272,512]{1,0:T(8,128)(2,1)S(1)} %pad_maximum_fusion.refs_2_), channel_id=1, source_target_pairs={{0,1},{2,3},{4,5},{6,7},{8,9},{10,11},{12,13},{14,15},{16,17},{18,... | collective-permute-start | bytes 835592 | tf_op jit(solution)/shard_map/ppermute | solution.py:323
  47.1 16.0 %collective-permute-start.9 = (bf16[272,512]{1,0:T(8,128)(2,1)S(1)}, bf16[272,512]{1,0:T(8,128)(2,1)S(1)}, u32[]{:S(2)}, u32[]{:S(2)}) collective-permute-start(bf16[272,512]{1,0:T(8,128)(2,1)S(1)} %collective-permute-done.4.refs_2_), channel_id=1, source_target_pairs={{0,1},{1,0},{2,3},{3,2},{4,5},{5,4},{6,7},{7,6},{8,9},{9,8},{10,11... | collective-permute-start | bytes 835592 | tf_op jit(solution)/shard_map/ppermute | solution.py:323
  53.8 9.3 %collective-permute-start.11 = (bf16[272,512]{1,0:T(8,128)(2,1)S(1)}, bf16[272,512]{1,0:T(8,128)(2,1)S(1)}, u32[]{:S(2)}, u32[]{:S(2)}) collective-permute-start(bf16[272,512]{1,0:T(8,128)(2,1)S(1)} %collective-permute-done.10.refs_4_), channel_id=1, source_target_pairs={{0,1},{1,0},{2,3},{3,2},{4,5},{5,4},{6,7},{7,6},{8,9},{9,8},{10,11... | collective-permute-start | bytes 835592 | tf_op jit(solution)/shard_map/ppermute | solution.py:323
  53.9 20.2 %collective-permute-start.6 = (bf16[272,512]{1,0:T(8,128)(2,1)S(1)}, bf16[272,512]{1,0:T(8,128)(2,1)S(1)}, u32[]{:S(2)}, u32[]{:S(2)}) collective-permute-start(bf16[272,512]{1,0:T(8,128)(2,1)S(1)} %collective-permute-done.5.refs_2_), channel_id=1, source_target_pairs={{1,0},{3,2},{5,4},{7,6},{9,8},{11,10},{13,12},{15,14},{17,16},{19,... | collective-permute-start | bytes 835592 | tf_op jit(solution)/shard_map/ppermute | solution.py:323
  56.2 17.9 %collective-permute-start.8 = (bf16[272,512]{1,0:T(8,128)(2,1)S(1)}, bf16[272,512]{1,0:T(8,128)(2,1)S(1)}, u32[]{:S(2)}, u32[]{:S(2)}) collective-permute-start(bf16[272,512]{1,0:T(8,128)(2,1)S(1)} %collective-permute-done.7.refs_4_), channel_id=1, source_target_pairs={{0,1},{1,0},{2,3},{3,2},{4,5},{5,4},{6,7},{7,6},{8,9},{9,8},{10,11... | collective-permute-start | bytes 835592 | tf_op jit(solution)/shard_map/ppermute | solution.py:323
  58.4 25.2 %collective-permute-start.3 = (bf16[2,128,512]{2,1,0:T(8,128)(2,1)S(1)}, bf16[2,128,512]{2,1,0:T(8,128)(2,1)S(1)}, u32[]{:S(2)}, u32[]{:S(2)}) collective-permute-start(bf16[2,128,512]{2,1,0:T(8,128)(2,1)S(1)} %pad_maximum_fusion.1), channel_id=1, source_target_pairs={{0,1},{1,0},{2,3},{3,2},{4,5},{5,4},{6,7},{7,6},{8,9},{9,8},{10,11... | collective-permute-start | bytes 786440 | tf_op jit(solution)/shard_map/ppermute | solution.py:323
  61.8 1.3 %copy-start.1 = (f32[2,128,2048]{2,1,0:T(8,128)}, f32[2,128,2048]{2,1,0:T(8,128)S(1)}, u32[]{:S(2)}) copy-start(f32[2,128,2048]{2,1,0:T(8,128)S(1)} %get-tuple-element.20.refs_6_) | copy-start | bytes 6291460

commit v2 on v0

v2 whole, which is shorter than its diff:
```python
import functools
import math

import jax
import jax.numpy as jnp
from jax import lax
from jax.experimental import pallas as pl
from jax.experimental.pallas import tpu as pltpu
from jax.sharding import PartitionSpec as P

KV_HEADS = 4
HEAD = 128
ROW = 4
FAR = -1e30
SCALE = HEAD ** (-0.5) * math.log2(math.e)
F32 = jnp.float32
BF16 = jnp.bfloat16
VMEM = pltpu.VMEM
IN_SMEM = pl.BlockSpec(memory_space=pltpu.SMEM)
IN_VMEM = pl.BlockSpec(memory_space=pltpu.VMEM)
LOGS = 16


def nt_dot(a, b):
    return lax.dot_general(a, b, (((1,), (1,)), ((), ())), preferred_element_type=F32)


def tn_dot(a, b, precision=None):
    return lax.dot_general(
        a, b, (((0,), (0,)), ((), ())), preferred_element_type=F32, precision=precision
    )


def lanes(number, width):
    return pl.ds(pl.multiple_of(number * width, width), width)


def call(kernel, name, micros, place, args, outs, scratch=()):
    return pl.pallas_call(
        kernel,
        name=name,
        out_shape=outs,
        in_specs=[IN_SMEM] + [IN_VMEM] * len(args),
        out_specs=jax.tree.map(lambda _: IN_VMEM, outs),
        scratch_shapes=list(scratch),
        cost_estimate=pl.CostEstimate(
            flops=int(micros * 1.15e9), bytes_accessed=0, transcendentals=0
        ),
        compiler_params=pltpu.CompilerParams(vmem_limit_bytes=24 * 1024 * 1024),
    )(place, *args)


def shaped(*shape, dtype=BF16):
    return jax.ShapeDtypeStruct(shape, dtype)


def pack_kernel(place, x_ref, write_ref, read_ref, codes_ref, kv_ref, seg_ref, own, small, to_c):
    core = place[0]
    tokens, state = write_ref.shape
    heads = codes_ref.shape[1]
    own[0:tokens, :] = kv_ref[0]
    own[tokens : 2 * tokens, :] = kv_ref[1]
    seg = (seg_ref[...] + 1).astype(F32).astype(BF16)
    own[2 * tokens :, 0:tokens] = jnp.broadcast_to(seg, (16, tokens))
    own[2 * tokens :, tokens:] = jnp.zeros((16, own.shape[1] - tokens), BF16)
    codes = codes_ref[...]
    high = (codes >> 6).astype(F32)
    low = (codes & 63).astype(F32)
    gap = jnp.zeros((tokens, 64 - heads), F32)
    both = jnp.concatenate([high, gap, low, gap], axis=1).astype(BF16)
    small[:, 0:state] = write_ref[...]
    small[:, state : 2 * state] = read_ref[...]
    small[:, 2 * state :] = both
    half = x_ref.shape[1] // 2
    to_c[:, 0:half] = x_ref[:, lanes(1 - core, half)]
    to_c[:, half : half + state] = write_ref[...]
    to_c[:, half + state : half + 2 * state] = read_ref[...]
    to_c[:, half + 2 * state :] = both


def attend_kernel(kinds, first, last, place, q_ref, own_ref, *refs):
    count = len(kinds)
    rows = q_ref.shape[1]
    pieces = refs[:count]
    at = count
    if not first:
        acc_in, peak_in, sum_in = refs[at : at + 3]
        at += 3
    if last:
        out_ref = refs[at]
        at += 1
    else:
        acc_out, peak_out, sum_out = refs[at : at + 3]
        at += 3
    k_all, v_all, bias = refs[at : at + 3]
    core = place[0]
    chip = place[3]
    codes = own_ref[2 * rows : 2 * rows + 16, 0:rows].astype(F32)
    mine = jnp.transpose(jnp.broadcast_to(codes[0:1], (rows, rows)))
    i = lax.broadcasted_iota(jnp.int32, (rows, rows), 0)
    j = lax.broadcasted_iota(jnp.int32, (rows, rows), 1)
    for n, (behind, other) in enumerate(kinds):
        theirs = pieces[n][2 * rows : 2 * rows + 16, 0:rows].astype(F32)[0:1]
        if behind == 0 and not other:
            ok = j <= i
        elif behind == 0:
            ok = j < rows * core
        elif behind == 4 and not other:
            ok = j > i + jnp.where(chip >= behind, 0, rows)
        elif behind == 4:
            ok = j < jnp.where((chip >= behind) & (core == 0), rows, 0)
        else:
            ok = j < jnp.where(chip >= behind, rows, 0)
        bias[:, n * rows : (n + 1) * rows] = jnp.where((theirs == mine) & ok, 0.0, FAR)
    v_all[:, HEAD:] = jnp.ones((count * rows, HEAD), BF16)
    group = q_ref.shape[2] // HEAD // KV_HEADS

    def one(head, _):
        here = lanes(head, HEAD)
        for n in range(count):
            k_all[n * rows : (n + 1) * rows, :] = pieces[n][0:rows, here]
            v_all[n * rows : (n + 1) * rows, 0:HEAD] = pieces[n][rows : 2 * rows, here]
        for layer in range(2):
            for r in range(group):
                cols = lanes(head * group + r, HEAD)
                scores = nt_dot(q_ref[layer, :, cols], k_all[...]) * SCALE + bias[...]
                peak = jnp.max(scores, axis=1, keepdims=True)
                if first:
                    probs = jnp.exp2(scores - peak)
                else:
                    old = peak_in[layer, :, cols]
                    peak = jnp.maximum(old, peak)
                    fade = jnp.exp2(old - peak)
                    probs = jnp.concatenate(
                        [
                            jnp.exp2(scores[:, n * rows : (n + 1) * rows] - peak)
                            for n in range(count)
                        ],
                        axis=1,
                    )
                both = jnp.dot(probs.astype(BF16), v_all[...], preferred_element_type=F32)
                acc = both[:, :HEAD]
                total = both[:, HEAD:]
                if not first:
                    acc = acc + fade * acc_in[layer, :, cols]
                    total = total + fade * sum_in[layer, :, cols]
                if last:
                    out_ref[layer, :, cols] = (acc / total).astype(BF16)
                else:
                    acc_out[layer, :, cols] = acc
                    sum_out[layer, :, cols] = total
                    peak_out[layer, :, cols] = jnp.broadcast_to(peak, (rows, HEAD))
        return _

    lax.fori_loop(0, KV_HEADS, one, 0)


def attend(place, queries, own, pieces, kinds, carry, last):
    layers, tokens, width = queries.shape
    count = len(kinds)
    partial = shaped(layers, tokens, width, dtype=F32)
    return call(
        functools.partial(attend_kernel, kinds, carry is None, last),
        "attend%d" % kinds[-1][0],
        0.5 + 1.05 * count,
        place,
        [queries, own] + list(pieces) + list(carry or ()),
        shaped(layers, tokens, width) if last else (partial,) * 3,
        [
            VMEM((count * tokens, HEAD), BF16),
            VMEM((count * tokens, 2 * HEAD), BF16),
            VMEM((tokens, count * tokens), F32),
        ],
    )


def spread(columns, pairs, width):
    low = lax.broadcasted_iota(jnp.int32, (1, 2 * width), 1) < width
    parts = [
        jnp.where(low, columns[:, 2 * k : 2 * k + 1], columns[:, 2 * k + 1 : 2 * k + 2])
        for k in range(pairs)
    ]
    return jnp.concatenate(parts, axis=1)


def put_logs(ref, state, logs):
    one = logs.astype(BF16)
    rest = logs - one.astype(F32)
    two = rest.astype(BF16)
    three = (rest - two.astype(F32)).astype(BF16)
    row = lax.broadcasted_iota(jnp.int32, (LOGS, logs.shape[1]), 0)
    ref[state:, :] = jnp.where(row == 0, one, jnp.where(row == 1, two, three))


def get_logs(ref, state, cols):
    parts = ref[state:, cols].astype(F32)
    return parts[0:1] + parts[1:2] + parts[2:3]


def local_kernel(
    heads, state, place, x_ref, own_ref, c_ref, rate_ref, mixed_ref, tail_ref, run_ref, read_ref,
    xs, sm
):
    tokens = x_ref.shape[0]
    cols = xs.shape[2]
    width = cols // heads
    core = place[0]
    xs[core] = x_ref[:, lanes(core, cols)]
    sm[core] = own_ref[...]
    xs[1 - core] = c_ref[:, 0:cols]
    sm[1 - core] = c_ref[:, cols:]
    i = lax.broadcasted_iota(jnp.int32, (tokens, tokens), 0)
    j = lax.broadcasted_iota(jnp.int32, (tokens, tokens), 1)
    causal = j <= i
    lower_ones = causal.astype(F32)
    upper_ones = (i <= j).astype(F32)
    low = lax.broadcasted_iota(jnp.int32, (1, 2 * width), 1) < width
    rates = rate_ref[...]
    shift = lax.rem(128 - core * heads, 128)
    kept = None
    offset = None
    for b in range(2):
        write = sm[b, :, 0:state]
        read = sm[b, :, state : 2 * state]
        read_ref[b] = read
        high = sm[b, :, 2 * state :].astype(F32)
        little = pltpu.roll(high, 64, 1)
        level = jnp.floor(high * 0.0625)
        lower = high * 64.0 + little - 1024.0 * level
        step = -rates * (1.0 + lower * (1.0 / 128.0)) - 0.125 * level
        step = jnp.where(j < heads, pltpu.roll(step, shift, 1), 0.0)
        run = jnp.dot(
            lower_ones, step, preferred_element_type=F32, precision=lax.Precision.HIGHEST
        )
        run_t = tn_dot(step, upper_ones, lax.Precision.HIGHEST)
        end = run[tokens - 1 : tokens, :]
        run_ref[b] = run if b == 0 else run + offset
        offset = end if b == 0 else offset + end
        inner = jnp.where(causal, nt_dot(read, write), 0.0)
        to_end = jnp.exp(end - run)
        fade = jnp.exp(run)
        if b > 0:
            seen = jnp.dot(read, kept.astype(BF16), preferred_element_type=F32)
        scaled = []
        for pair in range(heads // 2):
            part = slice(pair * 2 * width, (pair + 1) * 2 * width)
            tile = xs[b, :, part]
            mixes = []
            for h in (2 * pair, 2 * pair + 1):
                gap = jnp.minimum(run[:, h : h + 1] - run_t[h : h + 1, :], 0.0)
                mixes.append((inner * jnp.exp(gap)).astype(BF16))
            zero = jnp.zeros_like(tile)
            stacked = jnp.concatenate(
                [jnp.where(low, tile, zero), jnp.where(low, zero, tile)], axis=0
            )
            mixed = jnp.dot(jnp.concatenate(mixes, axis=1), stacked, preferred_element_type=F32)
            if b > 0:
                mixed = mixed + seen[:, part] * jnp.where(
                    low, fade[:, 2 * pair : 2 * pair + 1], fade[:, 2 * pair + 1 : 2 * pair + 2]
                )
            mixed_ref[b, :, part] = mixed
            weight = jnp.where(
                low, to_end[:, 2 * pair : 2 * pair + 1], to_end[:, 2 * pair + 1 : 2 * pair + 2]
            )
            scaled.append((weight * tile.astype(F32)).astype(BF16))
        added = tn_dot(write, jnp.concatenate(scaled, axis=1))
        if b > 0:
            added = spread(jnp.exp(end), heads // 2, width) * kept + added
        kept = added
    tail_ref[0:state, :] = kept.astype(BF16)
    put_logs(tail_ref, state, spread(offset, heads // 2, width))


def row_kernel(state, place, tail_ref, y_ref, out_ref):
    y = place[1]
    cols = out_ref.shape[1]
    here = lanes(y, cols)
    mine = tail_ref[0:state, here].astype(F32)
    theirs = y_ref[0:state, here].astype(F32)
    my_log = get_logs(tail_ref, state, here)
    their_log = get_logs(y_ref, state, here)
    later = jnp.where(y == 0, theirs, mine)
    earlier = jnp.where(y == 0, mine, theirs)
    decay = jnp.exp(jnp.where(y == 0, their_log, my_log))
    out_ref[0:state, :] = (later + decay * earlier).astype(BF16)
    put_logs(out_ref, state, my_log + their_log)


def hop_kernel(state, distance, last, place, span_ref, before_ref, new_ref, *outs):
    ok = place[2] >= distance
    new = jnp.where(ok, new_ref[0:state, :].astype(F32), 0.0)
    logs = jnp.where(ok, get_logs(new_ref, state, slice(None)), 0.0)
    joined = [(before_ref, outs[0])] if last else [(span_ref, outs[0]), (before_ref, outs[1])]
    for old_ref, out_ref in joined:
        if old_ref is None:
            out_ref[0:state, :] = new.astype(BF16)
            put_logs(out_ref, state, logs)
        else:
            old_logs = get_logs(old_ref, state, slice(None))
            out_ref[0:state, :] = (
                old_ref[0:state, :].astype(F32) + jnp.exp(old_logs) * new
            ).astype(BF16)
            if not last:
                put_logs(out_ref, state, old_logs + logs)


def hop(state, distance, last, place, span, before, new):
    def kernel(place, *refs):
        refs = list(refs)
        span_ref = refs.pop(0)
        before_ref = refs.pop(0) if before is not None else None
        hop_kernel(state, distance, last, place, span_ref, before_ref, *refs)

    out = shaped(state if last else state + LOGS, span.shape[1])
    return call(
        kernel,
        "hop%d" % distance,
        0.6,
        place,
        [span] + ([before] if before is not None else []) + [new],
        (out,) if last else (out, out),
    )


def finish_kernel(
    heads, state, place, mixed_ref, run_ref, read_ref, mine_ref, other_ref, y_ref, self_ref, c_ref
):
    core = place[0]
    y = place[1]
    cols = mixed_ref.shape[2]
    width = cols // heads
    mine = mine_ref[...]
    other = other_ref[...]
    row_in = jnp.concatenate(
        [jnp.where(y == 0, mine, other), jnp.where(y == 0, other, mine)], axis=1
    ).astype(F32)
    decay = jnp.exp(get_logs(y_ref, state, slice(None)))
    entering = jnp.where(y == 0, row_in, y_ref[0:state, :].astype(F32) + decay * row_in)
    entering = entering.astype(BF16)
    a = lax.broadcasted_iota(jnp.int32, (4 * width, 2 * width), 0)
    b = lax.broadcasted_iota(jnp.int32, (4 * width, 2 * width), 1)
    same = (lax.rem(a, 2 * width) < width) == (b < width)
    average = jnp.where(same, 1.0 / width, 0.0).astype(BF16)
    low = lax.broadcasted_iota(jnp.int32, (1, 2 * width), 1) < width
    for out_ref, at in ((c_ref, 1 - core), (self_ref, core)):
        seen = jnp.dot(read_ref[at], entering, preferred_element_type=F32)
        fade = jnp.exp(run_ref[at])
        for pair in range(heads // 2):
            part = slice(pair * 2 * width, (pair + 1) * 2 * width)
            tile = mixed_ref[at, :, part] + seen[:, part] * jnp.where(
                low, fade[:, 2 * pair : 2 * pair + 1], fade[:, 2 * pair + 1 : 2 * pair + 2]
            )
            square = tile * tile
            big = square.astype(BF16)
            small = (square - big.astype(F32)).astype(BF16)
            mean = jnp.dot(
                jnp.concatenate([big, small], axis=1), average, preferred_element_type=F32
            )
            out_ref[:, part] = (tile * lax.rsqrt(mean + 1e-05)).astype(BF16)


def collect_kernel(place, self_ref, c_ref, out_ref):
    core = place[0]
    cols = self_ref.shape[1]
    out_ref[:, lanes(core, cols)] = self_ref[...]
    out_ref[:, lanes(1 - core, cols)] = c_ref[...]


def after(value, *others):
    return lax.optimization_barrier((value, *others))[0]


def shards(
    ssm_inputs, state_write, state_read, decay_codes, decay_rate, queries, keys_values, segment_ids
):
    tokens, channels = ssm_inputs.shape
    heads = decay_rate.shape[0]
    state = state_write.shape[1]
    cols = channels // 2
    devices = lax.axis_size("seq")
    rows = devices // ROW
    rank = lax.axis_index("seq")
    core, y = rank % 2, (rank // 2) % 2
    place = jnp.stack([core, y, rank // ROW, rank // 2]).astype(jnp.int32)
    send = lambda x, route: lax.ppermute(x, "seq", [(i, route(i)) for i in range(devices)])
    swap_c = lambda i: i ^ 1
    swap_y = lambda i: i ^ 2
    up = lambda n: lambda i: (i + n * ROW) % devices
    kv_width = keys_values.shape[2]
    rates = jnp.pad(decay_rate, (0, 128 - heads))[None, :]

    own, small, to_c = call(
        pack_kernel,
        "pack",
        1.5,
        place,
        [ssm_inputs, state_write, state_read, decay_codes, keys_values, segment_ids[None, :]],
        (
            shaped(2 * tokens + 16, kv_width),
            shaped(tokens, 2 * state + 128),
            shaped(tokens, cols + 2 * state + 128),
        ),
    )
    from_c = send(to_c, swap_c)
    behind2 = send(own, up(1))
    partner = send(own, swap_c)

    mixed, tail, run, reads = call(
        functools.partial(local_kernel, heads // 2, state),
        "local",
        4.3,
        place,
        [ssm_inputs, small, from_c, rates],
        (
            shaped(2, tokens, cols, dtype=F32),
            shaped(state + LOGS, cols),
            shaped(2, tokens, 128, dtype=F32),
            shaped(2, tokens, state),
        ),
        [VMEM((2, tokens, cols), BF16), VMEM((2, tokens, 2 * state + 128), BF16)],
    )
    tail_y = send(tail, swap_y)
    behind4 = send(behind2, up(1))
    behind1 = send(jnp.where(y == 0, own, behind2), swap_y)
    behind2c = send(behind2, swap_c)
    carry = attend(
        place,
        after(queries, tail),
        own,
        [own, partner],
        ((0, False), (0, True)),
        None,
        False,
    )

    span = call(
        functools.partial(row_kernel, state),
        "row",
        0.6,
        place,
        [tail, tail_y],
        shaped(state + LOGS, cols // 2),
    )
    before = None
    distance = 1
    while distance < rows:
        new = send(span, up(distance))
        last = 2 * distance >= rows
        out = hop(state, distance, last, place, span, before, new)
        span, before = (None, out[0]) if last else out
        if distance == 1:
            behind3 = send(jnp.where(y == 0, behind2, behind4), swap_y)
            behind1c = send(behind1, swap_c)
            behind4c = send(behind4, swap_c)
            carry = attend(
                place,
                after(queries, carry[0]),
                own,
                [behind2, behind2c, behind1, behind1c],
                ((2, False), (2, True), (1, False), (1, True)),
                carry,
                False,
            )
        distance *= 2
    behind3c = send(behind3, swap_c)
    other_half = send(before, swap_y)
    mine, for_c = call(
        functools.partial(finish_kernel, heads // 2, state),
        "finish",
        1.7,
        place,
        [mixed, run, reads, before, other_half, tail_y],
        (shaped(tokens, cols),) * 2,
    )
    back_c = send(for_c, swap_c)
    attn_output = attend(
        place,
        queries,
        own,
        [behind4, behind4c, behind3, behind3c],
        ((4, False), (4, True), (3, False), (3, True)),
        carry,
        True,
    )
    ssm_output = call(
        collect_kernel, "collect", 0.8, place, [mine, back_c], shaped(tokens, channels)
    )
    return (ssm_output, attn_output)


def solution(mesh):
    return jax.shard_map(
        shards,
        mesh=mesh,
        in_specs=(
            P(("groups", "seq"), None),
            P(("groups", "seq"), None),
            P(("groups", "seq"), None),
            P(("groups", "seq"), None),
            P(),
            P(None, ("groups", "seq"), None),
            P(None, ("groups", "seq"), None),
            P(("groups", "seq")),
        ),
        out_specs=(P(("groups", "seq"), None), P(None, ("groups", "seq"), None)),
        check_vma=False,
    )
```

time: 290 us -> 60.7 us (0.21)
  starting transfers between devices: 93.5 us -> 17.5 us
  matrix products: 48.4 us -> 0 us
  blocking collectives: 33.1 us -> 0 us
  other arithmetic: 25.9 us -> 0.13 us
  Pallas kernels: 0 us -> 23.6 us
  waiting for transfers between devices: 33.8 us -> 13.2 us
  local copies, waits for them, and re-layouts: 22.5 us -> 4.99 us
  loops' own time: 16.3 us -> 0 us
  between operations: 14.5 us -> 0.79 us
    ppermute x16 -> x15, starting transfers between devices: 93.5 us -> 17.5 us  [shards(): lax.ppermute(x, 'seq', [(i, route(i)) for i in range(devices)])]
    all_gather x1 -> x0, blocking collectives: 33.1 us -> none  [entering(): pieces = jax.tree.map(lambda part: lax.all_gather(part, axis), value)]
    dot_general x12 -> x0, matrix products: 29.7 us -> none  [the longest x8 26 us: attend_item(): jnp.einsum('gqk,kd->gqd', probs.astype(jnp.bfloat16), head_values, prefer...]
    pallas_call x0 -> x10, Pallas kernels: none -> 23.6 us  [call(): pl.pallas_call(kernel, name=name, out_shape=outs, in_specs=[IN_SMEM] + [I...]
    select_n x15 -> x1, other arithmetic: 21.9 us -> 0.05 us  [shards(): behind1 = send(jnp.where(y == 0, own, behind2), swap_y)]
    ppermute x16 -> x15, waiting for transfers between devices: 33.8 us -> 13.2 us  [shards(): lax.ppermute(x, 'seq', [(i, route(i)) for i in range(devices)])]
    sub x8 -> x0, matrix products: 18.6 us -> none  [attend_item(): probs = jnp.where(allowed[None], jnp.exp(masked - peak), 0.0)]
    another operation x2 -> x0, loops' own time: 16.3 us -> none  [the longest x1 15.7 us: shards(): lax.map(attend_item, (query_heads, jnp.arange(2 * KV_HEADS, dtype=jnp.int...]
  transfers between devices with their start and end apart: 17 -> 15, of which waited for: 9 -> 4; matrix products, arithmetic and copies ran while one was open for 23% -> 0% of each run, Pallas kernels for 0% -> 36%
where the time goes in v2:
time: 60.7 us; the launch traced here: 60.3 us
  Pallas kernels  23.6 us (39%)
  starting transfers between devices  17.5 us (29%)
  waiting for transfers between devices  13.2 us (22%)
  local copies, waits for them, and re-layouts  4.99 us (8%)
  between operations  0.79 us (1%)
    pallas_call x10, Pallas kernels, call(): pl.pallas_call(kernel, name=name, out_shape=outs, in_specs=[IN_SMEM] + [I...  23.6 us
    ppermute x15, starting transfers between devices, shards(): lax.ppermute(x, 'seq', [(i, route(i)) for i in range(devices)])  17.5 us
    ppermute x15, waiting for transfers between devices, shards(): lax.ppermute(x, 'seq', [(i, route(i)) for i in range(devices)])  13.2 us
    unnamed x15, local copies, waits for them, and re-layouts  4.99 us
  transfers between devices with their start and end apart: 15, of which 4 were waited for; matrix products, arithmetic and copies ran while one was open for 0% of the time, Pallas kernels for 36%

profile of v2, /device:TPU:1, one launch (start us, length us, event | category | flops | bytes accessed | tf_op | source)
XLA Modules:
  0.0 60.3 jit_solution(4984073623886558423)
XLA Ops:
  0.7 0.8 %copy.10.codes_ref = s32[128,32]{1,0:T(8,128)S(1)} copy(s32[128,32]{0,1:T(8,128)} %param.11) | data formatting | bytes 32768 | tf_op args[3]
  1.5 0.1 pad_add_fusion.place
  1.6 0.0 copy-start.1
  1.6 1.0 %copy-done.1 = bf16[128,2048]{1,0:T(8,128)(2,1)S(1)} copy-done((bf16[128,2048]{1,0:T(8,128)(2,1)S(1)}, bf16[128,2048]{1,0:T(8,128)(2,1)}, u32[]{:S(2)}) %copy-start.1) | copy-done | bytes 524312
  2.6 0.0 copy-start.2
  2.6 0.9 %copy-done.2 = bf16[2,128,512]{2,1,0:T(8,128)(2,1)S(1)} copy-done((bf16[2,128,512]{2,1,0:T(8,128)(2,1)S(1)}, bf16[2,128,512]{2,1,0:T(8,128)(2,1)}, u32[]{:S(2)}) %copy-start.2) | copy-done | bytes 262168
  3.6 0.0 copy-start.3
  3.6 0.8 %copy-done.3 = bf16[128,128]{1,0:T(8,128)(2,1)S(1)} copy-done((bf16[128,128]{1,0:T(8,128)(2,1)S(1)}, bf16[128,128]{1,0:T(8,128)(2,1)}, u32[]{:S(2)}) %copy-start.3) | copy-done | bytes 32792
  4.3 0.0 copy-start.4
  4.3 0.8 %copy-done.4 = bf16[128,128]{1,0:T(8,128)(2,1)S(1)} copy-done((bf16[128,128]{1,0:T(8,128)(2,1)S(1)}, bf16[128,128]{1,0:T(8,128)(2,1)}, u32[]{:S(2)}) %copy-start.4) | copy-done | bytes 32792
  5.1 0.0 copy-start.5
  5.1 0.7 %copy-done.5 = s32[128]{0:T(128)S(1)} copy-done((s32[128]{0:T(128)S(1)}, s32[128]{0:T(128)}, u32[]{:S(2)}) %copy-start.5) | copy-done | bytes 536
  5.8 0.0 copy-start.6
  5.8 0.6 %pack.1 = (bf16[272,512]{1,0:T(8,128)(2,1)S(1)}, bf16[128,384]{1,0:T(8,128)(2,1)S(1)}, bf16[128,1408]{1,0:T(8,128)(2,1)S(1)}) custom-call(s32[4]{0:T(128)S(1)} %pad_add_fusion.place, bf16[128,2048]{1,0:T(8,128)(2,1)S(1)} %copy-done.1, bf16[128,128]{1,0:T(8,128)(2,1)S(1)} %copy-done.3, bf16[128,128]{1,0:T(8,128)(2,1)S(1)} %copy-done.4, ...), custom_call_target="tpu_custom_call" | custom-call | flops 1724999936 | tf_op jit(solution)/shard_map/pack/pallas_call | solution.py:39
  6.4 0.1 collective-permute-start
  6.5 2.7 %collective-permute-start.6 = (bf16[272,512]{1,0:T(8,128)(2,1)S(1)}, bf16[272,512]{1,0:T(8,128)(2,1)S(1)}, u32[]{:S(2)}, u32[]{:S(2)}) collective-permute-start(bf16[272,512]{1,0:T(8,128)(2,1)S(1)} %get-tuple-element.31.own_ref.refs_0_), channel_id=1, source_target_pairs={{0,4},{1,5},{2,6},{3,7},{4,8},{5,9},{6,10},{7,11},{8,12},{9,13},{1... | collective-permute-start | bytes 835592 | tf_op jit(solution)/shard_map/ppermute | solution.py:385
  9.2 0.0 copy-done.6
  9.3 0.0 collective-permute-done.c_ref
  9.3 3.8 %local.1 = (f32[2,128,1024]{2,1,0:T(8,128)S(1)}, bf16[144,1024]{1,0:T(8,128)(2,1)S(1)}, f32[2,128,128]{2,1,0:T(8,128)S(1)}, bf16[2,128,128]{2,1,0:T(8,128)(2,1)S(1)}) custom-call(s32[4]{0:T(128)S(1)} %pad_add_fusion.place, bf16[128,2048]{1,0:T(8,128)(2,1)S(1)} %copy-done.1, bf16[128,384]{1,0:T(8,128)(2,1)S(1)} %get-tuple-element.21.own_ref, ...), custom_call_target="tpu_custom_call" | custom-call | flops 4944999936 | tf_op jit(solution)/shard_map/local/pallas_call | solution.py:39
  13.1 1.3 %collective-permute-start.1 = (bf16[144,1024]{1,0:T(8,128)(2,1)S(1)}, bf16[144,1024]{1,0:T(8,128)(2,1)S(1)}, u32[]{:S(2)}, u32[]{:S(2)}) collective-permute-start(bf16[144,1024]{1,0:T(8,128)(2,1)S(1)} %get-tuple-element.26.tail_ref), channel_id=1, source_target_pairs={{0,2},{1,3},{2,0},{3,1},{4,6},{5,7},{6,4},{7,5},{8,10},{9,11},{10,... | collective-permute-start | bytes 884744 | tf_op jit(solution)/shard_map/ppermute | solution.py:385
  14.4 3.9 %collective-permute-done.6.refs_0_ = bf16[272,512]{1,0:T(8,128)(2,1)S(1)} collective-permute-done((bf16[272,512]{1,0:T(8,128)(2,1)S(1)}, bf16[272,512]{1,0:T(8,128)(2,1)S(1)}, u32[]{:S(2)}, u32[]{:S(2)}) %collective-permute-start.6) | collective-permute-done | bytes 278560 | tf_op jit(solution)/shard_map/ppermute | solution.py:385
  18.2 0.0 collective-permute-start.7
  18.2 3.1 %collective-permute-done.1.y_ref = bf16[144,1024]{1,0:T(8,128)(2,1)S(1)} collective-permute-done((bf16[144,1024]{1,0:T(8,128)(2,1)S(1)}, bf16[144,1024]{1,0:T(8,128)(2,1)S(1)}, u32[]{:S(2)}, u32[]{:S(2)}) %collective-permute-start.1) | collective-permute-done | bytes 294944 | tf_op jit(solution)/shard_map/ppermute | solution.py:385
  21.4 0.6 %row.1.refs_0_ = bf16[144,512]{1,0:T(8,128)(2,1)S(1)} custom-call(s32[4]{0:T(128)S(1)} %pad_add_fusion.place, bf16[144,1024]{1,0:T(8,128)(2,1)S(1)} %get-tuple-element.26.tail_ref, bf16[144,1024]{1,0:T(8,128)(2,1)S(1)} %collective-permute-done.1.y_ref), custom_call_target="tpu_custom_call" | custom-call | flops 690000000 | tf_op jit(solution)/shard_map/row/pallas_call | solution.py:39
  22.0 1.3 %collective-permute-start.2 = (bf16[144,512]{1,0:T(8,128)(2,1)S(1)}, bf16[144,512]{1,0:T(8,128)(2,1)S(1)}, u32[]{:S(2)}, u32[]{:S(2)}) collective-permute-start(bf16[144,512]{1,0:T(8,128)(2,1)S(1)} %row.1.refs_0_), channel_id=1, source_target_pairs={{0,4},{1,5},{2,6},{3,7},{4,8},{5,9},{6,10},{7,11},{8,12},{9,13},{1... | collective-permute-start | bytes 442376 | tf_op jit(solution)/shard_map/ppermute | solution.py:385
  23.3 4.3 %collective-permute-done.7.refs_0_ = bf16[272,512]{1,0:T(8,128)(2,1)S(1)} collective-permute-done((bf16[272,512]{1,0:T(8,128)(2,1)S(1)}, bf16[272,512]{1,0:T(8,128)(2,1)S(1)}, u32[]{:S(2)}, u32[]{:S(2)}) %collective-permute-start.7) | collective-permute-done | bytes 278560 | tf_op jit(solution)/shard_map/ppermute | solution.py:385
  27.6 0.0 copy-start
  27.7 1.0 %collective-permute-start.13 = (bf16[272,512]{1,0:T(8,128)(2,1)S(1)}, bf16[272,512]{1,0:T(8,128)(2,1)S(1)}, u32[]{:S(2)}, u32[]{:S(2)}) collective-permute-start(bf16[272,512]{1,0:T(8,128)(2,1)S(1)} %get-tuple-element.40), channel_id=1, source_target_pairs={{0,2},{1,3},{2,0},{3,1},{4,6},{5,7},{6,4},{7,5},{8,10},{9,11},{10,... | collective-permute-start | bytes 835592 | tf_op jit(solution)/shard_map/ppermute | solution.py:385
  28.7 3.2 %collective-permute-start.11 = (bf16[272,512]{1,0:T(8,128)(2,1)S(1)}, bf16[272,512]{1,0:T(8,128)(2,1)S(1)}, u32[]{:S(2)}, u32[]{:S(2)}) collective-permute-start(bf16[272,512]{1,0:T(8,128)(2,1)S(1)} %get-tuple-element.31.own_ref.refs_0_), channel_id=1, source_target_pairs={{0,1},{1,0},{2,3},{3,2},{4,5},{5,4},{6,7},{7,6},{8,9},{9,8},{10,11... | collective-permute-start | bytes 835592 | tf_op jit(solution)/shard_map/ppermute | solution.py:385
  31.9 0.0 collective-permute-done.2.refs_1_
  31.9 0.6 %hop1.1 = (bf16[144,512]{1,0:T(8,128)(2,1)S(1)}, bf16[144,512]{1,0:T(8,128)(2,1)S(1)}) custom-call(s32[4]{0:T(128)S(1)} %pad_add_fusion.place, bf16[144,512]{1,0:T(8,128)(2,1)S(1)} %row.1.refs_0_, bf16[144,512]{1,0:T(8,128)(2,1)S(1)} %collective-permute-done.2.refs_1_), custom_call_target="tpu_custom_call" | custom-call | flops 690000000 | tf_op jit(solution)/shard_map/hop1/pallas_call | solution.py:39
  32.5 0.1 collective-permute-start.3
  32.6 0.4 collective-permute-start.12
  33.0 1.1 %collective-permute-start.9 = (bf16[272,512]{1,0:T(8,128)(2,1)S(1)}, bf16[272,512]{1,0:T(8,128)(2,1)S(1)}, u32[]{:S(2)}, u32[]{:S(2)}) collective-permute-start(bf16[272,512]{1,0:T(8,128)(2,1)S(1)} %get-tuple-element.41), channel_id=1, source_target_pairs={{0,2},{1,3},{2,0},{3,1},{4,6},{5,7},{6,4},{7,5},{8,10},{9,11},{10,... | collective-permute-start | bytes 835592 | tf_op jit(solution)/shard_map/ppermute | solution.py:385
  34.2 0.0 collective-permute-done.13.refs_2_
  34.2 3.4 %collective-permute-start.14 = (bf16[272,512]{1,0:T(8,128)(2,1)S(1)}, bf16[272,512]{1,0:T(8,128)(2,1)S(1)}, u32[]{:S(2)}, u32[]{:S(2)}) collective-permute-start(bf16[272,512]{1,0:T(8,128)(2,1)S(1)} %collective-permute-done.13.refs_2_), channel_id=1, source_target_pairs={{0,1},{1,0},{2,3},{3,2},{4,5},{5,4},{6,7},{7,6},{8,9},{9,8},{10,11... | collective-permute-start | bytes 835592 | tf_op jit(solution)/shard_map/ppermute | solution.py:385
  37.6 1.9 %collective-permute-done.3.refs_2_ = bf16[144,512]{1,0:T(8,128)(2,1)S(1)} collective-permute-done((bf16[144,512]{1,0:T(8,128)(2,1)S(1)}, bf16[144,512]{1,0:T(8,128)(2,1)S(1)}, u32[]{:S(2)}, u32[]{:S(2)}) %collective-permute-start.3) | collective-permute-done | bytes 147488 | tf_op jit(solution)/shard_map/ppermute | solution.py:385
  39.5 0.6 hop2.1.mine_ref
  40.1 0.8 %collective-permute-start.4 = (bf16[128,512]{1,0:T(8,128)(2,1)S(1)}, bf16[128,512]{1,0:T(8,128)(2,1)S(1)}, u32[]{:S(2)}, u32[]{:S(2)}) collective-permute-start(bf16[128,512]{1,0:T(8,128)(2,1)S(1)} %hop2.1.mine_ref), channel_id=1, source_target_pairs={{0,2},{1,3},{2,0},{3,1},{4,6},{5,7},{6,4},{7,5},{8,10},{9,11},{10,... | collective-permute-start | bytes 393224 | tf_op jit(solution)/shard_map/ppermute | solution.py:385
  40.9 0.0 collective-permute-done.11.refs_1_
  40.9 0.0 copy-done
  40.9 3.2 %attend0.1 = (f32[2,128,2048]{2,1,0:T(8,128)S(1)}, f32[2,128,2048]{2,1,0:T(8,128)S(1)}, f32[2,128,2048]{2,1,0:T(8,128)S(1)}) custom-call(s32[4]{0:T(128)S(1)} %pad_add_fusion.place, bf16[2,128,2048]{2,1,0:T(8,128)(2,1)S(1)} %copy-done, bf16[272,512]{1,0:T(8,128)(2,1)S(1)} %get-tuple-element.31.own_ref.refs_0_, ...), custom_call_target="tpu_custom_call" | custom-call | flops 2990000128 | tf_op jit(solution)/shard_map/attend0/pallas_call | solution.py:39
  44.2 1.3 %collective-permute-start.8 = (bf16[272,512]{1,0:T(8,128)(2,1)S(1)}, bf16[272,512]{1,0:T(8,128)(2,1)S(1)}, u32[]{:S(2)}, u32[]{:S(2)}) collective-permute-start(bf16[272,512]{1,0:T(8,128)(2,1)S(1)} %collective-permute-done.7.refs_0_), channel_id=1, source_target_pairs={{0,1},{1,0},{2,3},{3,2},{4,5},{5,4},{6,7},{7,6},{8,9},{9,8},{10,11... | collective-permute-start | bytes 835592 | tf_op jit(solution)/shard_map/ppermute | solution.py:385
  45.5 0.0 collective-permute-done.9.refs_2_
  45.5 0.1 collective-permute-start.10
  45.5 0.0 collective-permute-done.4.other_ref
  45.6 1.5 %finish.1 = (bf16[128,1024]{1,0:T(8,128)(2,1)S(1)}, bf16[128,1024]{1,0:T(8,128)(2,1)S(1)}) custom-call(s32[4]{0:T(128)S(1)} %pad_add_fusion.place, f32[2,128,1024]{2,1,0:T(8,128)S(1)} %get-tuple-element.23.mixed_ref, f32[2,128,128]{2,1,0:T(8,128)S(1)} %get-tuple-element.24.run_ref, bf16[2,128,128]{2,1,0:T(8,128)(2,1)S(1)} %get-tuple-element.25.read_ref, ...), custom_call_target="tpu_custom_call" | custom-call | flops 1955000064 | tf_op jit(solution)/shard_map/finish/pallas_call | solution.py:39
  47.1 0.6 collective-permute-start.5
  47.7 0.0 collective-permute-done.12.refs_1_
  47.7 0.0 collective-permute-done.14.refs_3_
  47.7 5.0 %attend1.1 = (f32[2,128,2048]{2,1,0:T(8,128)S(1)}, f32[2,128,2048]{2,1,0:T(8,128)S(1)}, f32[2,128,2048]{2,1,0:T(8,128)S(1)}) custom-call(s32[4]{0:T(128)S(1)} %pad_add_fusion.place, bf16[2,128,2048]{2,1,0:T(8,128)(2,1)S(1)} %copy-done, bf16[272,512]{1,0:T(8,128)(2,1)S(1)} %get-tuple-element.31.own_ref.refs_0_, ...), custom_call_target="tpu_custom_call" | custom-call | flops 5405000192 | tf_op jit(solution)/shard_map/attend1/pallas_call | solution.py:39
  52.7 0.0 collective-permute-done.8.refs_1_
  52.7 0.0 collective-permute-done.10.refs_3_
  52.8 6.2 %attend3.1 = bf16[2,128,2048]{2,1,0:T(8,128)(2,1)} custom-call(s32[4]{0:T(128)S(1)} %pad_add_fusion.place, bf16[2,128,2048]{2,1,0:T(8,128)(2,1)S(1)} %copy-done, bf16[272,512]{1,0:T(8,128)(2,1)S(1)} %get-tuple-element.31.own_ref.refs_0_, bf16[272,512]{1,0:T(8,128)(2,1)S(1)} %collective-permute-done.7.refs_0_, ...), custom_call_target="tpu_custom_call" | custom-call | flops 5405000192 | tf_op jit(solution)/shard_map/attend3/pallas_call | solution.py:39
  58.9 0.0 collective-permute-done.5.c_ref
  58.9 1.4 %collect.1 = bf16[128,2048]{1,0:T(8,128)(2,1)} custom-call(s32[4]{0:T(128)S(1)} %pad_add_fusion.place, bf16[128,1024]{1,0:T(8,128)(2,1)S(1)} %get-tuple-element.29.self_ref, bf16[128,1024]{1,0:T(8,128)(2,1)S(1)} %collective-permute-done.5.c_ref), custom_call_target="tpu_custom_call" | custom-call | flops 920000000 | tf_op jit(solution)/shard_map/collect/pallas_call | solution.py:39
  (2 shorter events, 0.1 us)
Async XLA Ops:
  1.6 1.0 %copy-start.1 = (bf16[128,2048]{1,0:T(8,128)(2,1)S(1)}, bf16[128,2048]{1,0:T(8,128)(2,1)}, u32[]{:S(2)}) copy-start(bf16[128,2048]{1,0:T(8,128)(2,1)} %x_ref.3) | copy-start | bytes 1572868
  2.6 0.9 %copy-start.2 = (bf16[2,128,512]{2,1,0:T(8,128)(2,1)S(1)}, bf16[2,128,512]{2,1,0:T(8,128)(2,1)}, u32[]{:S(2)}) copy-start(bf16[2,128,512]{2,1,0:T(8,128)(2,1)} %kv_ref.1) | copy-start | bytes 786436
  3.6 0.8 %copy-start.3 = (bf16[128,128]{1,0:T(8,128)(2,1)S(1)}, bf16[128,128]{1,0:T(8,128)(2,1)}, u32[]{:S(2)}) copy-start(bf16[128,128]{1,0:T(8,128)(2,1)} %write_ref.1) | copy-start | bytes 98308
  4.3 0.8 %copy-start.4 = (bf16[128,128]{1,0:T(8,128)(2,1)S(1)}, bf16[128,128]{1,0:T(8,128)(2,1)}, u32[]{:S(2)}) copy-start(bf16[128,128]{1,0:T(8,128)(2,1)} %read_ref.1) | copy-start | bytes 98308
  5.1 0.7 %copy-start.5 = (s32[128]{0:T(128)S(1)}, s32[128]{0:T(128)}, u32[]{:S(2)}) copy-start(s32[128]{0:T(128)} %param.15) | copy-start | bytes 1540
  5.8 3.5 %copy-start.6 = (f32[32]{0:T(128)S(1)}, f32[32]{0:T(128)}, u32[]{:S(2)}) copy-start(f32[32]{0:T(128)} %param.12) | copy-start | bytes 388
  6.4 2.9 %collective-permute-start = (bf16[128,1408]{1,0:T(8,128)(2,1)S(1)}, bf16[128,1408]{1,0:T(8,128)(2,1)S(1)}, u32[]{:S(2)}, u32[]{:S(2)}) collective-permute-start(bf16[128,1408]{1,0:T(8,128)(2,1)S(1)} %get-tuple-element.22), channel_id=1, source_target_pairs={{0,1},{1,0},{2,3},{3,2},{4,5},{5,4},{6,7},{7,6},{8,9},{9,8},{10,11... | collective-permute-start | bytes 1081352 | tf_op jit(solution)/shard_map/ppermute | solution.py:385
  6.5 11.7 %collective-permute-start.6 = (bf16[272,512]{1,0:T(8,128)(2,1)S(1)}, bf16[272,512]{1,0:T(8,128)(2,1)S(1)}, u32[]{:S(2)}, u32[]{:S(2)}) collective-permute-start(bf16[272,512]{1,0:T(8,128)(2,1)S(1)} %get-tuple-element.31.own_ref.refs_0_), channel_id=1, source_target_pairs={{0,4},{1,5},{2,6},{3,7},{4,8},{5,9},{6,10},{7,11},{8,12},{9,13},{1... | collective-permute-start | bytes 835592 | tf_op jit(solution)/shard_map/ppermute | solution.py:385
  13.1 8.3 %collective-permute-start.1 = (bf16[144,1024]{1,0:T(8,128)(2,1)S(1)}, bf16[144,1024]{1,0:T(8,128)(2,1)S(1)}, u32[]{:S(2)}, u32[]{:S(2)}) collective-permute-start(bf16[144,1024]{1,0:T(8,128)(2,1)S(1)} %get-tuple-element.26.tail_ref), channel_id=1, source_target_pairs={{0,2},{1,3},{2,0},{3,1},{4,6},{5,7},{6,4},{7,5},{8,10},{9,11},{10,... | collective-permute-start | bytes 884744 | tf_op jit(solution)/shard_map/ppermute | solution.py:385
  18.2 9.4 %collective-permute-start.7 = (bf16[272,512]{1,0:T(8,128)(2,1)S(1)}, bf16[272,512]{1,0:T(8,128)(2,1)S(1)}, u32[]{:S(2)}, u32[]{:S(2)}) collective-permute-start(bf16[272,512]{1,0:T(8,128)(2,1)S(1)} %collective-permute-done.6.refs_0_), channel_id=1, source_target_pairs={{0,4},{1,5},{2,6},{3,7},{4,8},{5,9},{6,10},{7,11},{8,12},{9,13},{1... | collective-permute-start | bytes 835592 | tf_op jit(solution)/shard_map/ppermute | solution.py:385
  22.0 9.9 %collective-permute-start.2 = (bf16[144,512]{1,0:T(8,128)(2,1)S(1)}, bf16[144,512]{1,0:T(8,128)(2,1)S(1)}, u32[]{:S(2)}, u32[]{:S(2)}) collective-permute-start(bf16[144,512]{1,0:T(8,128)(2,1)S(1)} %row.1.refs_0_), channel_id=1, source_target_pairs={{0,4},{1,5},{2,6},{3,7},{4,8},{5,9},{6,10},{7,11},{8,12},{9,13},{1... | collective-permute-start | bytes 442376 | tf_op jit(solution)/shard_map/ppermute | solution.py:385
  27.6 13.3 %copy-start = (bf16[2,128,2048]{2,1,0:T(8,128)(2,1)S(1)}, bf16[2,128,2048]{2,1,0:T(8,128)(2,1)}, u32[]{:S(2)}) copy-start(bf16[2,128,2048]{2,1,0:T(8,128)(2,1)} %q_ref.3) | copy-start | bytes 3145732
  27.7 6.5 %collective-permute-start.13 = (bf16[272,512]{1,0:T(8,128)(2,1)S(1)}, bf16[272,512]{1,0:T(8,128)(2,1)S(1)}, u32[]{:S(2)}, u32[]{:S(2)}) collective-permute-start(bf16[272,512]{1,0:T(8,128)(2,1)S(1)} %get-tuple-element.40), channel_id=1, source_target_pairs={{0,2},{1,3},{2,0},{3,1},{4,6},{5,7},{6,4},{7,5},{8,10},{9,11},{10,... | collective-permute-start | bytes 835592 | tf_op jit(solution)/shard_map/ppermute | solution.py:385
  28.7 12.2 %collective-permute-start.11 = (bf16[272,512]{1,0:T(8,128)(2,1)S(1)}, bf16[272,512]{1,0:T(8,128)(2,1)S(1)}, u32[]{:S(2)}, u32[]{:S(2)}) collective-permute-start(bf16[272,512]{1,0:T(8,128)(2,1)S(1)} %get-tuple-element.31.own_ref.refs_0_), channel_id=1, source_target_pairs={{0,1},{1,0},{2,3},{3,2},{4,5},{5,4},{6,7},{7,6},{8,9},{9,8},{10,11... | collective-permute-start | bytes 835592 | tf_op jit(solution)/shard_map/ppermute | solution.py:385
  32.5 7.0 %collective-permute-start.3 = (bf16[144,512]{1,0:T(8,128)(2,1)S(1)}, bf16[144,512]{1,0:T(8,128)(2,1)S(1)}, u32[]{:S(2)}, u32[]{:S(2)}) collective-permute-start(bf16[144,512]{1,0:T(8,128)(2,1)S(1)} %get-tuple-element.27.refs_0_), channel_id=1, source_target_pairs={{0,8},{1,9},{2,10},{3,11},{4,12},{5,13},{6,14},{7,15},{8,0},{9,1},... | collective-permute-start | bytes 442376 | tf_op jit(solution)/shard_map/ppermute | solution.py:385
  32.6 15.1 %collective-permute-start.12 = (bf16[272,512]{1,0:T(8,128)(2,1)S(1)}, bf16[272,512]{1,0:T(8,128)(2,1)S(1)}, u32[]{:S(2)}, u32[]{:S(2)}) collective-permute-start(bf16[272,512]{1,0:T(8,128)(2,1)S(1)} %collective-permute-done.6.refs_0_), channel_id=1, source_target_pairs={{0,1},{1,0},{2,3},{3,2},{4,5},{5,4},{6,7},{7,6},{8,9},{9,8},{10,11... | collective-permute-start | bytes 835592 | tf_op jit(solution)/shard_map/ppermute | solution.py:385
  33.0 12.4 %collective-permute-start.9 = (bf16[272,512]{1,0:T(8,128)(2,1)S(1)}, bf16[272,512]{1,0:T(8,128)(2,1)S(1)}, u32[]{:S(2)}, u32[]{:S(2)}) collective-permute-start(bf16[272,512]{1,0:T(8,128)(2,1)S(1)} %get-tuple-element.41), channel_id=1, source_target_pairs={{0,2},{1,3},{2,0},{3,1},{4,6},{5,7},{6,4},{7,5},{8,10},{9,11},{10,... | collective-permute-start | bytes 835592 | tf_op jit(solution)/shard_map/ppermute | solution.py:385
  34.2 13.5 %collective-permute-start.14 = (bf16[272,512]{1,0:T(8,128)(2,1)S(1)}, bf16[272,512]{1,0:T(8,128)(2,1)S(1)}, u32[]{:S(2)}, u32[]{:S(2)}) collective-permute-start(bf16[272,512]{1,0:T(8,128)(2,1)S(1)} %collective-permute-done.13.refs_2_), channel_id=1, source_target_pairs={{0,1},{1,0},{2,3},{3,2},{4,5},{5,4},{6,7},{7,6},{8,9},{9,8},{10,11... | collective-permute-start | bytes 835592 | tf_op jit(solution)/shard_map/ppermute | solution.py:385
  40.1 5.4 %collective-permute-start.4 = (bf16[128,512]{1,0:T(8,128)(2,1)S(1)}, bf16[128,512]{1,0:T(8,128)(2,1)S(1)}, u32[]{:S(2)}, u32[]{:S(2)}) collective-permute-start(bf16[128,512]{1,0:T(8,128)(2,1)S(1)} %hop2.1.mine_ref), channel_id=1, source_target_pairs={{0,2},{1,3},{2,0},{3,1},{4,6},{5,7},{6,4},{7,5},{8,10},{9,11},{10,... | collective-permute-start | bytes 393224 | tf_op jit(solution)/shard_map/ppermute | solution.py:385
  44.2 8.6 %collective-permute-start.8 = (bf16[272,512]{1,0:T(8,128)(2,1)S(1)}, bf16[272,512]{1,0:T(8,128)(2,1)S(1)}, u32[]{:S(2)}, u32[]{:S(2)}) collective-permute-start(bf16[272,512]{1,0:T(8,128)(2,1)S(1)} %collective-permute-done.7.refs_0_), channel_id=1, source_target_pairs={{0,1},{1,0},{2,3},{3,2},{4,5},{5,4},{6,7},{7,6},{8,9},{9,8},{10,11... | collective-permute-start | bytes 835592 | tf_op jit(solution)/shard_map/ppermute | solution.py:385
  45.5 7.3 %collective-permute-start.10 = (bf16[272,512]{1,0:T(8,128)(2,1)S(1)}, bf16[272,512]{1,0:T(8,128)(2,1)S(1)}, u32[]{:S(2)}, u32[]{:S(2)}) collective-permute-start(bf16[272,512]{1,0:T(8,128)(2,1)S(1)} %collective-permute-done.9.refs_2_), channel_id=1, source_target_pairs={{0,1},{1,0},{2,3},{3,2},{4,5},{5,4},{6,7},{7,6},{8,9},{9,8},{10,11... | collective-permute-start | bytes 835592 | tf_op jit(solution)/shard_map/ppermute | solution.py:385
  47.1 11.8 %collective-permute-start.5 = (bf16[128,1024]{1,0:T(8,128)(2,1)S(1)}, bf16[128,1024]{1,0:T(8,128)(2,1)S(1)}, u32[]{:S(2)}, u32[]{:S(2)}) collective-permute-start(bf16[128,1024]{1,0:T(8,128)(2,1)S(1)} %get-tuple-element.30), channel_id=1, source_target_pairs={{0,1},{1,0},{2,3},{3,2},{4,5},{5,4},{6,7},{7,6},{8,9},{9,8},{10,11... | collective-permute-start | bytes 786440 | tf_op jit(solution)/shard_map/ppermute | solution.py:385

commit v3 on v2

--- a/solution.py
+++ b/solution.py
@@ -35,47 +35,66 @@
     return pl.ds(pl.multiple_of(number * width, width), width)
 
 
-def call(kernel, name, micros, place, args, outs, scratch=()):
+def call(kernel, name, micros, place, args, outs, scratch=(), stay=False):
+    spec = pl.BlockSpec(memory_space=pltpu.HBM) if stay else IN_VMEM
     return pl.pallas_call(
         kernel,
         name=name,
         out_shape=outs,
-        in_specs=[IN_SMEM] + [IN_VMEM] * len(args),
+        in_specs=[IN_SMEM] + [spec] * len(args),
         out_specs=jax.tree.map(lambda _: IN_VMEM, outs),
         scratch_shapes=list(scratch),
         cost_estimate=pl.CostEstimate(
             flops=int(micros * 1.15e9), bytes_accessed=0, transcendentals=0
         ),
         compiler_params=pltpu.CompilerParams(vmem_limit_bytes=24 * 1024 * 1024),
-    )(place, *args)
+    )(place, *[pltpu.with_memory_space_constraint(a, pltpu.HBM) if stay else a for a in args])
 
 
 def shaped(*shape, dtype=BF16):
     return jax.ShapeDtypeStruct(shape, dtype)
 
 
-def pack_kernel(place, x_ref, write_ref, read_ref, codes_ref, kv_ref, seg_ref, own, small, to_c):
+def pack_kernel(
+    place, x, write, read, codes, kv, seg, rate, own, mine, to_c, rates, code_buf, seg_buf, rate_buf,
+    sems
+):
     core = place[0]
-    tokens, state = write_ref.shape
-    heads = codes_ref.shape[1]
-    own[0:tokens, :] = kv_ref[0]
-    own[tokens : 2 * tokens, :] = kv_ref[1]
-    seg = (seg_ref[...] + 1).astype(F32).astype(BF16)
-    own[2 * tokens :, 0:tokens] = jnp.broadcast_to(seg, (16, tokens))
+    tokens, state = write.shape
+    heads = codes.shape[0]
+    half = x.shape[1] // 2
+    copies = [
+        (kv.at[0], own.at[0:tokens]),
+        (kv.at[1], own.at[tokens : 2 * tokens]),
+        (x.at[:, lanes(1 - core, half)], to_c.at[:, 0:half]),
+        (write, to_c.at[:, half : half + state]),
+        (read, to_c.at[:, half + state : half + 2 * state]),
+        (codes, code_buf),
+        (seg, seg_buf),
+        (rate, rate_buf),
+        (x.at[:, lanes(core, half)], mine.at[:, 0:half]),
+        (write, mine.at[:, half : half + state]),
+        (read, mine.at[:, half + state : half + 2 * state]),
+    ]
+    copies = [
+        pltpu.make_async_copy(source, target, sems.at[n])
+        for n, (source, target) in enumerate(copies)
+    ]
+    for copy in copies:
+        copy.start()
     own[2 * tokens :, tokens:] = jnp.zeros((16, own.shape[1] - tokens), BF16)
-    codes = codes_ref[...]
-    high = (codes >> 6).astype(F32)
-    low = (codes & 63).astype(F32)
-    gap = jnp.zeros((tokens, 64 - heads), F32)
-    both = jnp.concatenate([high, gap, low, gap], axis=1).astype(BF16)
-    small[:, 0:state] = write_ref[...]
-    small[:, state : 2 * state] = read_ref[...]
-    small[:, 2 * state :] = both
-    half = x_ref.shape[1] // 2
-    to_c[:, 0:half] = x_ref[:, lanes(1 - core, half)]
-    to_c[:, half : half + state] = write_ref[...]
-    to_c[:, half + state : half + 2 * state] = read_ref[...]
+    for copy in copies:
+        copy.wait()
+    codes_of = (seg_buf[...] + 1).astype(F32).astype(BF16)
+    own[2 * tokens :, 0:tokens] = jnp.broadcast_to(codes_of, (16, tokens))
+    code = code_buf[...]
+    high = (code >> 6).astype(F32)
+    low = (code & 63).astype(F32)
+    gap = jnp.zeros((64 - heads, tokens), F32)
+    both = jnp.transpose(jnp.concatenate([high, gap, low, gap], axis=0)).astype(BF16)
+    mine[:, half + 2 * state :] = both
     to_c[:, half + 2 * state :] = both
+    rates[...] = jnp.concatenate([rate_buf[...], jnp.zeros((1, 128 - heads), F32)], axis=1)
 
 
 def attend_kernel(kinds, first, last, place, q_ref, own_ref, *refs):
@@ -192,23 +211,21 @@
     ref[state:, :] = jnp.where(row == 0, one, jnp.where(row == 1, two, three))
 
 
-def get_logs(ref, state, cols):
-    parts = ref[state:, cols].astype(F32)
+def get_logs(ref, state):
+    parts = ref[state:, :].astype(F32)
     return parts[0:1] + parts[1:2] + parts[2:3]
 
 
 def local_kernel(
-    heads, state, place, x_ref, own_ref, c_ref, rate_ref, mixed_ref, tail_ref, run_ref, read_ref,
-    xs, sm
+    heads, state, place, own_ref, c_ref, rate_ref, mixed_ref, mine_ref, give_ref, run_ref, read_ref,
+    xs, tail
 ):
-    tokens = x_ref.shape[0]
-    cols = xs.shape[2]
+    tokens = own_ref.shape[0]
+    cols = mixed_ref.shape[2]
     width = cols // heads
     core = place[0]
-    xs[core] = x_ref[:, lanes(core, cols)]
-    sm[core] = own_ref[...]
-    xs[1 - core] = c_ref[:, 0:cols]
-    sm[1 - core] = c_ref[:, cols:]
+    xs[core] = own_ref[...]
+    xs[1 - core] = c_ref[...]
     i = lax.broadcasted_iota(jnp.int32, (tokens, tokens), 0)
     j = lax.broadcasted_iota(jnp.int32, (tokens, tokens), 1)
     causal = j <= i
@@ -220,10 +237,10 @@
     kept = None
     offset = None
     for b in range(2):
-        write = sm[b, :, 0:state]
-        read = sm[b, :, state : 2 * state]
+        write = xs[b, :, cols : cols + state]
+        read = xs[b, :, cols + state : cols + 2 * state]
         read_ref[b] = read
-        high = sm[b, :, 2 * state :].astype(F32)
+        high = xs[b, :, cols + 2 * state :].astype(F32)
         little = pltpu.roll(high, 64, 1)
         level = jnp.floor(high * 0.0625)
         lower = high * 64.0 + little - 1024.0 * level
@@ -267,63 +284,60 @@
         if b > 0:
             added = spread(jnp.exp(end), heads // 2, width) * kept + added
         kept = added
-    tail_ref[0:state, :] = kept.astype(BF16)
-    put_logs(tail_ref, state, spread(offset, heads // 2, width))
-
-
-def row_kernel(state, place, tail_ref, y_ref, out_ref):
+    tail[0:state, :] = kept.astype(BF16)
+    put_logs(tail, state, spread(offset, heads // 2, width))
     y = place[1]
-    cols = out_ref.shape[1]
-    here = lanes(y, cols)
-    mine = tail_ref[0:state, here].astype(F32)
-    theirs = y_ref[0:state, here].astype(F32)
-    my_log = get_logs(tail_ref, state, here)
-    their_log = get_logs(y_ref, state, here)
-    later = jnp.where(y == 0, theirs, mine)
-    earlier = jnp.where(y == 0, mine, theirs)
-    decay = jnp.exp(jnp.where(y == 0, their_log, my_log))
-    out_ref[0:state, :] = (later + decay * earlier).astype(BF16)
-    put_logs(out_ref, state, my_log + their_log)
-
-
-def hop_kernel(state, distance, last, place, span_ref, before_ref, new_ref, *outs):
+    mine_ref[...] = tail[:, lanes(y, cols // 2)]
+    give_ref[...] = tail[:, lanes(1 - y, cols // 2)]
+
+
+def row_kernel(state, place, tail_ref, y_ref, span_ref, first_ref):
+    first = place[1] == 0
+    mine = tail_ref[0:state, :].astype(F32)
+    theirs = y_ref[0:state, :].astype(F32)
+    my_log = get_logs(tail_ref, state)
+    their_log = get_logs(y_ref, state)
+    later = jnp.where(first, theirs, mine)
+    earlier = jnp.where(first, mine, theirs)
+    decay = jnp.exp(jnp.where(first, their_log, my_log))
+    span_ref[0:state, :] = (later + decay * earlier).astype(BF16)
+    put_logs(span_ref, state, my_log + their_log)
+    first_ref[...] = jnp.where(first, tail_ref[...].astype(F32), y_ref[...].astype(F32)).astype(BF16)
+
+
+def join(state, old_ref, new, new_logs):
+    if old_ref is None:
+        return new, new_logs
+    logs = get_logs(old_ref, state)
+    return old_ref[0:state, :].astype(F32) + jnp.exp(logs) * new, logs + new_logs
+
+
+def hop_kernel(state, distance, last, place, *refs):
+    refs = list(refs)
+    span_ref = refs.pop(0)
+    before_ref = refs.pop(0) if distance > 1 else None
+    new_ref = refs.pop(0)
     ok = place[2] >= distance
     new = jnp.where(ok, new_ref[0:state, :].astype(F32), 0.0)
-    logs = jnp.where(ok, get_logs(new_ref, state, slice(None)), 0.0)
-    joined = [(before_ref, outs[0])] if last else [(span_ref, outs[0]), (before_ref, outs[1])]
-    for old_ref, out_ref in joined:
-        if old_ref is None:
-            out_ref[0:state, :] = new.astype(BF16)
-            put_logs(out_ref, state, logs)
-        else:
-            old_logs = get_logs(old_ref, state, slice(None))
-            out_ref[0:state, :] = (
-                old_ref[0:state, :].astype(F32) + jnp.exp(old_logs) * new
-            ).astype(BF16)
-            if not last:
-                put_logs(out_ref, state, old_logs + logs)
-
-
-def hop(state, distance, last, place, span, before, new):
-    def kernel(place, *refs):
-        refs = list(refs)
-        span_ref = refs.pop(0)
-        before_ref = refs.pop(0) if before is not None else None
-        hop_kernel(state, distance, last, place, span_ref, before_ref, *refs)
-
-    out = shaped(state if last else state + LOGS, span.shape[1])
-    return call(
-        kernel,
-        "hop%d" % distance,
-        0.6,
-        place,
-        [span] + ([before] if before is not None else []) + [new],
-        (out,) if last else (out, out),
-    )
+    new_logs = jnp.where(ok, get_logs(new_ref, state), 0.0)
+    before, before_logs = join(state, before_ref, new, new_logs)
+    if last:
+        first_ref, keep_ref, give_ref = refs
+        second, _ = join(state, first_ref, before, before_logs)
+        y = place[1]
+        keep_ref[...] = jnp.where(y == 0, before, second).astype(BF16)
+        give_ref[...] = jnp.where(y == 0, second, before).astype(BF16)
+    else:
+        span_out, before_out = refs
+        span, span_logs = join(state, span_ref, new, new_logs)
+        span_out[0:state, :] = span.astype(BF16)
+        put_logs(span_out, state, span_logs)
+        before_out[0:state, :] = before.astype(BF16)
+        put_logs(before_out, state, before_logs)
 
 
 def finish_kernel(
-    heads, state, place, mixed_ref, run_ref, read_ref, mine_ref, other_ref, y_ref, self_ref, c_ref
+    heads, state, place, mixed_ref, run_ref, read_ref, mine_ref, other_ref, self_ref, c_ref
 ):
     core = place[0]
     y = place[1]
@@ -331,12 +345,9 @@
     width = cols // heads
     mine = mine_ref[...]
     other = other_ref[...]
-    row_in = jnp.concatenate(
+    entering = jnp.concatenate(
         [jnp.where(y == 0, mine, other), jnp.where(y == 0, other, mine)], axis=1
-    ).astype(F32)
-    decay = jnp.exp(get_logs(y_ref, state, slice(None)))
-    entering = jnp.where(y == 0, row_in, y_ref[0:state, :].astype(F32) + decay * row_in)
-    entering = entering.astype(BF16)
+    )
     a = lax.broadcasted_iota(jnp.int32, (4 * width, 2 * width), 0)
     b = lax.broadcasted_iota(jnp.int32, (4 * width, 2 * width), 1)
     same = (lax.rem(a, 2 * width) < width) == (b < width)
@@ -387,103 +398,149 @@
     swap_y = lambda i: i ^ 2
     up = lambda n: lambda i: (i + n * ROW) % devices
     kv_width = keys_values.shape[2]
-    rates = jnp.pad(decay_rate, (0, 128 - heads))[None, :]
-
-    own, small, to_c = call(
+    half = cols // 2
+
+    own, mine, to_c, rates = call(
         pack_kernel,
         "pack",
         1.5,
         place,
-        [ssm_inputs, state_write, state_read, decay_codes, keys_values, segment_ids[None, :]],
+        [
+            ssm_inputs,
+            state_write,
+            state_read,
+            decay_codes.T,
+            keys_values,
+            segment_ids[None, :],
+            decay_rate[None, :],
+        ],
         (
             shaped(2 * tokens + 16, kv_width),
-            shaped(tokens, 2 * state + 128),
             shaped(tokens, cols + 2 * state + 128),
+            shaped(tokens, cols + 2 * state + 128),
+            shaped(1, 128, dtype=F32),
         ),
+        [
+            VMEM((heads, tokens), jnp.int32),
+            VMEM((1, tokens), jnp.int32),
+            VMEM((1, heads), F32),
+            pltpu.SemaphoreType.DMA((11,)),
+        ],
+        True,
     )
     from_c = send(to_c, swap_c)
     behind2 = send(own, up(1))
     partner = send(own, swap_c)
 
-    mixed, tail, run, reads = call(
+    mixed, tail, tail_out, run, reads = call(
         functools.partial(local_kernel, heads // 2, state),
         "local",
         4.3,
         place,
-        [ssm_inputs, small, from_c, rates],
+        [mine, from_c, rates],
         (
             shaped(2, tokens, cols, dtype=F32),
-            shaped(state + LOGS, cols),
+            shaped(state + LOGS, half),
+            shaped(state + LOGS, half),
             shaped(2, tokens, 128, dtype=F32),
             shaped(2, tokens, state),
         ),
-        [VMEM((2, tokens, cols), BF16), VMEM((2, tokens, 2 * state + 128), BF16)],
-    )
-    tail_y = send(tail, swap_y)
-    behind4 = send(behind2, up(1))
-    behind1 = send(jnp.where(y == 0, own, behind2), swap_y)
-    behind2c = send(behind2, swap_c)
+        [
+            VMEM((2, tokens, cols + 2 * state + 128), BF16),
+            VMEM((state + LOGS, cols), BF16),
+        ],
+    )
+    tail_y = send(tail_out, swap_y)
     carry = attend(
-        place,
-        after(queries, tail),
-        own,
-        [own, partner],
-        ((0, False), (0, True)),
-        None,
-        False,
-    )
-
-    span = call(
+        place, after(queries, tail), own, [own, partner], ((0, False), (0, True)), None, False
+    )
+    tail_y = after(tail_y, carry[0])
+    span, first = call(
         functools.partial(row_kernel, state),
         "row",
         0.6,
         place,
         [tail, tail_y],
-        shaped(state + LOGS, cols // 2),
-    )
+        (shaped(state + LOGS, half),) * 2,
+    )
+    new = send(span, up(1))
+    behind2 = after(behind2, span)
+    behind4 = send(behind2, up(1))
+    to_y = jnp.where(y == 0, own, behind2)
+    behind1 = send(to_y, swap_y)
+    behind2c = send(behind2, swap_c)
+    carry = attend(
+        place,
+        lax.optimization_barrier((queries, span, to_y))[0],
+        own,
+        [behind2, behind2c],
+        ((2, False), (2, True)),
+        carry,
+        False,
+    )
+    new = after(new, carry[0])
+    behind4, behind1 = after(behind4, carry[0]), after(behind1, carry[0])
+
+    to_y = jnp.where(y == 0, behind2, behind4)
+    behind3 = send(to_y, swap_y)
+    behind1c = send(behind1, swap_c)
+    behind4c = send(behind4, swap_c)
     before = None
     distance = 1
     while distance < rows:
-        new = send(span, up(distance))
         last = 2 * distance >= rows
-        out = hop(state, distance, last, place, span, before, new)
-        span, before = (None, out[0]) if last else out
+        out = call(
+            functools.partial(hop_kernel, state, distance, last),
+            "hop%d" % distance,
+            0.6,
+            place,
+            [span] + [before] * (distance > 1) + [new] + [first] * last,
+            (shaped(state, half) if last else shaped(state + LOGS, half),) * 2,
+        )
+        if last:
+            keep, give = out
+        else:
+            span, before = out
+            new = send(span, up(2 * distance))
         if distance == 1:
-            behind3 = send(jnp.where(y == 0, behind2, behind4), swap_y)
-            behind1c = send(behind1, swap_c)
-            behind4c = send(behind4, swap_c)
             carry = attend(
                 place,
-                after(queries, carry[0]),
+                lax.optimization_barrier((queries, span, to_y))[0],
                 own,
-                [behind2, behind2c, behind1, behind1c],
-                ((2, False), (2, True), (1, False), (1, True)),
+                [behind1, behind1c, behind4, behind4c],
+                ((1, False), (1, True), (4, False), (4, True)),
                 carry,
                 False,
             )
+            new, behind3 = after(new, carry[0]), after(behind3, carry[0])
+            behind3c = send(behind3, swap_c)
         distance *= 2
-    behind3c = send(behind3, swap_c)
-    other_half = send(before, swap_y)
-    mine, for_c = call(
+    other_half = send(give, swap_y)
+    done, for_c = call(
         functools.partial(finish_kernel, heads // 2, state),
         "finish",
         1.7,
         place,
-        [mixed, run, reads, before, other_half, tail_y],
+        [mixed, run, reads, keep, other_half],
         (shaped(tokens, cols),) * 2,
     )
     back_c = send(for_c, swap_c)
     attn_output = attend(
         place,
-        queries,
+        after(queries, for_c),
         own,
-        [behind4, behind4c, behind3, behind3c],
-        ((4, False), (4, True), (3, False), (3, True)),
+        [behind3, behind3c],
+        ((3, False), (3, True)),
         carry,
         True,
     )
     ssm_output = call(
-        collect_kernel, "collect", 0.8, place, [mine, back_c], shaped(tokens, channels)
+        collect_kernel,
+        "collect",
+        0.8,
+        place,
+        [done, after(back_c, attn_output)],
+        shaped(tokens, channels),
     )
     return (ssm_output, attn_output)
 

time: 60.7 us -> 58.2 us (0.959)
  waiting for transfers between devices: 13.2 us -> 8.48 us
  starting transfers between devices: 17.5 us -> 13.5 us
  Pallas kernels: 23.6 us -> 26.9 us
  local copies, waits for them, and re-layouts: 4.99 us -> 8.12 us
    ppermute x15, waiting for transfers between devices: 13.2 us -> 8.48 us  [shards(): lax.ppermute(x, 'seq', [(i, route(i)) for i in range(devices)])]
    ppermute x15, starting transfers between devices: 17.5 us -> 13.5 us  [shards(): lax.ppermute(x, 'seq', [(i, route(i)) for i in range(devices)])]
    pallas_call x10 -> x11, Pallas kernels: 23.6 us -> 26.9 us  [call(): pl.pallas_call(kernel, name=name, out_shape=outs, in_specs=[IN_SMEM] + [s...]
    unnamed x15 -> x14, local copies, waits for them, and re-layouts: 4.99 us -> 8.12 us
  transfers between devices with their start and end apart: 15 -> 15, of which waited for: 4 -> 3; matrix products, arithmetic and copies ran while one was open for 0% -> 0% of each run, Pallas kernels for 36% -> 41%
where the time goes in v3:
time: 58.2 us; the launch traced here: 57.9 us
  Pallas kernels  26.9 us (46%)
  starting transfers between devices  13.5 us (23%)
  waiting for transfers between devices  8.48 us (15%)
  local copies, waits for them, and re-layouts  8.12 us (14%)
  between operations  0.78 us (1%)
    pallas_call x11, Pallas kernels, call(): pl.pallas_call(kernel, name=name, out_shape=outs, in_specs=[IN_SMEM] + [s...  26.9 us
    ppermute x15, starting transfers between devices, shards(): lax.ppermute(x, 'seq', [(i, route(i)) for i in range(devices)])  13.5 us
    ppermute x15, waiting for transfers between devices, shards(): lax.ppermute(x, 'seq', [(i, route(i)) for i in range(devices)])  8.48 us
    unnamed x14, local copies, waits for them, and re-layouts  8.12 us
  transfers between devices with their start and end apart: 15, of which 3 were waited for; matrix products, arithmetic and copies ran while one was open for 0% of the time, Pallas kernels for 41%

profile of v3, /device:TPU:1, one launch (start us, length us, event | category | flops | bytes accessed | tf_op | source)
XLA Modules:
  0.0 57.9 jit_solution(11436865192938345415)
XLA Ops:
  0.7 0.1 pad_add_fusion.place
  0.7 2.0 %pack.1 = (bf16[272,512]{1,0:T(8,128)(2,1)S(1)}, bf16[128,1408]{1,0:T(8,128)(2,1)S(1)}, bf16[128,1408]{1,0:T(8,128)(2,1)S(1)}, f32[1,128]{1,0:T(1,128)S(1)}) custom-call(s32[4]{0:T(128)S(1)} %pad_add_fusion.place, bf16[128,2048]{1,0:T(8,128)(2,1)} %x.1, bf16[128,128]{1,0:T(8,128)(2,1)} %write.1, bf16[128,128]{1,0:T(8,128)(2,1)} %read.1, s32[32,128]{1,0:T(8,128)} %bitcast.7, ...), custom_call_target="tpu_custom_call" | custom-call | flops 1724999936 | tf_op jit(solution)/shard_map/pack/pallas_call | solution.py:40
  2.7 0.1 collective-permute-start
  2.9 0.5 collective-permute-start.2
  3.3 2.4 %collective-permute-start.4 = (bf16[272,512]{1,0:T(8,128)(2,1)S(1)}, bf16[272,512]{1,0:T(8,128)(2,1)S(1)}, u32[]{:S(2)}, u32[]{:S(2)}) collective-permute-start(bf16[272,512]{1,0:T(8,128)(2,1)S(1)} %get-tuple-element.49.own_ref.refs_0_), channel_id=1, source_target_pairs={{0,4},{1,5},{2,6},{3,7},{4,8},{5,9},{6,10},{7,11},{8,12},{9,13},{1... | collective-permute-start | bytes 835592 | tf_op jit(solution)/shard_map/ppermute | solution.py:396
  5.7 0.0 collective-permute-done.c_ref
  5.7 0.0 copy-start
  5.7 3.8 %local.1 = (f32[2,128,1024]{2,1,0:T(8,128)S(1)}, bf16[144,512]{1,0:T(8,128)(2,1)S(1)}, bf16[144,512]{1,0:T(8,128)(2,1)S(1)}, f32[2,128,128]{2,1,0:T(8,128)S(1)}, bf16[2,128,128]{2,1,0:T(8,128)(2,1)S(1)}) custom-call(s32[4]{0:T(128)S(1)} %pad_add_fusion.place, bf16[128,1408]{1,0:T(8,128)(2,1)S(1)} %get-tuple-element.40.own_ref, ...), custom_call_target="tpu_custom_call" | custom-call | flops 4944999936 | tf_op jit(solution)/shard_map/local/pallas_call | solution.py:40
  9.5 1.3 %collective-permute-start.1 = (bf16[144,512]{1,0:T(8,128)(2,1)S(1)}, bf16[144,512]{1,0:T(8,128)(2,1)S(1)}, u32[]{:S(2)}, u32[]{:S(2)}) collective-permute-start(bf16[144,512]{1,0:T(8,128)(2,1)S(1)} %get-tuple-element.47), channel_id=1, source_target_pairs={{0,2},{1,3},{2,0},{3,1},{4,6},{5,7},{6,4},{7,5},{8,10},{9,11},{10,... | collective-permute-start | bytes 442376 | tf_op jit(solution)/shard_map/ppermute | solution.py:396
  10.8 0.0 collective-permute-done.2.refs_1_
  10.8 0.0 copy-done
  10.8 3.3 %attend0.1 = (f32[2,128,2048]{2,1,0:T(8,128)S(1)}, f32[2,128,2048]{2,1,0:T(8,128)S(1)}, f32[2,128,2048]{2,1,0:T(8,128)S(1)}) custom-call(s32[4]{0:T(128)S(1)} %pad_add_fusion.place, bf16[2,128,2048]{2,1,0:T(8,128)(2,1)S(1)} %copy-done, bf16[272,512]{1,0:T(8,128)(2,1)S(1)} %get-tuple-element.49.own_ref.refs_0_, ...), custom_call_target="tpu_custom_call" | custom-call | flops 2990000128 | tf_op jit(solution)/shard_map/attend0/pallas_call | solution.py:40
  14.1 0.0 copy-start.1
  14.1 1.3 %copy-done.1 = f32[2,128,2048]{2,1,0:T(8,128)} copy-done((f32[2,128,2048]{2,1,0:T(8,128)}, f32[2,128,2048]{2,1,0:T(8,128)S(1)}, u32[]{:S(2)}) %copy-start.1) | copy-done | bytes 2097176
  15.4 0.0 copy-start.5
  15.4 1.4 %copy-done.5 = f32[2,128,2048]{2,1,0:T(8,128)} copy-done((f32[2,128,2048]{2,1,0:T(8,128)}, f32[2,128,2048]{2,1,0:T(8,128)S(1)}, u32[]{:S(2)}) %copy-start.5) | copy-done | bytes 2097176
  16.8 0.0 copy-start.3
  16.8 0.0 collective-permute-done.1.y_ref
  16.8 0.6 %row.1 = (bf16[144,512]{1,0:T(8,128)(2,1)S(1)}, bf16[144,512]{1,0:T(8,128)(2,1)S(1)}) custom-call(s32[4]{0:T(128)S(1)} %pad_add_fusion.place, bf16[144,512]{1,0:T(8,128)(2,1)S(1)} %get-tuple-element.46.tail_ref, bf16[144,512]{1,0:T(8,128)(2,1)S(1)} %collective-permute-done.1.y_ref), custom_call_target="tpu_custom_call" | custom-call | flops 690000000 | tf_op jit(solution)/shard_map/row/pallas_call | solution.py:40
  17.4 0.0 collective-permute-done.4.refs_0_
  17.4 0.7 %copy-done.3 = f32[2,128,2048]{2,1,0:T(8,128)} copy-done((f32[2,128,2048]{2,1,0:T(8,128)}, f32[2,128,2048]{2,1,0:T(8,128)S(1)}, u32[]{:S(2)}) %copy-start.3) | copy-done | bytes 2097176
  18.1 1.0 %collective-permute-start.5 = (bf16[272,512]{1,0:T(8,128)(2,1)S(1)}, bf16[272,512]{1,0:T(8,128)(2,1)S(1)}, u32[]{:S(2)}, u32[]{:S(2)}) collective-permute-start(bf16[272,512]{1,0:T(8,128)(2,1)S(1)} %collective-permute-done.4.refs_0_), channel_id=1, source_target_pairs={{0,1},{1,0},{2,3},{3,2},{4,5},{5,4},{6,7},{7,6},{8,9},{9,8},{10,11... | collective-permute-start | bytes 835592 | tf_op jit(solution)/shard_map/ppermute | solution.py:396
  19.1 0.3 collective-permute-start.8
  19.4 1.3 %collective-permute-start.7 = (bf16[272,512]{1,0:T(8,128)(2,1)S(1)}, bf16[272,512]{1,0:T(8,128)(2,1)S(1)}, u32[]{:S(2)}, u32[]{:S(2)}) collective-permute-start(bf16[272,512]{1,0:T(8,128)(2,1)S(1)} %collective-permute-done.4.refs_0_), channel_id=1, source_target_pairs={{0,4},{1,5},{2,6},{3,7},{4,8},{5,9},{6,10},{7,11},{8,12},{9,13},{1... | collective-permute-start | bytes 835592 | tf_op jit(solution)/shard_map/ppermute | solution.py:396
  20.7 1.3 %collective-permute-start.3 = (bf16[144,512]{1,0:T(8,128)(2,1)S(1)}, bf16[144,512]{1,0:T(8,128)(2,1)S(1)}, u32[]{:S(2)}, u32[]{:S(2)}) collective-permute-start(bf16[144,512]{1,0:T(8,128)(2,1)S(1)} %get-tuple-element.52.refs_0_), channel_id=1, source_target_pairs={{0,4},{1,5},{2,6},{3,7},{4,8},{5,9},{6,10},{7,11},{8,12},{9,13},{1... | collective-permute-start | bytes 442376 | tf_op jit(solution)/shard_map/ppermute | solution.py:396
  22.0 0.0 collective-permute-done.5.refs_1_
  22.0 0.0 copy-start.2
  22.0 1.6 %copy-done.2 = f32[2,128,2048]{2,1,0:T(8,128)S(1)} copy-done((f32[2,128,2048]{2,1,0:T(8,128)S(1)}, f32[2,128,2048]{2,1,0:T(8,128)}, u32[]{:S(2)}) %copy-start.2) | copy-done | bytes 2097176
  23.6 0.0 copy-start.4
  23.6 1.6 %copy-done.4 = f32[2,128,2048]{2,1,0:T(8,128)S(1)} copy-done((f32[2,128,2048]{2,1,0:T(8,128)S(1)}, f32[2,128,2048]{2,1,0:T(8,128)}, u32[]{:S(2)}) %copy-start.4) | copy-done | bytes 2097176
  25.2 0.0 copy-start.6
  25.2 1.6 %copy-done.6 = f32[2,128,2048]{2,1,0:T(8,128)S(1)} copy-done((f32[2,128,2048]{2,1,0:T(8,128)S(1)}, f32[2,128,2048]{2,1,0:T(8,128)}, u32[]{:S(2)}) %copy-start.6) | copy-done | bytes 2097176
  26.8 3.5 %attend2.1 = (f32[2,128,2048]{2,1,0:T(8,128)S(1)}, f32[2,128,2048]{2,1,0:T(8,128)S(1)}, f32[2,128,2048]{2,1,0:T(8,128)S(1)}) custom-call(s32[4]{0:T(128)S(1)} %pad_add_fusion.place, bf16[2,128,2048]{2,1,0:T(8,128)(2,1)S(1)} %copy-done, bf16[272,512]{1,0:T(8,128)(2,1)S(1)} %get-tuple-element.49.own_ref.refs_0_, ...), custom_call_target="tpu_custom_call" | custom-call | flops 2990000128 | tf_op jit(solution)/shard_map/attend2/pallas_call | solution.py:40
  30.3 0.0 collective-permute-done.8.refs_0_
  30.3 0.9 %collective-permute-start.9 = (bf16[272,512]{1,0:T(8,128)(2,1)S(1)}, bf16[272,512]{1,0:T(8,128)(2,1)S(1)}, u32[]{:S(2)}, u32[]{:S(2)}) collective-permute-start(bf16[272,512]{1,0:T(8,128)(2,1)S(1)} %collective-permute-done.8.refs_0_), channel_id=1, source_target_pairs={{0,1},{1,0},{2,3},{3,2},{4,5},{5,4},{6,7},{7,6},{8,9},{9,8},{10,11... | collective-permute-start | bytes 835592 | tf_op jit(solution)/shard_map/ppermute | solution.py:396
  31.2 0.0 collective-permute-done.7.refs_2_
  31.2 0.1 collective-permute-start.10
  31.3 1.1 %collective-permute-done.3.refs_1_ = bf16[144,512]{1,0:T(8,128)(2,1)S(1)} collective-permute-done((bf16[144,512]{1,0:T(8,128)(2,1)S(1)}, bf16[144,512]{1,0:T(8,128)(2,1)S(1)}, u32[]{:S(2)}, u32[]{:S(2)}) %collective-permute-start.3) | collective-permute-done | bytes 147488 | tf_op jit(solution)/shard_map/ppermute | solution.py:396
  32.4 1.3 %collective-permute-start.13 = (bf16[272,512]{1,0:T(8,128)(2,1)S(1)}, bf16[272,512]{1,0:T(8,128)(2,1)S(1)}, u32[]{:S(2)}, u32[]{:S(2)}) collective-permute-start(bf16[272,512]{1,0:T(8,128)(2,1)S(1)} %broadcast_select_fusion), channel_id=1, source_target_pairs={{0,2},{1,3},{2,0},{3,1},{4,6},{5,7},{6,4},{7,5},{8,10},{9,11},{10,... | collective-permute-start | bytes 835592 | tf_op jit(solution)/shard_map/ppermute | solution.py:396
  33.7 0.6 %hop1.1 = (bf16[144,512]{1,0:T(8,128)(2,1)S(1)}, bf16[144,512]{1,0:T(8,128)(2,1)S(1)}) custom-call(s32[4]{0:T(128)S(1)} %pad_add_fusion.place, bf16[144,512]{1,0:T(8,128)(2,1)S(1)} %get-tuple-element.52.refs_0_, bf16[144,512]{1,0:T(8,128)(2,1)S(1)} %collective-permute-done.3.refs_1_), custom_call_target="tpu_custom_call" | custom-call | flops 690000000 | tf_op jit(solution)/shard_map/hop1/pallas_call | solution.py:40
  34.3 0.6 collective-permute-start.6
  34.9 0.0 collective-permute-done.9.refs_1_
  34.9 0.0 collective-permute-done.10.refs_3_
  34.9 5.0 %attend4.1 = (f32[2,128,2048]{2,1,0:T(8,128)S(1)}, f32[2,128,2048]{2,1,0:T(8,128)S(1)}, f32[2,128,2048]{2,1,0:T(8,128)S(1)}) custom-call(s32[4]{0:T(128)S(1)} %pad_add_fusion.place, bf16[2,128,2048]{2,1,0:T(8,128)(2,1)S(1)} %copy-done, bf16[272,512]{1,0:T(8,128)(2,1)S(1)} %get-tuple-element.49.own_ref.refs_0_, ...), custom_call_target="tpu_custom_call" | custom-call | flops 5405000192 | tf_op jit(solution)/shard_map/attend4/pallas_call | solution.py:40
  40.0 3.8 %collective-permute-done.6.refs_2_ = bf16[144,512]{1,0:T(8,128)(2,1)S(1)} collective-permute-done((bf16[144,512]{1,0:T(8,128)(2,1)S(1)}, bf16[144,512]{1,0:T(8,128)(2,1)S(1)}, u32[]{:S(2)}, u32[]{:S(2)}) %collective-permute-start.6) | collective-permute-done | bytes 147488 | tf_op jit(solution)/shard_map/ppermute | solution.py:396
  43.8 0.6 %hop2.1 = (bf16[128,512]{1,0:T(8,128)(2,1)S(1)}, bf16[128,512]{1,0:T(8,128)(2,1)S(1)}) custom-call(s32[4]{0:T(128)S(1)} %pad_add_fusion.place, bf16[144,512]{1,0:T(8,128)(2,1)S(1)} %get-tuple-element.59.refs_0_, bf16[144,512]{1,0:T(8,128)(2,1)S(1)} %get-tuple-element.60.refs_1_, bf16[144,512]{1,0:T(8,128)(2,1)S(1)} %collective-permute-done.6.refs_2_, ...), custom_call_target="tpu_custom_call" | custom-call | flops 690000000 | tf_op jit(solution)/shard_map/hop2/pallas_call | solution.py:40
  44.4 0.3 collective-permute-start.11
  44.7 0.0 collective-permute-done.13.refs_0_
  44.7 0.8 %collective-permute-start.14 = (bf16[272,512]{1,0:T(8,128)(2,1)S(1)}, bf16[272,512]{1,0:T(8,128)(2,1)S(1)}, u32[]{:S(2)}, u32[]{:S(2)}) collective-permute-start(bf16[272,512]{1,0:T(8,128)(2,1)S(1)} %collective-permute-done.13.refs_0_), channel_id=1, source_target_pairs={{0,1},{1,0},{2,3},{3,2},{4,5},{5,4},{6,7},{7,6},{8,9},{9,8},{10,11... | collective-permute-start | bytes 835592 | tf_op jit(solution)/shard_map/ppermute | solution.py:396
  45.5 3.6 %collective-permute-done.11.other_ref = bf16[128,512]{1,0:T(8,128)(2,1)S(1)} collective-permute-done((bf16[128,512]{1,0:T(8,128)(2,1)S(1)}, bf16[128,512]{1,0:T(8,128)(2,1)S(1)}, u32[]{:S(2)}, u32[]{:S(2)}) %collective-permute-start.11) | collective-permute-done | bytes 131104 | tf_op jit(solution)/shard_map/ppermute | solution.py:396
  49.1 1.5 %finish.1 = (bf16[128,1024]{1,0:T(8,128)(2,1)S(1)}, bf16[128,1024]{1,0:T(8,128)(2,1)S(1)}) custom-call(s32[4]{0:T(128)S(1)} %pad_add_fusion.place, f32[2,128,1024]{2,1,0:T(8,128)S(1)} %get-tuple-element.43.mixed_ref, f32[2,128,128]{2,1,0:T(8,128)S(1)} %get-tuple-element.44.run_ref, bf16[2,128,128]{2,1,0:T(8,128)(2,1)S(1)} %get-tuple-element.45.read_ref, ...), custom_call_target="tpu_custom_call" | custom-call | flops 1955000064 | tf_op jit(solution)/shard_map/finish/pallas_call | solution.py:40
  50.6 1.4 %collective-permute-start.12 = (bf16[128,1024]{1,0:T(8,128)(2,1)S(1)}, bf16[128,1024]{1,0:T(8,128)(2,1)S(1)}, u32[]{:S(2)}, u32[]{:S(2)}) collective-permute-start(bf16[128,1024]{1,0:T(8,128)(2,1)S(1)} %get-tuple-element.72), channel_id=1, source_target_pairs={{0,1},{1,0},{2,3},{3,2},{4,5},{5,4},{6,7},{7,6},{8,9},{9,8},{10,11... | collective-permute-start | bytes 786440 | tf_op jit(solution)/shard_map/ppermute | solution.py:396
  52.0 0.0 collective-permute-done.14.refs_1_
  52.0 4.6 %attend3.1 = bf16[2,128,2048]{2,1,0:T(8,128)(2,1)} custom-call(s32[4]{0:T(128)S(1)} %pad_add_fusion.place, bf16[2,128,2048]{2,1,0:T(8,128)(2,1)S(1)} %copy-done, bf16[272,512]{1,0:T(8,128)(2,1)S(1)} %get-tuple-element.49.own_ref.refs_0_, bf16[272,512]{1,0:T(8,128)(2,1)S(1)} %collective-permute-done.13.refs_0_, ...), custom_call_target="tpu_custom_call" | custom-call | flops 2990000128 | tf_op jit(solution)/shard_map/attend3/pallas_call | solution.py:40
  56.6 0.0 collective-permute-done.12.c_ref
  56.6 1.4 %collect.1 = bf16[128,2048]{1,0:T(8,128)(2,1)} custom-call(s32[4]{0:T(128)S(1)} %pad_add_fusion.place, bf16[128,1024]{1,0:T(8,128)(2,1)S(1)} %get-tuple-element.71.self_ref, bf16[128,1024]{1,0:T(8,128)(2,1)S(1)} %collective-permute-done.12.c_ref), custom_call_target="tpu_custom_call" | custom-call | flops 920000000 | tf_op jit(solution)/shard_map/collect/pallas_call | solution.py:40
  (2 shorter events, 0.1 us)
Async XLA Ops:
  2.7 2.9 %collective-permute-start = (bf16[128,1408]{1,0:T(8,128)(2,1)S(1)}, bf16[128,1408]{1,0:T(8,128)(2,1)S(1)}, u32[]{:S(2)}, u32[]{:S(2)}) collective-permute-start(bf16[128,1408]{1,0:T(8,128)(2,1)S(1)} %get-tuple-element.41), channel_id=1, source_target_pairs={{0,1},{1,0},{2,3},{3,2},{4,5},{5,4},{6,7},{7,6},{8,9},{9,8},{10,11... | collective-permute-start | bytes 1081352 | tf_op jit(solution)/shard_map/ppermute | solution.py:396
  2.9 8.0 %collective-permute-start.2 = (bf16[272,512]{1,0:T(8,128)(2,1)S(1)}, bf16[272,512]{1,0:T(8,128)(2,1)S(1)}, u32[]{:S(2)}, u32[]{:S(2)}) collective-permute-start(bf16[272,512]{1,0:T(8,128)(2,1)S(1)} %get-tuple-element.49.own_ref.refs_0_), channel_id=1, source_target_pairs={{0,1},{1,0},{2,3},{3,2},{4,5},{5,4},{6,7},{7,6},{8,9},{9,8},{10,11... | collective-permute-start | bytes 835592 | tf_op jit(solution)/shard_map/ppermute | solution.py:396
  3.3 14.1 %collective-permute-start.4 = (bf16[272,512]{1,0:T(8,128)(2,1)S(1)}, bf16[272,512]{1,0:T(8,128)(2,1)S(1)}, u32[]{:S(2)}, u32[]{:S(2)}) collective-permute-start(bf16[272,512]{1,0:T(8,128)(2,1)S(1)} %get-tuple-element.49.own_ref.refs_0_), channel_id=1, source_target_pairs={{0,4},{1,5},{2,6},{3,7},{4,8},{5,9},{6,10},{7,11},{8,12},{9,13},{1... | collective-permute-start | bytes 835592 | tf_op jit(solution)/shard_map/ppermute | solution.py:396
  5.7 5.1 %copy-start = (bf16[2,128,2048]{2,1,0:T(8,128)(2,1)S(1)}, bf16[2,128,2048]{2,1,0:T(8,128)(2,1)}, u32[]{:S(2)}) copy-start(bf16[2,128,2048]{2,1,0:T(8,128)(2,1)} %q_ref.3) | copy-start | bytes 3145732
  9.5 7.2 %collective-permute-start.1 = (bf16[144,512]{1,0:T(8,128)(2,1)S(1)}, bf16[144,512]{1,0:T(8,128)(2,1)S(1)}, u32[]{:S(2)}, u32[]{:S(2)}) collective-permute-start(bf16[144,512]{1,0:T(8,128)(2,1)S(1)} %get-tuple-element.47), channel_id=1, source_target_pairs={{0,2},{1,3},{2,0},{3,1},{4,6},{5,7},{6,4},{7,5},{8,10},{9,11},{10,... | collective-permute-start | bytes 442376 | tf_op jit(solution)/shard_map/ppermute | solution.py:396
  14.1 1.3 %copy-start.1 = (f32[2,128,2048]{2,1,0:T(8,128)}, f32[2,128,2048]{2,1,0:T(8,128)S(1)}, u32[]{:S(2)}) copy-start(f32[2,128,2048]{2,1,0:T(8,128)S(1)} %get-tuple-element.50.refs_2_) | copy-start | bytes 6291460
  15.4 1.4 %copy-start.5 = (f32[2,128,2048]{2,1,0:T(8,128)}, f32[2,128,2048]{2,1,0:T(8,128)S(1)}, u32[]{:S(2)}) copy-start(f32[2,128,2048]{2,1,0:T(8,128)S(1)} %get-tuple-element.56.refs_4_) | copy-start | bytes 6291460
  16.8 1.4 %copy-start.3 = (f32[2,128,2048]{2,1,0:T(8,128)}, f32[2,128,2048]{2,1,0:T(8,128)S(1)}, u32[]{:S(2)}) copy-start(f32[2,128,2048]{2,1,0:T(8,128)S(1)} %get-tuple-element.55.refs_3_) | copy-start | bytes 6291460
  18.1 3.9 %collective-permute-start.5 = (bf16[272,512]{1,0:T(8,128)(2,1)S(1)}, bf16[272,512]{1,0:T(8,128)(2,1)S(1)}, u32[]{:S(2)}, u32[]{:S(2)}) collective-permute-start(bf16[272,512]{1,0:T(8,128)(2,1)S(1)} %collective-permute-done.4.refs_0_), channel_id=1, source_target_pairs={{0,1},{1,0},{2,3},{3,2},{4,5},{5,4},{6,7},{7,6},{8,9},{9,8},{10,11... | collective-permute-start | bytes 835592 | tf_op jit(solution)/shard_map/ppermute | solution.py:396
  19.1 11.1 %collective-permute-start.8 = (bf16[272,512]{1,0:T(8,128)(2,1)S(1)}, bf16[272,512]{1,0:T(8,128)(2,1)S(1)}, u32[]{:S(2)}, u32[]{:S(2)}) collective-permute-start(bf16[272,512]{1,0:T(8,128)(2,1)S(1)} %broadcast_select_fusion.1), channel_id=1, source_target_pairs={{0,2},{1,3},{2,0},{3,1},{4,6},{5,7},{6,4},{7,5},{8,10},{9,11},{10,... | collective-permute-start | bytes 835592 | tf_op jit(solution)/shard_map/ppermute | solution.py:396
  19.4 11.8 %collective-permute-start.7 = (bf16[272,512]{1,0:T(8,128)(2,1)S(1)}, bf16[272,512]{1,0:T(8,128)(2,1)S(1)}, u32[]{:S(2)}, u32[]{:S(2)}) collective-permute-start(bf16[272,512]{1,0:T(8,128)(2,1)S(1)} %collective-permute-done.4.refs_0_), channel_id=1, source_target_pairs={{0,4},{1,5},{2,6},{3,7},{4,8},{5,9},{6,10},{7,11},{8,12},{9,13},{1... | collective-permute-start | bytes 835592 | tf_op jit(solution)/shard_map/ppermute | solution.py:396
  20.7 11.6 %collective-permute-start.3 = (bf16[144,512]{1,0:T(8,128)(2,1)S(1)}, bf16[144,512]{1,0:T(8,128)(2,1)S(1)}, u32[]{:S(2)}, u32[]{:S(2)}) collective-permute-start(bf16[144,512]{1,0:T(8,128)(2,1)S(1)} %get-tuple-element.52.refs_0_), channel_id=1, source_target_pairs={{0,4},{1,5},{2,6},{3,7},{4,8},{5,9},{6,10},{7,11},{8,12},{9,13},{1... | collective-permute-start | bytes 442376 | tf_op jit(solution)/shard_map/ppermute | solution.py:396
  22.0 1.6 %copy-start.2 = (f32[2,128,2048]{2,1,0:T(8,128)S(1)}, f32[2,128,2048]{2,1,0:T(8,128)}, u32[]{:S(2)}) copy-start(f32[2,128,2048]{2,1,0:T(8,128)} %copy-done.1) | copy-start | bytes 6291460
  23.6 1.6 %copy-start.4 = (f32[2,128,2048]{2,1,0:T(8,128)S(1)}, f32[2,128,2048]{2,1,0:T(8,128)}, u32[]{:S(2)}) copy-start(f32[2,128,2048]{2,1,0:T(8,128)} %copy-done.3) | copy-start | bytes 6291460
  25.2 1.6 %copy-start.6 = (f32[2,128,2048]{2,1,0:T(8,128)S(1)}, f32[2,128,2048]{2,1,0:T(8,128)}, u32[]{:S(2)}) copy-start(f32[2,128,2048]{2,1,0:T(8,128)} %copy-done.5) | copy-start | bytes 6291460
  30.3 4.6 %collective-permute-start.9 = (bf16[272,512]{1,0:T(8,128)(2,1)S(1)}, bf16[272,512]{1,0:T(8,128)(2,1)S(1)}, u32[]{:S(2)}, u32[]{:S(2)}) collective-permute-start(bf16[272,512]{1,0:T(8,128)(2,1)S(1)} %collective-permute-done.8.refs_0_), channel_id=1, source_target_pairs={{0,1},{1,0},{2,3},{3,2},{4,5},{5,4},{6,7},{7,6},{8,9},{9,8},{10,11... | collective-permute-start | bytes 835592 | tf_op jit(solution)/shard_map/ppermute | solution.py:396
  31.2 3.7 %collective-permute-start.10 = (bf16[272,512]{1,0:T(8,128)(2,1)S(1)}, bf16[272,512]{1,0:T(8,128)(2,1)S(1)}, u32[]{:S(2)}, u32[]{:S(2)}) collective-permute-start(bf16[272,512]{1,0:T(8,128)(2,1)S(1)} %collective-permute-done.7.refs_2_), channel_id=1, source_target_pairs={{0,1},{1,0},{2,3},{3,2},{4,5},{5,4},{6,7},{7,6},{8,9},{9,8},{10,11... | collective-permute-start | bytes 835592 | tf_op jit(solution)/shard_map/ppermute | solution.py:396
  32.4 12.3 %collective-permute-start.13 = (bf16[272,512]{1,0:T(8,128)(2,1)S(1)}, bf16[272,512]{1,0:T(8,128)(2,1)S(1)}, u32[]{:S(2)}, u32[]{:S(2)}) collective-permute-start(bf16[272,512]{1,0:T(8,128)(2,1)S(1)} %broadcast_select_fusion), channel_id=1, source_target_pairs={{0,2},{1,3},{2,0},{3,1},{4,6},{5,7},{6,4},{7,5},{8,10},{9,11},{10,... | collective-permute-start | bytes 835592 | tf_op jit(solution)/shard_map/ppermute | solution.py:396
  34.3 9.4 %collective-permute-start.6 = (bf16[144,512]{1,0:T(8,128)(2,1)S(1)}, bf16[144,512]{1,0:T(8,128)(2,1)S(1)}, u32[]{:S(2)}, u32[]{:S(2)}) collective-permute-start(bf16[144,512]{1,0:T(8,128)(2,1)S(1)} %get-tuple-element.59.refs_0_), channel_id=1, source_target_pairs={{0,8},{1,9},{2,10},{3,11},{4,12},{5,13},{6,14},{7,15},{8,0},{9,1},... | collective-permute-start | bytes 442376 | tf_op jit(solution)/shard_map/ppermute | solution.py:396
  44.4 4.6 %collective-permute-start.11 = (bf16[128,512]{1,0:T(8,128)(2,1)S(1)}, bf16[128,512]{1,0:T(8,128)(2,1)S(1)}, u32[]{:S(2)}, u32[]{:S(2)}) collective-permute-start(bf16[128,512]{1,0:T(8,128)(2,1)S(1)} %get-tuple-element.70), channel_id=1, source_target_pairs={{0,2},{1,3},{2,0},{3,1},{4,6},{5,7},{6,4},{7,5},{8,10},{9,11},{10,... | collective-permute-start | bytes 393224 | tf_op jit(solution)/shard_map/ppermute | solution.py:396
  44.7 7.2 %collective-permute-start.14 = (bf16[272,512]{1,0:T(8,128)(2,1)S(1)}, bf16[272,512]{1,0:T(8,128)(2,1)S(1)}, u32[]{:S(2)}, u32[]{:S(2)}) collective-permute-start(bf16[272,512]{1,0:T(8,128)(2,1)S(1)} %collective-permute-done.13.refs_0_), channel_id=1, source_target_pairs={{0,1},{1,0},{2,3},{3,2},{4,5},{5,4},{6,7},{7,6},{8,9},{9,8},{10,11... | collective-permute-start | bytes 835592 | tf_op jit(solution)/shard_map/ppermute | solution.py:396
  50.6 6.0 %collective-permute-start.12 = (bf16[128,1024]{1,0:T(8,128)(2,1)S(1)}, bf16[128,1024]{1,0:T(8,128)(2,1)S(1)}, u32[]{:S(2)}, u32[]{:S(2)}) collective-permute-start(bf16[128,1024]{1,0:T(8,128)(2,1)S(1)} %get-tuple-element.72), channel_id=1, source_target_pairs={{0,1},{1,0},{2,3},{3,2},{4,5},{5,4},{6,7},{7,6},{8,9},{9,8},{10,11... | collective-permute-start | bytes 786440 | tf_op jit(solution)/shard_map/ppermute | solution.py:396

commit v4 on v3

--- a/solution.py
+++ b/solution.py
@@ -35,7 +35,7 @@
     return pl.ds(pl.multiple_of(number * width, width), width)
 
 
-def call(kernel, name, micros, place, args, outs, scratch=(), stay=False):
+def call(kernel, name, micros, place, args, outs, scratch=(), stay=False, mib=8):
     spec = pl.BlockSpec(memory_space=pltpu.HBM) if stay else IN_VMEM
     return pl.pallas_call(
         kernel,
@@ -47,7 +47,7 @@
         cost_estimate=pl.CostEstimate(
             flops=int(micros * 1.15e9), bytes_accessed=0, transcendentals=0
         ),
-        compiler_params=pltpu.CompilerParams(vmem_limit_bytes=24 * 1024 * 1024),
+        compiler_params=pltpu.CompilerParams(vmem_limit_bytes=mib * 1024 * 1024),
     )(place, *[pltpu.with_memory_space_constraint(a, pltpu.HBM) if stay else a for a in args])
 
 
@@ -183,13 +183,16 @@
         "attend%d" % kinds[-1][0],
         0.5 + 1.05 * count,
         place,
-        [queries, own] + list(pieces) + list(carry or ()),
+        [queries, own]
+        + list(pieces)
+        + [pltpu.with_memory_space_constraint(part, pltpu.VMEM) for part in carry or ()],
         shaped(layers, tokens, width) if last else (partial,) * 3,
         [
             VMEM((count * tokens, HEAD), BF16),
             VMEM((count * tokens, 2 * HEAD), BF16),
             VMEM((tokens, count * tokens), F32),
         ],
+        mib=20,
     )
 
 
@@ -291,7 +294,18 @@
     give_ref[...] = tail[:, lanes(1 - y, cols // 2)]
 
 
-def row_kernel(state, place, tail_ref, y_ref, span_ref, first_ref):
+def pick(place, low_ref, high_ref, out_ref):
+    @pl.when(place[1] == 0)
+    def _():
+        out_ref[...] = low_ref[...]
+
+    @pl.when(place[1] != 0)
+    def _():
+        out_ref[...] = high_ref[...]
+
+
+def row_kernel(state, place, tail_ref, y_ref, low_ref, high_ref, span_ref, first_ref, to_y):
+    pick(place, low_ref, high_ref, to_y)
     first = place[1] == 0
     mine = tail_ref[0:state, :].astype(F32)
     theirs = y_ref[0:state, :].astype(F32)
@@ -455,36 +469,19 @@
         place, after(queries, tail), own, [own, partner], ((0, False), (0, True)), None, False
     )
     tail_y = after(tail_y, carry[0])
-    span, first = call(
+    span, first, to_y = call(
         functools.partial(row_kernel, state),
         "row",
-        0.6,
-        place,
-        [tail, tail_y],
-        (shaped(state + LOGS, half),) * 2,
+        20.0,
+        place,
+        [tail, tail_y, own, behind2],
+        (shaped(state + LOGS, half),) * 2 + (shaped(2 * tokens + 16, kv_width),),
     )
     new = send(span, up(1))
     behind2 = after(behind2, span)
     behind4 = send(behind2, up(1))
-    to_y = jnp.where(y == 0, own, behind2)
     behind1 = send(to_y, swap_y)
     behind2c = send(behind2, swap_c)
-    carry = attend(
-        place,
-        lax.optimization_barrier((queries, span, to_y))[0],
-        own,
-        [behind2, behind2c],
-        ((2, False), (2, True)),
-        carry,
-        False,
-    )
-    new = after(new, carry[0])
-    behind4, behind1 = after(behind4, carry[0]), after(behind1, carry[0])
-
-    to_y = jnp.where(y == 0, behind2, behind4)
-    behind3 = send(to_y, swap_y)
-    behind1c = send(behind1, swap_c)
-    behind4c = send(behind4, swap_c)
     before = None
     distance = 1
     while distance < rows:
@@ -492,7 +489,7 @@
         out = call(
             functools.partial(hop_kernel, state, distance, last),
             "hop%d" % distance,
-            0.6,
+            20.0,
             place,
             [span] + [before] * (distance > 1) + [new] + [first] * last,
             (shaped(state, half) if last else shaped(state + LOGS, half),) * 2,
@@ -505,17 +502,39 @@
         if distance == 1:
             carry = attend(
                 place,
-                lax.optimization_barrier((queries, span, to_y))[0],
+                after(queries, before),
                 own,
-                [behind1, behind1c, behind4, behind4c],
-                ((1, False), (1, True), (4, False), (4, True)),
+                [behind2, behind2c],
+                ((2, False), (2, True)),
                 carry,
                 False,
             )
-            new, behind3 = after(new, carry[0]), after(behind3, carry[0])
-            behind3c = send(behind3, swap_c)
+            behind4, behind1 = after(behind4, carry[0]), after(behind1, carry[0])
+            behind1c = send(behind1, swap_c)
+            behind4c = send(behind4, swap_c)
+            to_y = call(
+                pick,
+                "pick",
+                20.0,
+                place,
+                [behind2, behind4],
+                shaped(2 * tokens + 16, kv_width),
+            )
+            behind3 = send(to_y, swap_y)
+            new = after(new, to_y)
         distance *= 2
-    other_half = send(give, swap_y)
+    carry = attend(
+        place,
+        after(queries, give),
+        own,
+        [behind1, behind1c, behind4, behind4c],
+        ((1, False), (1, True), (4, False), (4, True)),
+        carry,
+        False,
+    )
+    behind3 = after(behind3, carry[0])
+    behind3c = send(behind3, swap_c)
+    other_half = after(send(give, swap_y), carry[0])
     done, for_c = call(
         functools.partial(finish_kernel, heads // 2, state),
         "finish",

time: 58.2 us -> 51.8 us (0.89)
  local copies, waits for them, and re-layouts: 8.12 us -> 0.01 us
  starting transfers between devices: 13.5 us -> 15.8 us
  waiting for transfers between devices: 8.48 us -> 7.02 us
  Pallas kernels: 26.9 us -> 27.6 us
    unnamed x14 -> x2, local copies, waits for them, and re-layouts: 8.12 us -> 0.01 us
    ppermute x15, starting transfers between devices: 13.5 us -> 15.8 us  [shards(): lax.ppermute(x, 'seq', [(i, route(i)) for i in range(devices)])]
    ppermute x15, waiting for transfers between devices: 8.48 us -> 7.02 us  [shards(): lax.ppermute(x, 'seq', [(i, route(i)) for i in range(devices)])]
    pallas_call x11 -> x12, Pallas kernels: 26.9 us -> 27.6 us  [call(): pl.pallas_call(kernel, name=name, out_shape=outs, in_specs=[IN_SMEM] + [s...]
  transfers between devices with their start and end apart: 15 -> 15, of which waited for: 3 -> 4; matrix products, arithmetic and copies ran while one was open for 0% -> 0% of each run, Pallas kernels for 41% -> 46%
where the time goes in v4:
time: 51.8 us; the launch traced here: 51.2 us
  Pallas kernels  27.6 us (53%)
  starting transfers between devices  15.8 us (31%)
  waiting for transfers between devices  7.02 us (14%)
  between operations  0.77 us (1%)
    pallas_call x12, Pallas kernels, call(): pl.pallas_call(kernel, name=name, out_shape=outs, in_specs=[IN_SMEM] + [s...  27.6 us
    ppermute x15, starting transfers between devices, shards(): lax.ppermute(x, 'seq', [(i, route(i)) for i in range(devices)])  15.8 us
    ppermute x15, waiting for transfers between devices, shards(): lax.ppermute(x, 'seq', [(i, route(i)) for i in range(devices)])  7.02 us
  transfers between devices with their start and end apart: 15, of which 4 were waited for; matrix products, arithmetic and copies ran while one was open for 0% of the time, Pallas kernels for 46%

profile of v4, /device:TPU:1, one launch (start us, length us, event | category | flops | bytes accessed | tf_op | source)
XLA Modules:
  0.0 51.2 jit_solution(9092122274950072030)
XLA Ops:
  0.7 0.1 pad_add_fusion.place
  0.7 2.0 %pack.1 = (bf16[272,512]{1,0:T(8,128)(2,1)S(1)}, bf16[128,1408]{1,0:T(8,128)(2,1)S(1)}, bf16[128,1408]{1,0:T(8,128)(2,1)S(1)}, f32[1,128]{1,0:T(1,128)S(1)}) custom-call(s32[4]{0:T(128)S(1)} %pad_add_fusion.place, bf16[128,2048]{1,0:T(8,128)(2,1)} %x.1, bf16[128,128]{1,0:T(8,128)(2,1)} %write.1, bf16[128,128]{1,0:T(8,128)(2,1)} %read.1, s32[32,128]{1,0:T(8,128)} %bitcast.7, ...), custom_call_target="tpu_custom_call" | custom-call | flops 1724999936 | tf_op jit(solution)/shard_map/pack/pallas_call | solution.py:40
  2.7 0.1 collective-permute-start
  2.9 2.7 %collective-permute-start.3 = (bf16[272,512]{1,0:T(8,128)(2,1)S(1)}, bf16[272,512]{1,0:T(8,128)(2,1)S(1)}, u32[]{:S(2)}, u32[]{:S(2)}) collective-permute-start(bf16[272,512]{1,0:T(8,128)(2,1)S(1)} %get-tuple-element.50.own_ref.refs_0_.low_ref), channel_id=1, source_target_pairs={{0,4},{1,5},{2,6},{3,7},{4,8},{5,9},{6,10},{7,11},{8,12},{9,13},{1... | collective-permute-start | bytes 835592 | tf_op jit(solution)/shard_map/ppermute | solution.py:410
  5.6 0.3 collective-permute-start.2
  6.0 0.0 collective-permute-done.c_ref
  6.0 0.0 copy-start
  6.0 3.8 %local.1 = (f32[2,128,1024]{2,1,0:T(8,128)S(1)}, bf16[144,512]{1,0:T(8,128)(2,1)S(1)}, bf16[144,512]{1,0:T(8,128)(2,1)S(1)}, f32[2,128,128]{2,1,0:T(8,128)S(1)}, bf16[2,128,128]{2,1,0:T(8,128)(2,1)S(1)}) custom-call(s32[4]{0:T(128)S(1)} %pad_add_fusion.place, bf16[128,1408]{1,0:T(8,128)(2,1)S(1)} %get-tuple-element.41.own_ref, ...), custom_call_target="tpu_custom_call" | custom-call | flops 4944999936 | tf_op jit(solution)/shard_map/local/pallas_call | solution.py:40
  9.8 1.3 %collective-permute-start.1 = (bf16[144,512]{1,0:T(8,128)(2,1)S(1)}, bf16[144,512]{1,0:T(8,128)(2,1)S(1)}, u32[]{:S(2)}, u32[]{:S(2)}) collective-permute-start(bf16[144,512]{1,0:T(8,128)(2,1)S(1)} %get-tuple-element.48), channel_id=1, source_target_pairs={{0,2},{1,3},{2,0},{3,1},{4,6},{5,7},{6,4},{7,5},{8,10},{9,11},{10,... | collective-permute-start | bytes 442376 | tf_op jit(solution)/shard_map/ppermute | solution.py:410
  11.1 0.0 collective-permute-done.2.refs_1_
  11.1 0.0 copy-done
  11.1 3.2 %attend0.1 = (f32[2,128,2048]{2,1,0:T(8,128)S(1)}, f32[2,128,2048]{2,1,0:T(8,128)S(1)}, f32[2,128,2048]{2,1,0:T(8,128)S(1)}) custom-call(s32[4]{0:T(128)S(1)} %pad_add_fusion.place, bf16[2,128,2048]{2,1,0:T(8,128)(2,1)S(1)} %copy-done, bf16[272,512]{1,0:T(8,128)(2,1)S(1)} %get-tuple-element.50.own_ref.refs_0_.low_ref, ...), custom_call_target="tpu_custom_call" | custom-call | flops 2990000128 | tf_op jit(solution)/shard_map/attend0/pallas_call | solution.py:40
  14.4 0.8 %collective-permute-done.1.y_ref = bf16[144,512]{1,0:T(8,128)(2,1)S(1)} collective-permute-done((bf16[144,512]{1,0:T(8,128)(2,1)S(1)}, bf16[144,512]{1,0:T(8,128)(2,1)S(1)}, u32[]{:S(2)}, u32[]{:S(2)}) %collective-permute-start.1) | collective-permute-done | bytes 147488 | tf_op jit(solution)/shard_map/ppermute | solution.py:410
  15.2 0.0 collective-permute-done.3.high_ref.refs_0_.low_ref
  15.2 0.7 %row.1 = (bf16[144,512]{1,0:T(8,128)(2,1)S(1)}, bf16[144,512]{1,0:T(8,128)(2,1)S(1)}, bf16[272,512]{1,0:T(8,128)(2,1)S(1)}) custom-call(s32[4]{0:T(128)S(1)} %pad_add_fusion.place, bf16[144,512]{1,0:T(8,128)(2,1)S(1)} %get-tuple-element.47.tail_ref, bf16[144,512]{1,0:T(8,128)(2,1)S(1)} %collective-permute-done.1.y_ref, ...), custom_call_target="tpu_custom_call" | custom-call | flops 23000000512 | tf_op jit(solution)/shard_map/row/pallas_call | solution.py:40
  15.8 1.4 %collective-permute-start.4 = (bf16[144,512]{1,0:T(8,128)(2,1)S(1)}, bf16[144,512]{1,0:T(8,128)(2,1)S(1)}, u32[]{:S(2)}, u32[]{:S(2)}) collective-permute-start(bf16[144,512]{1,0:T(8,128)(2,1)S(1)} %get-tuple-element.53.refs_0_), channel_id=1, source_target_pairs={{0,4},{1,5},{2,6},{3,7},{4,8},{5,9},{6,10},{7,11},{8,12},{9,13},{1... | collective-permute-start | bytes 442376 | tf_op jit(solution)/shard_map/ppermute | solution.py:410
  17.2 1.2 %collective-permute-start.7 = (bf16[272,512]{1,0:T(8,128)(2,1)S(1)}, bf16[272,512]{1,0:T(8,128)(2,1)S(1)}, u32[]{:S(2)}, u32[]{:S(2)}) collective-permute-start(bf16[272,512]{1,0:T(8,128)(2,1)S(1)} %collective-permute-done.3.high_ref.refs_0_.low_ref), channel_id=1, source_target_pairs={{0,1},{1,0},{2,3},{3,2},{4,5},{5,4},{6,7},{7,6},{8,9},{9,8},{10,11... | collective-permute-start | bytes 835592 | tf_op jit(solution)/shard_map/ppermute | solution.py:410
  18.4 1.3 %collective-permute-start.6 = (bf16[272,512]{1,0:T(8,128)(2,1)S(1)}, bf16[272,512]{1,0:T(8,128)(2,1)S(1)}, u32[]{:S(2)}, u32[]{:S(2)}) collective-permute-start(bf16[272,512]{1,0:T(8,128)(2,1)S(1)} %collective-permute-done.3.high_ref.refs_0_.low_ref), channel_id=1, source_target_pairs={{0,4},{1,5},{2,6},{3,7},{4,8},{5,9},{6,10},{7,11},{8,12},{9,13},{1... | collective-permute-start | bytes 835592 | tf_op jit(solution)/shard_map/ppermute | solution.py:410
  19.7 1.2 %collective-permute-start.9 = (bf16[272,512]{1,0:T(8,128)(2,1)S(1)}, bf16[272,512]{1,0:T(8,128)(2,1)S(1)}, u32[]{:S(2)}, u32[]{:S(2)}) collective-permute-start(bf16[272,512]{1,0:T(8,128)(2,1)S(1)} %get-tuple-element.67), channel_id=1, source_target_pairs={{0,2},{1,3},{2,0},{3,1},{4,6},{5,7},{6,4},{7,5},{8,10},{9,11},{10,... | collective-permute-start | bytes 835592 | tf_op jit(solution)/shard_map/ppermute | solution.py:410
  21.0 1.1 %collective-permute-done.4.refs_1_ = bf16[144,512]{1,0:T(8,128)(2,1)S(1)} collective-permute-done((bf16[144,512]{1,0:T(8,128)(2,1)S(1)}, bf16[144,512]{1,0:T(8,128)(2,1)S(1)}, u32[]{:S(2)}, u32[]{:S(2)}) %collective-permute-start.4) | collective-permute-done | bytes 147488 | tf_op jit(solution)/shard_map/ppermute | solution.py:410
  22.1 0.6 %hop1.1 = (bf16[144,512]{1,0:T(8,128)(2,1)S(1)}, bf16[144,512]{1,0:T(8,128)(2,1)S(1)}) custom-call(s32[4]{0:T(128)S(1)} %pad_add_fusion.place, bf16[144,512]{1,0:T(8,128)(2,1)S(1)} %get-tuple-element.53.refs_0_, bf16[144,512]{1,0:T(8,128)(2,1)S(1)} %collective-permute-done.4.refs_1_), custom_call_target="tpu_custom_call" | custom-call | flops 23000000512 | tf_op jit(solution)/shard_map/hop1/pallas_call | solution.py:40
  22.7 0.6 %collective-permute-start.5 = (bf16[144,512]{1,0:T(8,128)(2,1)S(1)}, bf16[144,512]{1,0:T(8,128)(2,1)S(1)}, u32[]{:S(2)}, u32[]{:S(2)}) collective-permute-start(bf16[144,512]{1,0:T(8,128)(2,1)S(1)} %get-tuple-element.54.refs_0_), channel_id=1, source_target_pairs={{0,8},{1,9},{2,10},{3,11},{4,12},{5,13},{6,14},{7,15},{8,0},{9,1},... | collective-permute-start | bytes 442376 | tf_op jit(solution)/shard_map/ppermute | solution.py:410
  23.3 0.0 collective-permute-done.7.refs_1_
  23.3 3.5 %attend2.1 = (f32[2,128,2048]{2,1,0:T(8,128)S(1)}, f32[2,128,2048]{2,1,0:T(8,128)S(1)}, f32[2,128,2048]{2,1,0:T(8,128)S(1)}) custom-call(s32[4]{0:T(128)S(1)} %pad_add_fusion.place, bf16[2,128,2048]{2,1,0:T(8,128)(2,1)S(1)} %copy-done, bf16[272,512]{1,0:T(8,128)(2,1)S(1)} %get-tuple-element.50.own_ref.refs_0_.low_ref, ...), custom_call_target="tpu_custom_call" | custom-call | flops 2990000128 | tf_op jit(solution)/shard_map/attend2/pallas_call | solution.py:40
  26.8 2.2 %collective-permute-done.6.high_ref.refs_2_ = bf16[272,512]{1,0:T(8,128)(2,1)S(1)} collective-permute-done((bf16[272,512]{1,0:T(8,128)(2,1)S(1)}, bf16[272,512]{1,0:T(8,128)(2,1)S(1)}, u32[]{:S(2)}, u32[]{:S(2)}) %collective-permute-start.6) | collective-permute-done | bytes 278560 | tf_op jit(solution)/shard_map/ppermute | solution.py:410
  29.0 0.6 %pick.1 = bf16[272,512]{1,0:T(8,128)(2,1)S(1)} custom-call(s32[4]{0:T(128)S(1)} %pad_add_fusion.place, bf16[272,512]{1,0:T(8,128)(2,1)S(1)} %collective-permute-done.3.high_ref.refs_0_.low_ref, bf16[272,512]{1,0:T(8,128)(2,1)S(1)} %collective-permute-done.6.high_ref.refs_2_), custom_call_target="tpu_custom_call" | custom-call | flops 23000000512 | tf_op jit(solution)/shard_map/pick/pallas_call | solution.py:40
  29.5 1.7 %collective-permute-start.11 = (bf16[272,512]{1,0:T(8,128)(2,1)S(1)}, bf16[272,512]{1,0:T(8,128)(2,1)S(1)}, u32[]{:S(2)}, u32[]{:S(2)}) collective-permute-start(bf16[272,512]{1,0:T(8,128)(2,1)S(1)} %collective-permute-done.6.high_ref.refs_2_), channel_id=1, source_target_pairs={{0,1},{1,0},{2,3},{3,2},{4,5},{5,4},{6,7},{7,6},{8,9},{9,8},{10,11... | collective-permute-start | bytes 835592 | tf_op jit(solution)/shard_map/ppermute | solution.py:410
  31.3 1.3 %collective-permute-start.13 = (bf16[272,512]{1,0:T(8,128)(2,1)S(1)}, bf16[272,512]{1,0:T(8,128)(2,1)S(1)}, u32[]{:S(2)}, u32[]{:S(2)}) collective-permute-start(bf16[272,512]{1,0:T(8,128)(2,1)S(1)} %pick.1), channel_id=1, source_target_pairs={{0,2},{1,3},{2,0},{3,1},{4,6},{5,7},{6,4},{7,5},{8,10},{9,11},{10,... | collective-permute-start | bytes 835592 | tf_op jit(solution)/shard_map/ppermute | solution.py:410
  32.5 0.0 collective-permute-done.9.refs_0_
  32.5 0.3 collective-permute-start.10
  32.9 2.9 %collective-permute-done.5.refs_2_ = bf16[144,512]{1,0:T(8,128)(2,1)S(1)} collective-permute-done((bf16[144,512]{1,0:T(8,128)(2,1)S(1)}, bf16[144,512]{1,0:T(8,128)(2,1)S(1)}, u32[]{:S(2)}, u32[]{:S(2)}) %collective-permute-start.5) | collective-permute-done | bytes 147488 | tf_op jit(solution)/shard_map/ppermute | solution.py:410
  35.7 0.6 %hop2.1 = (bf16[128,512]{1,0:T(8,128)(2,1)S(1)}, bf16[128,512]{1,0:T(8,128)(2,1)S(1)}) custom-call(s32[4]{0:T(128)S(1)} %pad_add_fusion.place, bf16[144,512]{1,0:T(8,128)(2,1)S(1)} %get-tuple-element.54.refs_0_, bf16[144,512]{1,0:T(8,128)(2,1)S(1)} %get-tuple-element.55.refs_1_, bf16[144,512]{1,0:T(8,128)(2,1)S(1)} %collective-permute-done.5.refs_2_, ...), custom_call_target="tpu_custom_call" | custom-call | flops 23000000512 | tf_op jit(solution)/shard_map/hop2/pallas_call | solution.py:40
  36.4 1.3 %collective-permute-start.8 = (bf16[128,512]{1,0:T(8,128)(2,1)S(1)}, bf16[128,512]{1,0:T(8,128)(2,1)S(1)}, u32[]{:S(2)}, u32[]{:S(2)}) collective-permute-start(bf16[128,512]{1,0:T(8,128)(2,1)S(1)} %get-tuple-element.65), channel_id=1, source_target_pairs={{0,2},{1,3},{2,0},{3,1},{4,6},{5,7},{6,4},{7,5},{8,10},{9,11},{10,... | collective-permute-start | bytes 393224 | tf_op jit(solution)/shard_map/ppermute | solution.py:410
  37.7 0.0 collective-permute-done.11.refs_3_
  37.7 0.0 collective-permute-done.10.refs_1_
  37.7 5.1 %attend4.1 = (f32[2,128,2048]{2,1,0:T(8,128)S(1)}, f32[2,128,2048]{2,1,0:T(8,128)S(1)}, f32[2,128,2048]{2,1,0:T(8,128)S(1)}) custom-call(s32[4]{0:T(128)S(1)} %pad_add_fusion.place, bf16[2,128,2048]{2,1,0:T(8,128)(2,1)S(1)} %copy-done, bf16[272,512]{1,0:T(8,128)(2,1)S(1)} %get-tuple-element.50.own_ref.refs_0_.low_ref, ...), custom_call_target="tpu_custom_call" | custom-call | flops 5405000192 | tf_op jit(solution)/shard_map/attend4/pallas_call | solution.py:40
  42.8 0.0 collective-permute-done.13.refs_0_
  42.8 0.8 %collective-permute-start.14 = (bf16[272,512]{1,0:T(8,128)(2,1)S(1)}, bf16[272,512]{1,0:T(8,128)(2,1)S(1)}, u32[]{:S(2)}, u32[]{:S(2)}) collective-permute-start(bf16[272,512]{1,0:T(8,128)(2,1)S(1)} %collective-permute-done.13.refs_0_), channel_id=1, source_target_pairs={{0,1},{1,0},{2,3},{3,2},{4,5},{5,4},{6,7},{7,6},{8,9},{9,8},{10,11... | collective-permute-start | bytes 835592 | tf_op jit(solution)/shard_map/ppermute | solution.py:410
  43.6 0.0 collective-permute-done.8.other_ref
  43.6 1.5 %finish.1 = (bf16[128,1024]{1,0:T(8,128)(2,1)S(1)}, bf16[128,1024]{1,0:T(8,128)(2,1)S(1)}) custom-call(s32[4]{0:T(128)S(1)} %pad_add_fusion.place, f32[2,128,1024]{2,1,0:T(8,128)S(1)} %get-tuple-element.44.mixed_ref, f32[2,128,128]{2,1,0:T(8,128)S(1)} %get-tuple-element.45.run_ref, bf16[2,128,128]{2,1,0:T(8,128)(2,1)S(1)} %get-tuple-element.46.read_ref, ...), custom_call_target="tpu_custom_call" | custom-call | flops 1955000064 | tf_op jit(solution)/shard_map/finish/pallas_call | solution.py:40
  45.1 0.1 collective-permute-start.12
  45.2 0.0 collective-permute-done.14.refs_1_
  45.2 4.6 %attend3.1 = bf16[2,128,2048]{2,1,0:T(8,128)(2,1)} custom-call(s32[4]{0:T(128)S(1)} %pad_add_fusion.place, bf16[2,128,2048]{2,1,0:T(8,128)(2,1)S(1)} %copy-done, bf16[272,512]{1,0:T(8,128)(2,1)S(1)} %get-tuple-element.50.own_ref.refs_0_.low_ref, bf16[272,512]{1,0:T(8,128)(2,1)S(1)} %collective-permute-done.13.refs_0_, ...), custom_call_target="tpu_custom_call" | custom-call | flops 2990000128 | tf_op jit(solution)/shard_map/attend3/pallas_call | solution.py:40
  49.8 0.0 collective-permute-done.12.c_ref
  49.8 1.4 %collect.1 = bf16[128,2048]{1,0:T(8,128)(2,1)} custom-call(s32[4]{0:T(128)S(1)} %pad_add_fusion.place, bf16[128,1024]{1,0:T(8,128)(2,1)S(1)} %get-tuple-element.73.self_ref, bf16[128,1024]{1,0:T(8,128)(2,1)S(1)} %collective-permute-done.12.c_ref), custom_call_target="tpu_custom_call" | custom-call | flops 920000000 | tf_op jit(solution)/shard_map/collect/pallas_call | solution.py:40
Async XLA Ops:
  2.7 3.2 %collective-permute-start = (bf16[128,1408]{1,0:T(8,128)(2,1)S(1)}, bf16[128,1408]{1,0:T(8,128)(2,1)S(1)}, u32[]{:S(2)}, u32[]{:S(2)}) collective-permute-start(bf16[128,1408]{1,0:T(8,128)(2,1)S(1)} %get-tuple-element.42), channel_id=1, source_target_pairs={{0,1},{1,0},{2,3},{3,2},{4,5},{5,4},{6,7},{7,6},{8,9},{9,8},{10,11... | collective-permute-start | bytes 1081352 | tf_op jit(solution)/shard_map/ppermute | solution.py:410
  2.9 12.3 %collective-permute-start.3 = (bf16[272,512]{1,0:T(8,128)(2,1)S(1)}, bf16[272,512]{1,0:T(8,128)(2,1)S(1)}, u32[]{:S(2)}, u32[]{:S(2)}) collective-permute-start(bf16[272,512]{1,0:T(8,128)(2,1)S(1)} %get-tuple-element.50.own_ref.refs_0_.low_ref), channel_id=1, source_target_pairs={{0,4},{1,5},{2,6},{3,7},{4,8},{5,9},{6,10},{7,11},{8,12},{9,13},{1... | collective-permute-start | bytes 835592 | tf_op jit(solution)/shard_map/ppermute | solution.py:410
  5.6 5.5 %collective-permute-start.2 = (bf16[272,512]{1,0:T(8,128)(2,1)S(1)}, bf16[272,512]{1,0:T(8,128)(2,1)S(1)}, u32[]{:S(2)}, u32[]{:S(2)}) collective-permute-start(bf16[272,512]{1,0:T(8,128)(2,1)S(1)} %get-tuple-element.50.own_ref.refs_0_.low_ref), channel_id=1, source_target_pairs={{0,1},{1,0},{2,3},{3,2},{4,5},{5,4},{6,7},{7,6},{8,9},{9,8},{10,11... | collective-permute-start | bytes 835592 | tf_op jit(solution)/shard_map/ppermute | solution.py:410
  6.0 5.1 %copy-start = (bf16[2,128,2048]{2,1,0:T(8,128)(2,1)S(1)}, bf16[2,128,2048]{2,1,0:T(8,128)(2,1)}, u32[]{:S(2)}) copy-start(bf16[2,128,2048]{2,1,0:T(8,128)(2,1)} %q_ref.3) | copy-start | bytes 3145732
  9.8 5.4 %collective-permute-start.1 = (bf16[144,512]{1,0:T(8,128)(2,1)S(1)}, bf16[144,512]{1,0:T(8,128)(2,1)S(1)}, u32[]{:S(2)}, u32[]{:S(2)}) collective-permute-start(bf16[144,512]{1,0:T(8,128)(2,1)S(1)} %get-tuple-element.48), channel_id=1, source_target_pairs={{0,2},{1,3},{2,0},{3,1},{4,6},{5,7},{6,4},{7,5},{8,10},{9,11},{10,... | collective-permute-start | bytes 442376 | tf_op jit(solution)/shard_map/ppermute | solution.py:410
  15.8 6.2 %collective-permute-start.4 = (bf16[144,512]{1,0:T(8,128)(2,1)S(1)}, bf16[144,512]{1,0:T(8,128)(2,1)S(1)}, u32[]{:S(2)}, u32[]{:S(2)}) collective-permute-start(bf16[144,512]{1,0:T(8,128)(2,1)S(1)} %get-tuple-element.53.refs_0_), channel_id=1, source_target_pairs={{0,4},{1,5},{2,6},{3,7},{4,8},{5,9},{6,10},{7,11},{8,12},{9,13},{1... | collective-permute-start | bytes 442376 | tf_op jit(solution)/shard_map/ppermute | solution.py:410
  17.2 6.1 %collective-permute-start.7 = (bf16[272,512]{1,0:T(8,128)(2,1)S(1)}, bf16[272,512]{1,0:T(8,128)(2,1)S(1)}, u32[]{:S(2)}, u32[]{:S(2)}) collective-permute-start(bf16[272,512]{1,0:T(8,128)(2,1)S(1)} %collective-permute-done.3.high_ref.refs_0_.low_ref), channel_id=1, source_target_pairs={{0,1},{1,0},{2,3},{3,2},{4,5},{5,4},{6,7},{7,6},{8,9},{9,8},{10,11... | collective-permute-start | bytes 835592 | tf_op jit(solution)/shard_map/ppermute | solution.py:410
  18.4 10.5 %collective-permute-start.6 = (bf16[272,512]{1,0:T(8,128)(2,1)S(1)}, bf16[272,512]{1,0:T(8,128)(2,1)S(1)}, u32[]{:S(2)}, u32[]{:S(2)}) collective-permute-start(bf16[272,512]{1,0:T(8,128)(2,1)S(1)} %collective-permute-done.3.high_ref.refs_0_.low_ref), channel_id=1, source_target_pairs={{0,4},{1,5},{2,6},{3,7},{4,8},{5,9},{6,10},{7,11},{8,12},{9,13},{1... | collective-permute-start | bytes 835592 | tf_op jit(solution)/shard_map/ppermute | solution.py:410
  19.7 12.8 %collective-permute-start.9 = (bf16[272,512]{1,0:T(8,128)(2,1)S(1)}, bf16[272,512]{1,0:T(8,128)(2,1)S(1)}, u32[]{:S(2)}, u32[]{:S(2)}) collective-permute-start(bf16[272,512]{1,0:T(8,128)(2,1)S(1)} %get-tuple-element.67), channel_id=1, source_target_pairs={{0,2},{1,3},{2,0},{3,1},{4,6},{5,7},{6,4},{7,5},{8,10},{9,11},{10,... | collective-permute-start | bytes 835592 | tf_op jit(solution)/shard_map/ppermute | solution.py:410
  22.7 13.0 %collective-permute-start.5 = (bf16[144,512]{1,0:T(8,128)(2,1)S(1)}, bf16[144,512]{1,0:T(8,128)(2,1)S(1)}, u32[]{:S(2)}, u32[]{:S(2)}) collective-permute-start(bf16[144,512]{1,0:T(8,128)(2,1)S(1)} %get-tuple-element.54.refs_0_), channel_id=1, source_target_pairs={{0,8},{1,9},{2,10},{3,11},{4,12},{5,13},{6,14},{7,15},{8,0},{9,1},... | collective-permute-start | bytes 442376 | tf_op jit(solution)/shard_map/ppermute | solution.py:410
  29.5 8.2 %collective-permute-start.11 = (bf16[272,512]{1,0:T(8,128)(2,1)S(1)}, bf16[272,512]{1,0:T(8,128)(2,1)S(1)}, u32[]{:S(2)}, u32[]{:S(2)}) collective-permute-start(bf16[272,512]{1,0:T(8,128)(2,1)S(1)} %collective-permute-done.6.high_ref.refs_2_), channel_id=1, source_target_pairs={{0,1},{1,0},{2,3},{3,2},{4,5},{5,4},{6,7},{7,6},{8,9},{9,8},{10,11... | collective-permute-start | bytes 835592 | tf_op jit(solution)/shard_map/ppermute | solution.py:410
  31.3 11.5 %collective-permute-start.13 = (bf16[272,512]{1,0:T(8,128)(2,1)S(1)}, bf16[272,512]{1,0:T(8,128)(2,1)S(1)}, u32[]{:S(2)}, u32[]{:S(2)}) collective-permute-start(bf16[272,512]{1,0:T(8,128)(2,1)S(1)} %pick.1), channel_id=1, source_target_pairs={{0,2},{1,3},{2,0},{3,1},{4,6},{5,7},{6,4},{7,5},{8,10},{9,11},{10,... | collective-permute-start | bytes 835592 | tf_op jit(solution)/shard_map/ppermute | solution.py:410
  32.5 5.2 %collective-permute-start.10 = (bf16[272,512]{1,0:T(8,128)(2,1)S(1)}, bf16[272,512]{1,0:T(8,128)(2,1)S(1)}, u32[]{:S(2)}, u32[]{:S(2)}) collective-permute-start(bf16[272,512]{1,0:T(8,128)(2,1)S(1)} %collective-permute-done.9.refs_0_), channel_id=1, source_target_pairs={{0,1},{1,0},{2,3},{3,2},{4,5},{5,4},{6,7},{7,6},{8,9},{9,8},{10,11... | collective-permute-start | bytes 835592 | tf_op jit(solution)/shard_map/ppermute | solution.py:410
  36.4 7.2 %collective-permute-start.8 = (bf16[128,512]{1,0:T(8,128)(2,1)S(1)}, bf16[128,512]{1,0:T(8,128)(2,1)S(1)}, u32[]{:S(2)}, u32[]{:S(2)}) collective-permute-start(bf16[128,512]{1,0:T(8,128)(2,1)S(1)} %get-tuple-element.65), channel_id=1, source_target_pairs={{0,2},{1,3},{2,0},{3,1},{4,6},{5,7},{6,4},{7,5},{8,10},{9,11},{10,... | collective-permute-start | bytes 393224 | tf_op jit(solution)/shard_map/ppermute | solution.py:410
  42.8 2.4 %collective-permute-start.14 = (bf16[272,512]{1,0:T(8,128)(2,1)S(1)}, bf16[272,512]{1,0:T(8,128)(2,1)S(1)}, u32[]{:S(2)}, u32[]{:S(2)}) collective-permute-start(bf16[272,512]{1,0:T(8,128)(2,1)S(1)} %collective-permute-done.13.refs_0_), channel_id=1, source_target_pairs={{0,1},{1,0},{2,3},{3,2},{4,5},{5,4},{6,7},{7,6},{8,9},{9,8},{10,11... | collective-permute-start | bytes 835592 | tf_op jit(solution)/shard_map/ppermute | solution.py:410
  45.1 4.7 %collective-permute-start.12 = (bf16[128,1024]{1,0:T(8,128)(2,1)S(1)}, bf16[128,1024]{1,0:T(8,128)(2,1)S(1)}, u32[]{:S(2)}, u32[]{:S(2)}) collective-permute-start(bf16[128,1024]{1,0:T(8,128)(2,1)S(1)} %get-tuple-element.74), channel_id=1, source_target_pairs={{0,1},{1,0},{2,3},{3,2},{4,5},{5,4},{6,7},{7,6},{8,9},{9,8},{10,11... | collective-permute-start | bytes 786440 | tf_op jit(solution)/shard_map/ppermute | solution.py:410

commit v5 on v4

--- a/solution.py
+++ b/solution.py
@@ -16,7 +16,6 @@
 F32 = jnp.float32
 BF16 = jnp.bfloat16
 VMEM = pltpu.VMEM
-IN_SMEM = pl.BlockSpec(memory_space=pltpu.SMEM)
 IN_VMEM = pl.BlockSpec(memory_space=pltpu.VMEM)
 LOGS = 16
 
@@ -35,20 +34,25 @@
     return pl.ds(pl.multiple_of(number * width, width), width)
 
 
-def call(kernel, name, micros, place, args, outs, scratch=(), stay=False, mib=8):
+def call(kernel, name, micros, args, outs, scratch=(), stay=False, mib=8):
     spec = pl.BlockSpec(memory_space=pltpu.HBM) if stay else IN_VMEM
+
+    def placed(*refs):
+        rank = lax.axis_index("seq")
+        kernel((rank & 1, (rank >> 1) & 1, rank >> 2, rank >> 1), *refs)
+
     return pl.pallas_call(
-        kernel,
+        placed,
         name=name,
         out_shape=outs,
-        in_specs=[IN_SMEM] + [spec] * len(args),
+        in_specs=[spec] * len(args),
         out_specs=jax.tree.map(lambda _: IN_VMEM, outs),
         scratch_shapes=list(scratch),
         cost_estimate=pl.CostEstimate(
             flops=int(micros * 1.15e9), bytes_accessed=0, transcendentals=0
         ),
         compiler_params=pltpu.CompilerParams(vmem_limit_bytes=mib * 1024 * 1024),
-    )(place, *[pltpu.with_memory_space_constraint(a, pltpu.HBM) if stay else a for a in args])
+    )(*[pltpu.with_memory_space_constraint(a, pltpu.HBM) if stay else a for a in args])
 
 
 def shaped(*shape, dtype=BF16):
@@ -56,7 +60,7 @@
 
 
 def pack_kernel(
-    place, x, write, read, codes, kv, seg, rate, own, mine, to_c, rates, code_buf, seg_buf, rate_buf,
+    place, x, write, read, codes, kv, seg, rate, own, docs, mine, to_c, rates, code_buf, seg_buf, rate_buf,
     sems
 ):
     core = place[0]
@@ -87,6 +91,7 @@
         copy.wait()
     codes_of = (seg_buf[...] + 1).astype(F32).astype(BF16)
     own[2 * tokens :, 0:tokens] = jnp.broadcast_to(codes_of, (16, tokens))
+    docs[...] = jnp.transpose(jnp.broadcast_to(codes_of.astype(F32), (tokens, tokens)))
     code = code_buf[...]
     high = (code >> 6).astype(F32)
     low = (code & 63).astype(F32)
@@ -97,7 +102,7 @@
     rates[...] = jnp.concatenate([rate_buf[...], jnp.zeros((1, 128 - heads), F32)], axis=1)
 
 
-def attend_kernel(kinds, first, last, place, q_ref, own_ref, *refs):
+def attend_kernel(kinds, first, last, place, q_ref, doc_ref, *refs):
     count = len(kinds)
     rows = q_ref.shape[1]
     pieces = refs[:count]
@@ -114,8 +119,7 @@
     k_all, v_all, bias = refs[at : at + 3]
     core = place[0]
     chip = place[3]
-    codes = own_ref[2 * rows : 2 * rows + 16, 0:rows].astype(F32)
-    mine = jnp.transpose(jnp.broadcast_to(codes[0:1], (rows, rows)))
+    mine = doc_ref[...]
     i = lax.broadcasted_iota(jnp.int32, (rows, rows), 0)
     j = lax.broadcasted_iota(jnp.int32, (rows, rows), 1)
     for n, (behind, other) in enumerate(kinds):
@@ -174,7 +178,7 @@
     lax.fori_loop(0, KV_HEADS, one, 0)
 
 
-def attend(place, queries, own, pieces, kinds, carry, last):
+def attend(queries, docs, pieces, kinds, carry, last):
     layers, tokens, width = queries.shape
     count = len(kinds)
     partial = shaped(layers, tokens, width, dtype=F32)
@@ -182,8 +186,7 @@
         functools.partial(attend_kernel, kinds, carry is None, last),
         "attend%d" % kinds[-1][0],
         0.5 + 1.05 * count,
-        place,
-        [queries, own]
+        [queries, docs]
         + list(pieces)
         + [pltpu.with_memory_space_constraint(part, pltpu.VMEM) for part in carry or ()],
         shaped(layers, tokens, width) if last else (partial,) * 3,
@@ -219,20 +222,19 @@
     return parts[0:1] + parts[1:2] + parts[2:3]
 
 
-def local_kernel(
-    heads, state, place, own_ref, c_ref, rate_ref, mixed_ref, mine_ref, give_ref, run_ref, read_ref,
+def states_kernel(
+    heads, state, place, own_ref, c_ref, rate_ref, mine_ref, give_ref, early_ref, run_ref, turn_ref,
     xs, tail
 ):
     tokens = own_ref.shape[0]
-    cols = mixed_ref.shape[2]
+    cols = early_ref.shape[1]
     width = cols // heads
-    core = place[0]
+    core, y = place[0], place[1]
     xs[core] = own_ref[...]
     xs[1 - core] = c_ref[...]
     i = lax.broadcasted_iota(jnp.int32, (tokens, tokens), 0)
     j = lax.broadcasted_iota(jnp.int32, (tokens, tokens), 1)
-    causal = j <= i
-    lower_ones = causal.astype(F32)
+    lower_ones = (j <= i).astype(F32)
     upper_ones = (i <= j).astype(F32)
     low = lax.broadcasted_iota(jnp.int32, (1, 2 * width), 1) < width
     rates = rate_ref[...]
@@ -241,8 +243,6 @@
     offset = None
     for b in range(2):
         write = xs[b, :, cols : cols + state]
-        read = xs[b, :, cols + state : cols + 2 * state]
-        read_ref[b] = read
         high = xs[b, :, cols + 2 * state :].astype(F32)
         little = pltpu.roll(high, 64, 1)
         level = jnp.floor(high * 0.0625)
@@ -252,22 +252,51 @@
         run = jnp.dot(
             lower_ones, step, preferred_element_type=F32, precision=lax.Precision.HIGHEST
         )
-        run_t = tn_dot(step, upper_ones, lax.Precision.HIGHEST)
+        run_ref[b] = run
+        turn_ref[b] = tn_dot(step, upper_ones, lax.Precision.HIGHEST)
         end = run[tokens - 1 : tokens, :]
-        run_ref[b] = run if b == 0 else run + offset
         offset = end if b == 0 else offset + end
-        inner = jnp.where(causal, nt_dot(read, write), 0.0)
         to_end = jnp.exp(end - run)
-        fade = jnp.exp(run)
+        scaled = []
+        for pair in range(heads // 2):
+            tile = xs[b, :, pair * 2 * width : (pair + 1) * 2 * width]
+            weight = jnp.where(
+                low, to_end[:, 2 * pair : 2 * pair + 1], to_end[:, 2 * pair + 1 : 2 * pair + 2]
+            )
+            scaled.append((weight * tile.astype(F32)).astype(BF16))
+        added = tn_dot(write, jnp.concatenate(scaled, axis=1))
+        if b == 0:
+            kept = added
+            early_ref[...] = kept.astype(BF16)
+        else:
+            kept = spread(jnp.exp(end), heads // 2, width) * kept + added
+    tail[0:state, :] = kept.astype(BF16)
+    put_logs(tail, state, spread(offset, heads // 2, width))
+    mine_ref[...] = tail[:, lanes(y, cols // 2)]
+    give_ref[...] = tail[:, lanes(1 - y, cols // 2)]
+
+
+def local_kernel(heads, state, place, xs, early_ref, run_ref, turn_ref, mixed_ref):
+    tokens = run_ref.shape[1]
+    cols = mixed_ref.shape[2]
+    width = cols // heads
+    i = lax.broadcasted_iota(jnp.int32, (tokens, tokens), 0)
+    j = lax.broadcasted_iota(jnp.int32, (tokens, tokens), 1)
+    low = lax.broadcasted_iota(jnp.int32, (1, 2 * width), 1) < width
+    for b in range(2):
+        write = xs[b, :, cols : cols + state]
+        read = xs[b, :, cols + state : cols + 2 * state]
+        run = run_ref[b]
+        inner = jnp.where(j <= i, nt_dot(read, write), 0.0)
         if b > 0:
-            seen = jnp.dot(read, kept.astype(BF16), preferred_element_type=F32)
-        scaled = []
+            fade = jnp.exp(run)
+            seen = jnp.dot(read, early_ref[...], preferred_element_type=F32)
         for pair in range(heads // 2):
             part = slice(pair * 2 * width, (pair + 1) * 2 * width)
             tile = xs[b, :, part]
             mixes = []
             for h in (2 * pair, 2 * pair + 1):
-                gap = jnp.minimum(run[:, h : h + 1] - run_t[h : h + 1, :], 0.0)
+                gap = jnp.minimum(run[:, h : h + 1] - turn_ref[b, h : h + 1, :], 0.0)
                 mixes.append((inner * jnp.exp(gap)).astype(BF16))
             zero = jnp.zeros_like(tile)
             stacked = jnp.concatenate(
@@ -279,19 +308,6 @@
                     low, fade[:, 2 * pair : 2 * pair + 1], fade[:, 2 * pair + 1 : 2 * pair + 2]
                 )
             mixed_ref[b, :, part] = mixed
-            weight = jnp.where(
-                low, to_end[:, 2 * pair : 2 * pair + 1], to_end[:, 2 * pair + 1 : 2 * pair + 2]
-            )
-            scaled.append((weight * tile.astype(F32)).astype(BF16))
-        added = tn_dot(write, jnp.concatenate(scaled, axis=1))
-        if b > 0:
-            added = spread(jnp.exp(end), heads // 2, width) * kept + added
-        kept = added
-    tail[0:state, :] = kept.astype(BF16)
-    put_logs(tail, state, spread(offset, heads // 2, width))
-    y = place[1]
-    mine_ref[...] = tail[:, lanes(y, cols // 2)]
-    give_ref[...] = tail[:, lanes(1 - y, cols // 2)]
 
 
 def pick(place, low_ref, high_ref, out_ref):
@@ -351,7 +367,7 @@
 
 
 def finish_kernel(
-    heads, state, place, mixed_ref, run_ref, read_ref, mine_ref, other_ref, self_ref, c_ref
+    heads, state, place, mixed_ref, run_ref, xs, mine_ref, other_ref, self_ref, c_ref
 ):
     core = place[0]
     y = place[1]
@@ -368,8 +384,10 @@
     average = jnp.where(same, 1.0 / width, 0.0).astype(BF16)
     low = lax.broadcasted_iota(jnp.int32, (1, 2 * width), 1) < width
     for out_ref, at in ((c_ref, 1 - core), (self_ref, core)):
-        seen = jnp.dot(read_ref[at], entering, preferred_element_type=F32)
-        fade = jnp.exp(run_ref[at])
+        read = xs[at, :, cols + state : cols + 2 * state]
+        seen = jnp.dot(read, entering, preferred_element_type=F32)
+        ahead = jnp.where(at == 0, 0.0, run_ref[0, run_ref.shape[1] - 1 :, :])
+        fade = jnp.exp(run_ref[at] + ahead)
         for pair in range(heads // 2):
             part = slice(pair * 2 * width, (pair + 1) * 2 * width)
             tile = mixed_ref[at, :, part] + seen[:, part] * jnp.where(
@@ -404,9 +422,6 @@
     cols = channels // 2
     devices = lax.axis_size("seq")
     rows = devices // ROW
-    rank = lax.axis_index("seq")
-    core, y = rank % 2, (rank // 2) % 2
-    place = jnp.stack([core, y, rank // ROW, rank // 2]).astype(jnp.int32)
     send = lambda x, route: lax.ppermute(x, "seq", [(i, route(i)) for i in range(devices)])
     swap_c = lambda i: i ^ 1
     swap_y = lambda i: i ^ 2
@@ -414,11 +429,10 @@
     kv_width = keys_values.shape[2]
     half = cols // 2
 
-    own, mine, to_c, rates = call(
+    own, docs, mine, to_c, rates = call(
         pack_kernel,
         "pack",
         1.5,
-        place,
         [
             ssm_inputs,
             state_write,
@@ -430,6 +444,7 @@
         ],
         (
             shaped(2 * tokens + 16, kv_width),
+            shaped(tokens, tokens, dtype=F32),
             shaped(tokens, cols + 2 * state + 128),
             shaped(tokens, cols + 2 * state + 128),
             shaped(1, 128, dtype=F32),
@@ -446,34 +461,30 @@
     behind2 = send(own, up(1))
     partner = send(own, swap_c)
 
-    mixed, tail, tail_out, run, reads = call(
-        functools.partial(local_kernel, heads // 2, state),
-        "local",
-        4.3,
-        place,
+    tail, tail_out, early, run, run_t, blocks = call(
+        functools.partial(states_kernel, heads // 2, state),
+        "states",
+        2.0,
         [mine, from_c, rates],
         (
-            shaped(2, tokens, cols, dtype=F32),
             shaped(state + LOGS, half),
             shaped(state + LOGS, half),
+            shaped(state, cols),
             shaped(2, tokens, 128, dtype=F32),
-            shaped(2, tokens, state),
+            shaped(2, 128, tokens, dtype=F32),
+            shaped(2, tokens, cols + 2 * state + 128),
         ),
-        [
-            VMEM((2, tokens, cols + 2 * state + 128), BF16),
-            VMEM((state + LOGS, cols), BF16),
-        ],
+        [VMEM((state + LOGS, cols), BF16)],
     )
     tail_y = send(tail_out, swap_y)
     carry = attend(
-        place, after(queries, tail), own, [own, partner], ((0, False), (0, True)), None, False
+        after(queries, tail), docs, [own, partner], ((0, False), (0, True)), None, False
     )
     tail_y = after(tail_y, carry[0])
     span, first, to_y = call(
         functools.partial(row_kernel, state),
         "row",
         20.0,
-        place,
         [tail, tail_y, own, behind2],
         (shaped(state + LOGS, half),) * 2 + (shaped(2 * tokens + 16, kv_width),),
     )
@@ -482,6 +493,14 @@
     behind4 = send(behind2, up(1))
     behind1 = send(to_y, swap_y)
     behind2c = send(behind2, swap_c)
+    mixed = call(
+        functools.partial(local_kernel, heads // 2, state),
+        "local",
+        3.0,
+        [after(blocks, span), early, run, run_t],
+        shaped(2, tokens, cols, dtype=F32),
+    )
+    new = after(new, mixed)
     before = None
     distance = 1
     while distance < rows:
@@ -490,7 +509,6 @@
             functools.partial(hop_kernel, state, distance, last),
             "hop%d" % distance,
             20.0,
-            place,
             [span] + [before] * (distance > 1) + [new] + [first] * last,
             (shaped(state, half) if last else shaped(state + LOGS, half),) * 2,
         )
@@ -501,9 +519,8 @@
             new = send(span, up(2 * distance))
         if distance == 1:
             carry = attend(
-                place,
                 after(queries, before),
-                own,
+                docs,
                 [behind2, behind2c],
                 ((2, False), (2, True)),
                 carry,
@@ -516,7 +533,6 @@
                 pick,
                 "pick",
                 20.0,
-                place,
                 [behind2, behind4],
                 shaped(2 * tokens + 16, kv_width),
             )
@@ -524,9 +540,8 @@
             new = after(new, to_y)
         distance *= 2
     carry = attend(
-        place,
         after(queries, give),
-        own,
+        docs,
         [behind1, behind1c, behind4, behind4c],
         ((1, False), (1, True), (4, False), (4, True)),
         carry,
@@ -539,15 +554,13 @@
         functools.partial(finish_kernel, heads // 2, state),
         "finish",
         1.7,
-        place,
-        [mixed, run, reads, keep, other_half],
+        [mixed, run, blocks, keep, other_half],
         (shaped(tokens, cols),) * 2,
     )
     back_c = send(for_c, swap_c)
     attn_output = attend(
-        place,
         after(queries, for_c),
-        own,
+        docs,
         [behind3, behind3c],
         ((3, False), (3, True)),
         carry,
@@ -557,7 +570,6 @@
         collect_kernel,
         "collect",
         0.8,
-        place,
         [done, after(back_c, attn_output)],
         shaped(tokens, channels),
     )

time: 51.8 us -> 47.4 us (0.915)
  Pallas kernels: 27.6 us -> 20.3 us
  waiting for transfers between devices: 7.02 us -> 9.88 us
  starting transfers between devices: 15.8 us -> 16.4 us
    pallas_call x12 -> x13, Pallas kernels: 27.6 us -> 20.3 us  [call(): pl.pallas_call(placed, name=name, out_shape=outs, in_specs=[spec] * len(a...]
    ppermute x15, waiting for transfers between devices: 7.02 us -> 9.88 us  [shards(): lax.ppermute(x, 'seq', [(i, route(i)) for i in range(devices)])]
    ppermute x15, starting transfers between devices: 15.8 us -> 16.4 us  [shards(): lax.ppermute(x, 'seq', [(i, route(i)) for i in range(devices)])]
  transfers between devices with their start and end apart: 15 -> 15, of which waited for: 4 -> 6; matrix products, arithmetic and copies ran while one was open for 0% -> 0% of each run, Pallas kernels for 46% -> 38%
where the time goes in v5:
time: 47.4 us; the launch traced here: 47.3 us
  Pallas kernels  20.3 us (43%)
  starting transfers between devices  16.4 us (35%)
  waiting for transfers between devices  9.88 us (21%)
  between operations  0.73 us (2%)
    pallas_call x13, Pallas kernels, call(): pl.pallas_call(placed, name=name, out_shape=outs, in_specs=[spec] * len(a...  20.3 us
    ppermute x15, starting transfers between devices, shards(): lax.ppermute(x, 'seq', [(i, route(i)) for i in range(devices)])  16.4 us
    ppermute x15, waiting for transfers between devices, shards(): lax.ppermute(x, 'seq', [(i, route(i)) for i in range(devices)])  9.88 us
  transfers between devices with their start and end apart: 15, of which 6 were waited for; matrix products, arithmetic and copies ran while one was open for 0% of the time, Pallas kernels for 38%

profile of v5, /device:TPU:1, one launch (start us, length us, event | category | flops | bytes accessed | tf_op | source)
XLA Modules:
  0.0 47.3 jit_solution(4262108906492710034)
XLA Ops:
  0.6 1.5 %pack.1 = (bf16[272,512]{1,0:T(8,128)(2,1)S(1)}, f32[128,128]{1,0:T(8,128)S(1)}, bf16[128,1408]{1,0:T(8,128)(2,1)S(1)}, bf16[128,1408]{1,0:T(8,128)(2,1)S(1)}, f32[1,128]{1,0:T(1,128)S(1)}) custom-call(bf16[128,2048]{1,0:T(8,128)(2,1)} %refs_0_.1, bf16[128,128]{1,0:T(8,128)(2,1)} %refs_1_.1, bf16[128,128]{1,0:T(8,128)(2,1)} %refs_2_.1, s32[32,128]{1,0:T(8,128)} %bitcast.3, ...), custom_call_target="tpu_custom_call" | custom-call | flops 1724999936 | tf_op jit(solution)/shard_map/pack/pallas_call | solution.py:44
  2.1 0.1 collective-permute-start
  2.2 0.5 collective-permute-start.2
  2.7 2.4 %collective-permute-start.3 = (bf16[272,512]{1,0:T(8,128)(2,1)S(1)}, bf16[272,512]{1,0:T(8,128)(2,1)S(1)}, u32[]{:S(2)}, u32[]{:S(2)}) collective-permute-start(bf16[272,512]{1,0:T(8,128)(2,1)S(1)} %get-tuple-element.53.refs_2_), channel_id=1, source_target_pairs={{0,4},{1,5},{2,6},{3,7},{4,8},{5,9},{6,10},{7,11},{8,12},{9,13},{1... | collective-permute-start | bytes 835592 | tf_op jit(solution)/shard_map/ppermute | solution.py:425
  5.0 0.0 collective-permute-done.refs_1_
  5.0 0.0 copy-start
  5.0 1.6 %states.1 = (bf16[144,512]{1,0:T(8,128)(2,1)S(1)}, bf16[144,512]{1,0:T(8,128)(2,1)S(1)}, bf16[128,1024]{1,0:T(8,128)(2,1)S(1)}, f32[2,128,128]{2,1,0:T(8,128)S(1...) custom-call(bf16[128,1408]{1,0:T(8,128)(2,1)S(1)} %get-tuple-element.45.refs_0_, ...), custom_call_target="tpu_custom_call" | custom-call | flops 2300000000 | tf_op jit(solution)/shard_map/states/pallas_call | solution.py:44
  6.7 1.3 %collective-permute-start.1 = (bf16[144,512]{1,0:T(8,128)(2,1)S(1)}, bf16[144,512]{1,0:T(8,128)(2,1)S(1)}, u32[]{:S(2)}, u32[]{:S(2)}) collective-permute-start(bf16[144,512]{1,0:T(8,128)(2,1)S(1)} %get-tuple-element.50), channel_id=1, source_target_pairs={{0,2},{1,3},{2,0},{3,1},{4,6},{5,7},{6,4},{7,5},{8,10},{9,11},{10,... | collective-permute-start | bytes 442376 | tf_op jit(solution)/shard_map/ppermute | solution.py:425
  8.0 0.0 collective-permute-done.2.refs_3_
  8.0 0.0 copy-done
  8.0 2.6 %attend0.1 = (f32[2,128,2048]{2,1,0:T(8,128)S(1)}, f32[2,128,2048]{2,1,0:T(8,128)S(1)}, f32[2,128,2048]{2,1,0:T(8,128)S(1)}) custom-call(bf16[2,128,2048]{2,1,0:T(8,128)(2,1)S(1)} %copy-done, f32[128,128]{1,0:T(8,128)S(1)} %get-tuple-element.52.refs_1_, bf16[272,512]{1,0:T(8,128)(2,1)S(1)} %get-tuple-element.53.refs_2_, ...), custom_call_target="tpu_custom_call" | custom-call | flops 2990000128 | tf_op jit(solution)/shard_map/attend0/pallas_call | solution.py:44
  10.6 0.8 %collective-permute-done.1.refs_1_ = bf16[144,512]{1,0:T(8,128)(2,1)S(1)} collective-permute-done((bf16[144,512]{1,0:T(8,128)(2,1)S(1)}, bf16[144,512]{1,0:T(8,128)(2,1)S(1)}, u32[]{:S(2)}, u32[]{:S(2)}) %collective-permute-start.1) | collective-permute-done | bytes 147488 | tf_op jit(solution)/shard_map/ppermute | solution.py:425
  11.4 2.3 %collective-permute-done.3.refs_3_.refs_2_.refs_0_ = bf16[272,512]{1,0:T(8,128)(2,1)S(1)} collective-permute-done((bf16[272,512]{1,0:T(8,128)(2,1)S(1)}, bf16[272,512]{1,0:T(8,128)(2,1)S(1)}, u32[]{:S(2)}, u32[]{:S(2)}) %collective-permute-start.3) | collective-permute-done | bytes 278560 | tf_op jit(solution)/shard_map/ppermute | solution.py:425
  13.7 0.1 row.1
  13.8 0.1 collective-permute-start.4
  13.9 1.0 %collective-permute-start.7 = (bf16[272,512]{1,0:T(8,128)(2,1)S(1)}, bf16[272,512]{1,0:T(8,128)(2,1)S(1)}, u32[]{:S(2)}, u32[]{:S(2)}) collective-permute-start(bf16[272,512]{1,0:T(8,128)(2,1)S(1)} %collective-permute-done.3.refs_3_.refs_2_.refs_0_), channel_id=1, source_target_pairs={{0,1},{1,0},{2,3},{3,2},{4,5},{5,4},{6,7},{7,6},{8,9},{9,8},{10,11... | collective-permute-start | bytes 835592 | tf_op jit(solution)/shard_map/ppermute | solution.py:425
  14.9 1.1 %collective-permute-start.6 = (bf16[272,512]{1,0:T(8,128)(2,1)S(1)}, bf16[272,512]{1,0:T(8,128)(2,1)S(1)}, u32[]{:S(2)}, u32[]{:S(2)}) collective-permute-start(bf16[272,512]{1,0:T(8,128)(2,1)S(1)} %collective-permute-done.3.refs_3_.refs_2_.refs_0_), channel_id=1, source_target_pairs={{0,4},{1,5},{2,6},{3,7},{4,8},{5,9},{6,10},{7,11},{8,12},{9,13},{1... | collective-permute-start | bytes 835592 | tf_op jit(solution)/shard_map/ppermute | solution.py:425
  16.1 1.2 %collective-permute-start.9 = (bf16[272,512]{1,0:T(8,128)(2,1)S(1)}, bf16[272,512]{1,0:T(8,128)(2,1)S(1)}, u32[]{:S(2)}, u32[]{:S(2)}) collective-permute-start(bf16[272,512]{1,0:T(8,128)(2,1)S(1)} %get-tuple-element.75), channel_id=1, source_target_pairs={{0,2},{1,3},{2,0},{3,1},{4,6},{5,7},{6,4},{7,5},{8,10},{9,11},{10,... | collective-permute-start | bytes 835592 | tf_op jit(solution)/shard_map/ppermute | solution.py:425
  17.3 1.1 %local.1.refs_0_ = f32[2,128,1024]{2,1,0:T(8,128)S(1)} custom-call(bf16[2,128,1408]{2,1,0:T(8,128)(2,1)S(1)} %get-tuple-element.57.refs_0_.refs_2_, bf16[128,1024]{1,0:T(8,128)(2,1)S(1)} %get-tuple-element.58.refs_1_, f32[2,128,128]{2,1,0:T(8,128)S(1)} %get-tuple-element.59.refs_2_.refs_1_, f32[2,128,128]{2,1,0:T(8,128)S(1)} %get-tuple-element.60.refs_3_), custom_call_target="tpu_custom_call" | custom-call | flops 3449999872 | tf_op jit(solution)/shard_map/local/pallas_call | solution.py:44
  18.4 1.7 %collective-permute-done.4.refs_1_ = bf16[144,512]{1,0:T(8,128)(2,1)S(1)} collective-permute-done((bf16[144,512]{1,0:T(8,128)(2,1)S(1)}, bf16[144,512]{1,0:T(8,128)(2,1)S(1)}, u32[]{:S(2)}, u32[]{:S(2)}) %collective-permute-start.4) | collective-permute-done | bytes 147488 | tf_op jit(solution)/shard_map/ppermute | solution.py:425
  20.1 0.1 hop1.1
  20.2 1.0 %collective-permute-start.5 = (bf16[144,512]{1,0:T(8,128)(2,1)S(1)}, bf16[144,512]{1,0:T(8,128)(2,1)S(1)}, u32[]{:S(2)}, u32[]{:S(2)}) collective-permute-start(bf16[144,512]{1,0:T(8,128)(2,1)S(1)} %get-tuple-element.62.refs_0_), channel_id=1, source_target_pairs={{0,8},{1,9},{2,10},{3,11},{4,12},{5,13},{6,14},{7,15},{8,0},{9,1},... | collective-permute-start | bytes 442376 | tf_op jit(solution)/shard_map/ppermute | solution.py:425
  21.2 0.0 collective-permute-done.7.refs_3_
  21.2 3.0 %attend2.1 = (f32[2,128,2048]{2,1,0:T(8,128)S(1)}, f32[2,128,2048]{2,1,0:T(8,128)S(1)}, f32[2,128,2048]{2,1,0:T(8,128)S(1)}) custom-call(bf16[2,128,2048]{2,1,0:T(8,128)(2,1)S(1)} %copy-done, f32[128,128]{1,0:T(8,128)S(1)} %get-tuple-element.52.refs_1_, bf16[272,512]{1,0:T(8,128)(2,1)S(1)} %collective-permute-done.3.refs_3_.refs_2_.refs_0_, ...), custom_call_target="tpu_custom_call" | custom-call | flops 2990000128 | tf_op jit(solution)/shard_map/attend2/pallas_call | solution.py:44
  24.2 1.9 %collective-permute-done.6.refs_1_.refs_4_ = bf16[272,512]{1,0:T(8,128)(2,1)S(1)} collective-permute-done((bf16[272,512]{1,0:T(8,128)(2,1)S(1)}, bf16[272,512]{1,0:T(8,128)(2,1)S(1)}, u32[]{:S(2)}, u32[]{:S(2)}) %collective-permute-start.6) | collective-permute-done | bytes 278560 | tf_op jit(solution)/shard_map/ppermute | solution.py:425
  26.1 3.5 %collective-permute-start.11 = (bf16[272,512]{1,0:T(8,128)(2,1)S(1)}, bf16[272,512]{1,0:T(8,128)(2,1)S(1)}, u32[]{:S(2)}, u32[]{:S(2)}) collective-permute-start(bf16[272,512]{1,0:T(8,128)(2,1)S(1)} %collective-permute-done.6.refs_1_.refs_4_), channel_id=1, source_target_pairs={{0,1},{1,0},{2,3},{3,2},{4,5},{5,4},{6,7},{7,6},{8,9},{9,8},{10,11... | collective-permute-start | bytes 835592 | tf_op jit(solution)/shard_map/ppermute | solution.py:425
  29.6 0.0 collective-permute-done.9.refs_2_
  29.6 1.1 %collective-permute-start.13 = (bf16[272,512]{1,0:T(8,128)(2,1)S(1)}, bf16[272,512]{1,0:T(8,128)(2,1)S(1)}, u32[]{:S(2)}, u32[]{:S(2)}) collective-permute-start(bf16[272,512]{1,0:T(8,128)(2,1)S(1)} %pick.1), channel_id=1, source_target_pairs={{0,2},{1,3},{2,0},{3,1},{4,6},{5,7},{6,4},{7,5},{8,10},{9,11},{10,... | collective-permute-start | bytes 835592 | tf_op jit(solution)/shard_map/ppermute | solution.py:425
  30.7 0.4 collective-permute-start.10
  31.1 2.7 %collective-permute-done.5.refs_2_ = bf16[144,512]{1,0:T(8,128)(2,1)S(1)} collective-permute-done((bf16[144,512]{1,0:T(8,128)(2,1)S(1)}, bf16[144,512]{1,0:T(8,128)(2,1)S(1)}, u32[]{:S(2)}, u32[]{:S(2)}) %collective-permute-start.5) | collective-permute-done | bytes 147488 | tf_op jit(solution)/shard_map/ppermute | solution.py:425
  33.8 0.1 hop2.1
  33.9 1.1 %collective-permute-start.8 = (bf16[128,512]{1,0:T(8,128)(2,1)S(1)}, bf16[128,512]{1,0:T(8,128)(2,1)S(1)}, u32[]{:S(2)}, u32[]{:S(2)}) collective-permute-start(bf16[128,512]{1,0:T(8,128)(2,1)S(1)} %get-tuple-element.73), channel_id=1, source_target_pairs={{0,2},{1,3},{2,0},{3,1},{4,6},{5,7},{6,4},{7,5},{8,10},{9,11},{10,... | collective-permute-start | bytes 393224 | tf_op jit(solution)/shard_map/ppermute | solution.py:425
  34.9 0.0 collective-permute-done.11.refs_5_
  34.9 0.0 collective-permute-done.10.refs_3_
  34.9 4.4 %attend4.1 = (f32[2,128,2048]{2,1,0:T(8,128)S(1)}, f32[2,128,2048]{2,1,0:T(8,128)S(1)}, f32[2,128,2048]{2,1,0:T(8,128)S(1)}) custom-call(bf16[2,128,2048]{2,1,0:T(8,128)(2,1)S(1)} %copy-done, f32[128,128]{1,0:T(8,128)S(1)} %get-tuple-element.52.refs_1_, bf16[272,512]{1,0:T(8,128)(2,1)S(1)} %collective-permute-done.9.refs_2_, ...), custom_call_target="tpu_custom_call" | custom-call | flops 5405000192 | tf_op jit(solution)/shard_map/attend4/pallas_call | solution.py:44
  39.4 0.0 collective-permute-done.13.refs_2_
  39.4 0.8 %collective-permute-start.14 = (bf16[272,512]{1,0:T(8,128)(2,1)S(1)}, bf16[272,512]{1,0:T(8,128)(2,1)S(1)}, u32[]{:S(2)}, u32[]{:S(2)}) collective-permute-start(bf16[272,512]{1,0:T(8,128)(2,1)S(1)} %collective-permute-done.13.refs_2_), channel_id=1, source_target_pairs={{0,1},{1,0},{2,3},{3,2},{4,5},{5,4},{6,7},{7,6},{8,9},{9,8},{10,11... | collective-permute-start | bytes 835592 | tf_op jit(solution)/shard_map/ppermute | solution.py:425
  40.2 0.4 collective-permute-done.8.refs_4_
  40.6 0.9 %finish.1 = (bf16[128,1024]{1,0:T(8,128)(2,1)S(1)}, bf16[128,1024]{1,0:T(8,128)(2,1)S(1)}) custom-call(f32[2,128,1024]{2,1,0:T(8,128)S(1)} %local.1.refs_0_, f32[2,128,128]{2,1,0:T(8,128)S(1)} %get-tuple-element.59.refs_2_.refs_1_, bf16[2,128,1408]{2,1,0:T(8,128)(2,1)S(1)} %get-tuple-element.57.refs_0_.refs_2_, ...), custom_call_target="tpu_custom_call" | custom-call | flops 1955000064 | tf_op jit(solution)/shard_map/finish/pallas_call | solution.py:44
  41.6 0.9 %collective-permute-start.12 = (bf16[128,1024]{1,0:T(8,128)(2,1)S(1)}, bf16[128,1024]{1,0:T(8,128)(2,1)S(1)}, u32[]{:S(2)}, u32[]{:S(2)}) collective-permute-start(bf16[128,1024]{1,0:T(8,128)(2,1)S(1)} %get-tuple-element.82), channel_id=1, source_target_pairs={{0,1},{1,0},{2,3},{3,2},{4,5},{5,4},{6,7},{7,6},{8,9},{9,8},{10,11... | collective-permute-start | bytes 786440 | tf_op jit(solution)/shard_map/ppermute | solution.py:425
  42.5 0.0 collective-permute-done.14.refs_3_
  42.5 4.0 %attend3.1 = bf16[2,128,2048]{2,1,0:T(8,128)(2,1)} custom-call(bf16[2,128,2048]{2,1,0:T(8,128)(2,1)S(1)} %copy-done, f32[128,128]{1,0:T(8,128)S(1)} %get-tuple-element.52.refs_1_, bf16[272,512]{1,0:T(8,128)(2,1)S(1)} %collective-permute-done.13.refs_2_, bf16[272,512]{1,0:T(8,128)(2,1)S(1)} %collective-permute-done.14.refs_3_, ...), custom_call_target="tpu_custom_call" | custom-call | flops 2990000128 | tf_op jit(solution)/shard_map/attend3/pallas_call | solution.py:44
  46.4 0.0 collective-permute-done.12.refs_1_
  46.5 0.8 %collect.1 = bf16[128,2048]{1,0:T(8,128)(2,1)} custom-call(bf16[128,1024]{1,0:T(8,128)(2,1)S(1)} %get-tuple-element.81.refs_0_, bf16[128,1024]{1,0:T(8,128)(2,1)S(1)} %collective-permute-done.12.refs_1_), custom_call_target="tpu_custom_call" | custom-call | flops 920000000 | tf_op jit(solution)/shard_map/collect/pallas_call | solution.py:44
  (1 shorter events, 0.0 us)
Async XLA Ops:
  2.1 2.9 %collective-permute-start = (bf16[128,1408]{1,0:T(8,128)(2,1)S(1)}, bf16[128,1408]{1,0:T(8,128)(2,1)S(1)}, u32[]{:S(2)}, u32[]{:S(2)}) collective-permute-start(bf16[128,1408]{1,0:T(8,128)(2,1)S(1)} %get-tuple-element.46), channel_id=1, source_target_pairs={{0,1},{1,0},{2,3},{3,2},{4,5},{5,4},{6,7},{7,6},{8,9},{9,8},{10,11... | collective-permute-start | bytes 1081352 | tf_op jit(solution)/shard_map/ppermute | solution.py:425
  2.2 5.8 %collective-permute-start.2 = (bf16[272,512]{1,0:T(8,128)(2,1)S(1)}, bf16[272,512]{1,0:T(8,128)(2,1)S(1)}, u32[]{:S(2)}, u32[]{:S(2)}) collective-permute-start(bf16[272,512]{1,0:T(8,128)(2,1)S(1)} %get-tuple-element.53.refs_2_), channel_id=1, source_target_pairs={{0,1},{1,0},{2,3},{3,2},{4,5},{5,4},{6,7},{7,6},{8,9},{9,8},{10,11... | collective-permute-start | bytes 835592 | tf_op jit(solution)/shard_map/ppermute | solution.py:425
  2.7 11.0 %collective-permute-start.3 = (bf16[272,512]{1,0:T(8,128)(2,1)S(1)}, bf16[272,512]{1,0:T(8,128)(2,1)S(1)}, u32[]{:S(2)}, u32[]{:S(2)}) collective-permute-start(bf16[272,512]{1,0:T(8,128)(2,1)S(1)} %get-tuple-element.53.refs_2_), channel_id=1, source_target_pairs={{0,4},{1,5},{2,6},{3,7},{4,8},{5,9},{6,10},{7,11},{8,12},{9,13},{1... | collective-permute-start | bytes 835592 | tf_op jit(solution)/shard_map/ppermute | solution.py:425
  5.0 2.9 %copy-start = (bf16[2,128,2048]{2,1,0:T(8,128)(2,1)S(1)}, bf16[2,128,2048]{2,1,0:T(8,128)(2,1)}, u32[]{:S(2)}) copy-start(bf16[2,128,2048]{2,1,0:T(8,128)(2,1)} %refs_0_.5) | copy-start | bytes 3145732
  6.7 4.7 %collective-permute-start.1 = (bf16[144,512]{1,0:T(8,128)(2,1)S(1)}, bf16[144,512]{1,0:T(8,128)(2,1)S(1)}, u32[]{:S(2)}, u32[]{:S(2)}) collective-permute-start(bf16[144,512]{1,0:T(8,128)(2,1)S(1)} %get-tuple-element.50), channel_id=1, source_target_pairs={{0,2},{1,3},{2,0},{3,1},{4,6},{5,7},{6,4},{7,5},{8,10},{9,11},{10,... | collective-permute-start | bytes 442376 | tf_op jit(solution)/shard_map/ppermute | solution.py:425
  13.8 6.2 %collective-permute-start.4 = (bf16[144,512]{1,0:T(8,128)(2,1)S(1)}, bf16[144,512]{1,0:T(8,128)(2,1)S(1)}, u32[]{:S(2)}, u32[]{:S(2)}) collective-permute-start(bf16[144,512]{1,0:T(8,128)(2,1)S(1)} %get-tuple-element.56.refs_0_), channel_id=1, source_target_pairs={{0,4},{1,5},{2,6},{3,7},{4,8},{5,9},{6,10},{7,11},{8,12},{9,13},{1... | collective-permute-start | bytes 442376 | tf_op jit(solution)/shard_map/ppermute | solution.py:425
  13.9 7.3 %collective-permute-start.7 = (bf16[272,512]{1,0:T(8,128)(2,1)S(1)}, bf16[272,512]{1,0:T(8,128)(2,1)S(1)}, u32[]{:S(2)}, u32[]{:S(2)}) collective-permute-start(bf16[272,512]{1,0:T(8,128)(2,1)S(1)} %collective-permute-done.3.refs_3_.refs_2_.refs_0_), channel_id=1, source_target_pairs={{0,1},{1,0},{2,3},{3,2},{4,5},{5,4},{6,7},{7,6},{8,9},{9,8},{10,11... | collective-permute-start | bytes 835592 | tf_op jit(solution)/shard_map/ppermute | solution.py:425
  14.9 11.2 %collective-permute-start.6 = (bf16[272,512]{1,0:T(8,128)(2,1)S(1)}, bf16[272,512]{1,0:T(8,128)(2,1)S(1)}, u32[]{:S(2)}, u32[]{:S(2)}) collective-permute-start(bf16[272,512]{1,0:T(8,128)(2,1)S(1)} %collective-permute-done.3.refs_3_.refs_2_.refs_0_), channel_id=1, source_target_pairs={{0,4},{1,5},{2,6},{3,7},{4,8},{5,9},{6,10},{7,11},{8,12},{9,13},{1... | collective-permute-start | bytes 835592 | tf_op jit(solution)/shard_map/ppermute | solution.py:425
  16.1 13.5 %collective-permute-start.9 = (bf16[272,512]{1,0:T(8,128)(2,1)S(1)}, bf16[272,512]{1,0:T(8,128)(2,1)S(1)}, u32[]{:S(2)}, u32[]{:S(2)}) collective-permute-start(bf16[272,512]{1,0:T(8,128)(2,1)S(1)} %get-tuple-element.75), channel_id=1, source_target_pairs={{0,2},{1,3},{2,0},{3,1},{4,6},{5,7},{6,4},{7,5},{8,10},{9,11},{10,... | collective-permute-start | bytes 835592 | tf_op jit(solution)/shard_map/ppermute | solution.py:425
  20.2 13.6 %collective-permute-start.5 = (bf16[144,512]{1,0:T(8,128)(2,1)S(1)}, bf16[144,512]{1,0:T(8,128)(2,1)S(1)}, u32[]{:S(2)}, u32[]{:S(2)}) collective-permute-start(bf16[144,512]{1,0:T(8,128)(2,1)S(1)} %get-tuple-element.62.refs_0_), channel_id=1, source_target_pairs={{0,8},{1,9},{2,10},{3,11},{4,12},{5,13},{6,14},{7,15},{8,0},{9,1},... | collective-permute-start | bytes 442376 | tf_op jit(solution)/shard_map/ppermute | solution.py:425
  26.1 8.8 %collective-permute-start.11 = (bf16[272,512]{1,0:T(8,128)(2,1)S(1)}, bf16[272,512]{1,0:T(8,128)(2,1)S(1)}, u32[]{:S(2)}, u32[]{:S(2)}) collective-permute-start(bf16[272,512]{1,0:T(8,128)(2,1)S(1)} %collective-permute-done.6.refs_1_.refs_4_), channel_id=1, source_target_pairs={{0,1},{1,0},{2,3},{3,2},{4,5},{5,4},{6,7},{7,6},{8,9},{9,8},{10,11... | collective-permute-start | bytes 835592 | tf_op jit(solution)/shard_map/ppermute | solution.py:425
  29.6 9.8 %collective-permute-start.13 = (bf16[272,512]{1,0:T(8,128)(2,1)S(1)}, bf16[272,512]{1,0:T(8,128)(2,1)S(1)}, u32[]{:S(2)}, u32[]{:S(2)}) collective-permute-start(bf16[272,512]{1,0:T(8,128)(2,1)S(1)} %pick.1), channel_id=1, source_target_pairs={{0,2},{1,3},{2,0},{3,1},{4,6},{5,7},{6,4},{7,5},{8,10},{9,11},{10,... | collective-permute-start | bytes 835592 | tf_op jit(solution)/shard_map/ppermute | solution.py:425
  30.7 4.2 %collective-permute-start.10 = (bf16[272,512]{1,0:T(8,128)(2,1)S(1)}, bf16[272,512]{1,0:T(8,128)(2,1)S(1)}, u32[]{:S(2)}, u32[]{:S(2)}) collective-permute-start(bf16[272,512]{1,0:T(8,128)(2,1)S(1)} %collective-permute-done.9.refs_2_), channel_id=1, source_target_pairs={{0,1},{1,0},{2,3},{3,2},{4,5},{5,4},{6,7},{7,6},{8,9},{9,8},{10,11... | collective-permute-start | bytes 835592 | tf_op jit(solution)/shard_map/ppermute | solution.py:425
  33.9 6.8 %collective-permute-start.8 = (bf16[128,512]{1,0:T(8,128)(2,1)S(1)}, bf16[128,512]{1,0:T(8,128)(2,1)S(1)}, u32[]{:S(2)}, u32[]{:S(2)}) collective-permute-start(bf16[128,512]{1,0:T(8,128)(2,1)S(1)} %get-tuple-element.73), channel_id=1, source_target_pairs={{0,2},{1,3},{2,0},{3,1},{4,6},{5,7},{6,4},{7,5},{8,10},{9,11},{10,... | collective-permute-start | bytes 393224 | tf_op jit(solution)/shard_map/ppermute | solution.py:425
  39.4 3.1 %collective-permute-start.14 = (bf16[272,512]{1,0:T(8,128)(2,1)S(1)}, bf16[272,512]{1,0:T(8,128)(2,1)S(1)}, u32[]{:S(2)}, u32[]{:S(2)}) collective-permute-start(bf16[272,512]{1,0:T(8,128)(2,1)S(1)} %collective-permute-done.13.refs_2_), channel_id=1, source_target_pairs={{0,1},{1,0},{2,3},{3,2},{4,5},{5,4},{6,7},{7,6},{8,9},{9,8},{10,11... | collective-permute-start | bytes 835592 | tf_op jit(solution)/shard_map/ppermute | solution.py:425
  41.6 4.9 %collective-permute-start.12 = (bf16[128,1024]{1,0:T(8,128)(2,1)S(1)}, bf16[128,1024]{1,0:T(8,128)(2,1)S(1)}, u32[]{:S(2)}, u32[]{:S(2)}) collective-permute-start(bf16[128,1024]{1,0:T(8,128)(2,1)S(1)} %get-tuple-element.82), channel_id=1, source_target_pairs={{0,1},{1,0},{2,3},{3,2},{4,5},{5,4},{6,7},{7,6},{8,9},{9,8},{10,11... | collective-permute-start | bytes 786440 | tf_op jit(solution)/shard_map/ppermute | solution.py:425

commit v6 on v5

--- a/solution.py
+++ b/solution.py
@@ -34,7 +34,8 @@
     return pl.ds(pl.multiple_of(number * width, width), width)
 
 
-def call(kernel, name, micros, args, outs, scratch=(), stay=False, mib=8):
+def call(kernel, name, micros, args, outs, scratch=(), stay=False, mib=8, leaves=False):
+    out_spec = pl.BlockSpec(memory_space=pltpu.HBM) if leaves else IN_VMEM
     spec = pl.BlockSpec(memory_space=pltpu.HBM) if stay else IN_VMEM
 
     def placed(*refs):
@@ -46,7 +47,7 @@
         name=name,
         out_shape=outs,
         in_specs=[spec] * len(args),
-        out_specs=jax.tree.map(lambda _: IN_VMEM, outs),
+        out_specs=jax.tree.map(lambda _: out_spec, outs),
         scratch_shapes=list(scratch),
         cost_estimate=pl.CostEstimate(
             flops=int(micros * 1.15e9), bytes_accessed=0, transcendentals=0
@@ -116,86 +117,149 @@
     else:
         acc_out, peak_out, sum_out = refs[at : at + 3]
         at += 3
-    k_all, v_all, bias = refs[at : at + 3]
+    bias = refs[at]
     core = place[0]
     chip = place[3]
-    mine = doc_ref[...]
-    i = lax.broadcasted_iota(jnp.int32, (rows, rows), 0)
-    j = lax.broadcasted_iota(jnp.int32, (rows, rows), 1)
-    for n, (behind, other) in enumerate(kinds):
-        theirs = pieces[n][2 * rows : 2 * rows + 16, 0:rows].astype(F32)[0:1]
-        if behind == 0 and not other:
-            ok = j <= i
-        elif behind == 0:
-            ok = j < rows * core
-        elif behind == 4 and not other:
-            ok = j > i + jnp.where(chip >= behind, 0, rows)
-        elif behind == 4:
-            ok = j < jnp.where((chip >= behind) & (core == 0), rows, 0)
-        else:
-            ok = j < jnp.where(chip >= behind, rows, 0)
-        bias[:, n * rows : (n + 1) * rows] = jnp.where((theirs == mine) & ok, 0.0, FAR)
-    v_all[:, HEAD:] = jnp.ones((count * rows, HEAD), BF16)
     group = q_ref.shape[2] // HEAD // KV_HEADS
-
-    def one(head, _):
-        here = lanes(head, HEAD)
-        for n in range(count):
-            k_all[n * rows : (n + 1) * rows, :] = pieces[n][0:rows, here]
-            v_all[n * rows : (n + 1) * rows, 0:HEAD] = pieces[n][rows : 2 * rows, here]
-        for layer in range(2):
-            for r in range(group):
-                cols = lanes(head * group + r, HEAD)
-                scores = nt_dot(q_ref[layer, :, cols], k_all[...]) * SCALE + bias[...]
+    if last:
+        final_ref = out_ref
+        out_ref, sems = refs[at + 1 :]
+
+    def leave(head):
+        cols = slice(head * group * HEAD, (head + 1) * group * HEAD)
+        return pltpu.make_async_copy(
+            out_ref.at[:, :, cols], final_ref.at[:, :, cols], sems.at[head]
+        )
+
+    def over_heads(body):
+        for head in range(KV_HEADS):
+            tiles = [
+                (layer, slice((head * group + r) * HEAD, (head * group + r + 1) * HEAD))
+                for layer in range(2)
+                for r in range(group)
+            ]
+            body(head, [tiles[n : n + 2] for n in range(0, len(tiles), 2)])
+            if last:
+                leave(head).start()
+        if last:
+            for head in range(KV_HEADS):
+                leave(head).wait()
+
+    def stack(ref, pair):
+        return jnp.concatenate([ref[layer, :, cols] for layer, cols in pair], axis=0)
+
+    def unstack(ref, pair, value):
+        for n, (layer, cols) in enumerate(pair):
+            ref[layer, :, cols] = value[n * rows : (n + 1) * rows]
+
+    def visit(here):
+        mine = doc_ref[...]
+        i = lax.broadcasted_iota(jnp.int32, (rows, rows), 0)
+        j = lax.broadcasted_iota(jnp.int32, (rows, rows), 1)
+        for n, (behind, other) in enumerate(kinds[:here]):
+            theirs = pieces[n][2 * rows : 2 * rows + 16, 0:rows].astype(F32)[0:1]
+            ok = theirs == mine
+            if behind == 0 and not other:
+                ok = ok & (j <= i)
+            elif behind == 0:
+                ok = ok & (j < rows * core)
+            elif behind == 4 and not other:
+                ok = ok & (j > i)
+            elif behind == 4:
+                ok = ok & (j < rows * (1 - core))
+            bias[:, n * rows : (n + 1) * rows] = jnp.where(ok, 0.0, FAR)
+        span = slice(0, here * rows)
+        ones = jnp.ones((rows, HEAD), BF16)
+
+        def body(head, pairs):
+            cols = slice(head * HEAD, (head + 1) * HEAD)
+            keys = jnp.concatenate([piece[0:rows, cols] for piece in pieces[:here]], axis=0)
+            values = jnp.concatenate(
+                [
+                    jnp.concatenate([piece[rows : 2 * rows, cols], ones], axis=1)
+                    for piece in pieces[:here]
+                ],
+                axis=0,
+            )
+            for pair in pairs:
+                scores = nt_dot(stack(q_ref, pair), keys) * SCALE
+                scores = scores + jnp.concatenate([bias[:, span]] * 2, axis=0)
                 peak = jnp.max(scores, axis=1, keepdims=True)
                 if first:
                     probs = jnp.exp2(scores - peak)
                 else:
-                    old = peak_in[layer, :, cols]
+                    old = stack(peak_in, pair)
                     peak = jnp.maximum(old, peak)
                     fade = jnp.exp2(old - peak)
                     probs = jnp.concatenate(
                         [
                             jnp.exp2(scores[:, n * rows : (n + 1) * rows] - peak)
-                            for n in range(count)
+                            for n in range(here)
                         ],
                         axis=1,
                     )
-                both = jnp.dot(probs.astype(BF16), v_all[...], preferred_element_type=F32)
+                both = jnp.dot(probs.astype(BF16), values, preferred_element_type=F32)
                 acc = both[:, :HEAD]
                 total = both[:, HEAD:]
                 if not first:
-                    acc = acc + fade * acc_in[layer, :, cols]
-                    total = total + fade * sum_in[layer, :, cols]
+                    acc = acc + fade * stack(acc_in, pair)
+                    total = total + fade * stack(sum_in, pair)
                 if last:
-                    out_ref[layer, :, cols] = (acc / total).astype(BF16)
+                    unstack(out_ref, pair, (acc / total).astype(BF16))
                 else:
-                    acc_out[layer, :, cols] = acc
-                    sum_out[layer, :, cols] = total
-                    peak_out[layer, :, cols] = jnp.broadcast_to(peak, (rows, HEAD))
-        return _
-
-    lax.fori_loop(0, KV_HEADS, one, 0)
+                    unstack(acc_out, pair, acc)
+                    unstack(sum_out, pair, total)
+                    unstack(peak_out, pair, jnp.broadcast_to(peak, acc.shape))
+
+        over_heads(body)
+
+    def skip():
+        def body(head, pairs):
+            for pair in pairs:
+                for layer, cols in pair:
+                    out_ref[layer, :, cols] = (
+                        acc_in[layer, :, cols] / sum_in[layer, :, cols]
+                    ).astype(BF16)
+
+        if last:
+            over_heads(body)
+        else:
+            acc_out[...] = acc_in[...]
+            sum_out[...] = sum_in[...]
+            peak_out[...] = peak_in[...]
+
+    steps = sorted({behind for behind, _ in kinds})
+    for n, behind in enumerate(steps):
+        here = sum(other <= behind for other, _ in kinds)
+        enough = chip >= behind
+        if n + 1 < len(steps):
+            enough = enough & (chip < steps[n + 1])
+        if behind == 0:
+            visit(here)
+        else:
+            pl.when(enough)(functools.partial(visit, here))
+    if not first:
+        pl.when(chip < steps[0])(skip)
 
 
 def attend(queries, docs, pieces, kinds, carry, last):
     layers, tokens, width = queries.shape
     count = len(kinds)
     partial = shaped(layers, tokens, width, dtype=F32)
+    args = [queries, docs] + list(pieces) + list(carry or ())
+    outs = shaped(layers, tokens, width) if last else (partial,) * 3
     return call(
         functools.partial(attend_kernel, kinds, carry is None, last),
         "attend%d" % kinds[-1][0],
         0.5 + 1.05 * count,
-        [queries, docs]
-        + list(pieces)
-        + [pltpu.with_memory_space_constraint(part, pltpu.VMEM) for part in carry or ()],
-        shaped(layers, tokens, width) if last else (partial,) * 3,
+        args,
+        outs,
         [
-            VMEM((count * tokens, HEAD), BF16),
-            VMEM((count * tokens, 2 * HEAD), BF16),
             VMEM((tokens, count * tokens), F32),
-        ],
+        ]
+        + ([VMEM(queries.shape, BF16), pltpu.SemaphoreType.DMA((KV_HEADS,))] if last else []),
         mib=20,
+        leaves=last,
     )
 
 
@@ -320,8 +384,7 @@
         out_ref[...] = high_ref[...]
 
 
-def row_kernel(state, place, tail_ref, y_ref, low_ref, high_ref, span_ref, first_ref, to_y):
-    pick(place, low_ref, high_ref, to_y)
+def row_kernel(state, place, tail_ref, y_ref, span_ref, first_ref):
     first = place[1] == 0
     mine = tail_ref[0:state, :].astype(F32)
     theirs = y_ref[0:state, :].astype(F32)
@@ -426,6 +489,9 @@
     swap_c = lambda i: i ^ 1
     swap_y = lambda i: i ^ 2
     up = lambda n: lambda i: (i + n * ROW) % devices
+    climb = lambda x, n=1: lax.ppermute(
+        x, "seq", [(i, i + n * ROW) for i in range(devices - n * ROW)]
+    )
     kv_width = keys_values.shape[2]
     half = cols // 2
 
@@ -480,24 +546,25 @@
     carry = attend(
         after(queries, tail), docs, [own, partner], ((0, False), (0, True)), None, False
     )
-    tail_y = after(tail_y, carry[0])
-    span, first, to_y = call(
+    tail_y = after(tail_y, carry[1])
+    span, first = call(
         functools.partial(row_kernel, state),
         "row",
         20.0,
-        [tail, tail_y, own, behind2],
-        (shaped(state + LOGS, half),) * 2 + (shaped(2 * tokens + 16, kv_width),),
+        [tail, tail_y],
+        (shaped(state + LOGS, half),) * 2,
     )
     new = send(span, up(1))
     behind2 = after(behind2, span)
-    behind4 = send(behind2, up(1))
+    to_y = call(pick, "pick", 20.0, [own, behind2], shaped(2 * tokens + 16, kv_width))
     behind1 = send(to_y, swap_y)
+    behind4 = send(after(behind2, to_y), up(1))
     behind2c = send(behind2, swap_c)
     mixed = call(
         functools.partial(local_kernel, heads // 2, state),
         "local",
         3.0,
-        [after(blocks, span), early, run, run_t],
+        [after(blocks, to_y), early, run, run_t],
         shaped(2, tokens, cols, dtype=F32),
     )
     new = after(new, mixed)
@@ -516,7 +583,7 @@
             keep, give = out
         else:
             span, before = out
-            new = send(span, up(2 * distance))
+            new = climb(span, 2 * distance)
         if distance == 1:
             carry = attend(
                 after(queries, before),
@@ -526,18 +593,11 @@
                 carry,
                 False,
             )
-            behind4, behind1 = after(behind4, carry[0]), after(behind1, carry[0])
+            behind4, behind1 = after(behind4, carry[1]), after(behind1, carry[1])
             behind1c = send(behind1, swap_c)
+            behind3 = climb(behind1)
             behind4c = send(behind4, swap_c)
-            to_y = call(
-                pick,
-                "pick",
-                20.0,
-                [behind2, behind4],
-                shaped(2 * tokens + 16, kv_width),
-            )
-            behind3 = send(to_y, swap_y)
-            new = after(new, to_y)
+            new = after(new, carry[1])
         distance *= 2
     carry = attend(
         after(queries, give),
@@ -547,9 +607,9 @@
         carry,
         False,
     )
-    behind3 = after(behind3, carry[0])
+    behind3 = after(behind3, carry[1])
     behind3c = send(behind3, swap_c)
-    other_half = after(send(give, swap_y), carry[0])
+    other_half = after(send(give, swap_y), carry[1])
     done, for_c = call(
         functools.partial(finish_kernel, heads // 2, state),
         "finish",

time: 47.4 us -> 41.4 us (0.87)
  the two profiles are of different devices: /device:TPU:1 before, /device:TPU:19 now
where the time goes in v6:
time: 41.4 us; the launch traced here: 41.2 us
  starting transfers between devices  16.7 us (40%)
  Pallas kernels  15.2 us (37%)
  waiting for transfers between devices  8.43 us (20%)
  between operations  0.77 us (2%)
    pallas_call x13, Pallas kernels, call(): pl.pallas_call(placed, name=name, out_shape=outs, in_specs=[spec] * len(a...  15.2 us
    ppermute x13, starting transfers between devices, shards(): lax.ppermute(x, 'seq', [(i, route(i)) for i in range(devices)])  13.5 us
    ppermute x13, waiting for transfers between devices, shards(): lax.ppermute(x, 'seq', [(i, route(i)) for i in range(devices)])  5.56 us
    ppermute x2, starting transfers between devices, shards(): lax.ppermute(x, 'seq', [(i, i + n * ROW) for i in range(devices - n * ROW)])  3.2 us
    ppermute x2, waiting for transfers between devices, shards(): lax.ppermute(x, 'seq', [(i, i + n * ROW) for i in range(devices - n * ROW)])  2.88 us
  transfers between devices with their start and end apart: 15, of which 5 were waited for; matrix products, arithmetic and copies ran while one was open for 0% of the time, Pallas kernels for 31%

profile of v6, /device:TPU:19, one launch (start us, length us, event | category | flops | bytes accessed | tf_op | source)
XLA Modules:
  0.0 41.2 jit_solution(13247575022371248367)
XLA Ops:
  0.6 1.5 %pack.1 = (bf16[272,512]{1,0:T(8,128)(2,1)S(1)}, f32[128,128]{1,0:T(8,128)S(1)}, bf16[128,1408]{1,0:T(8,128)(2,1)S(1)}, bf16[128,1408]{1,0:T(8,128)(2,1)S(1)}, f32[1,128]{1,0:T(1,128)S(1)}) custom-call(bf16[128,2048]{1,0:T(8,128)(2,1)} %refs_0_.1, bf16[128,128]{1,0:T(8,128)(2,1)} %refs_1_.1, bf16[128,128]{1,0:T(8,128)(2,1)} %refs_2_.1, s32[32,128]{1,0:T(8,128)} %bitcast.3, ...), custom_call_target="tpu_custom_call" | custom-call | flops 1724999936 | tf_op jit(solution)/shard_map/pack/pallas_call | solution.py:45
  2.1 0.7 %collective-permute-start = (bf16[128,1408]{1,0:T(8,128)(2,1)S(1)}, bf16[128,1408]{1,0:T(8,128)(2,1)S(1)}, u32[]{:S(2)}, u32[]{:S(2)}) collective-permute-start(bf16[128,1408]{1,0:T(8,128)(2,1)S(1)} %get-tuple-element.46), channel_id=1, source_target_pairs={{0,1},{1,0},{2,3},{3,2},{4,5},{5,4},{6,7},{7,6},{8,9},{9,8},{10,11... | collective-permute-start | bytes 1081352 | tf_op jit(solution)/shard_map/ppermute | solution.py:488
  2.8 0.1 collective-permute-start.3
  2.9 1.3 %collective-permute-start.1 = (bf16[272,512]{1,0:T(8,128)(2,1)S(1)}, bf16[272,512]{1,0:T(8,128)(2,1)S(1)}, u32[]{:S(2)}, u32[]{:S(2)}) collective-permute-start(bf16[272,512]{1,0:T(8,128)(2,1)S(1)} %get-tuple-element.49.refs_2_.refs_0_), channel_id=1, source_target_pairs={{0,4},{1,5},{2,6},{3,7},{4,8},{5,9},{6,10},{7,11},{8,12},{9,13},{1... | collective-permute-start | bytes 835592 | tf_op jit(solution)/shard_map/ppermute | solution.py:488
  4.2 0.0 collective-permute-done.refs_1_
  4.2 0.0 copy-start
  4.2 1.6 %states.1 = (bf16[144,512]{1,0:T(8,128)(2,1)S(1)}, bf16[144,512]{1,0:T(8,128)(2,1)S(1)}, bf16[128,1024]{1,0:T(8,128)(2,1)S(1)}, f32[2,128,128]{2,1,0:T(8,128)S(1...) custom-call(bf16[128,1408]{1,0:T(8,128)(2,1)S(1)} %get-tuple-element.45.refs_0_, ...), custom_call_target="tpu_custom_call" | custom-call | flops 2300000000 | tf_op jit(solution)/shard_map/states/pallas_call | solution.py:45
  5.8 1.3 %collective-permute-start.2 = (bf16[144,512]{1,0:T(8,128)(2,1)S(1)}, bf16[144,512]{1,0:T(8,128)(2,1)S(1)}, u32[]{:S(2)}, u32[]{:S(2)}) collective-permute-start(bf16[144,512]{1,0:T(8,128)(2,1)S(1)} %get-tuple-element.51), channel_id=1, source_target_pairs={{0,2},{1,3},{2,0},{3,1},{4,6},{5,7},{6,4},{7,5},{8,10},{9,11},{10,... | collective-permute-start | bytes 442376 | tf_op jit(solution)/shard_map/ppermute | solution.py:488
  7.2 0.0 collective-permute-done.3.refs_3_
  7.2 0.0 copy-done
  7.2 1.5 %attend0.1 = (f32[2,128,2048]{2,1,0:T(8,128)S(1)}, f32[2,128,2048]{2,1,0:T(8,128)S(1)}, f32[2,128,2048]{2,1,0:T(8,128)S(1)}) custom-call(bf16[2,128,2048]{2,1,0:T(8,128)(2,1)S(1)} %copy-done, f32[128,128]{1,0:T(8,128)S(1)} %get-tuple-element.53.refs_1_, bf16[272,512]{1,0:T(8,128)(2,1)S(1)} %get-tuple-element.49.refs_2_.refs_0_, ...), custom_call_target="tpu_custom_call" | custom-call | flops 2990000128 | tf_op jit(solution)/shard_map/attend0/pallas_call | solution.py:45
  8.7 1.9 %collective-permute-done.2.refs_1_ = bf16[144,512]{1,0:T(8,128)(2,1)S(1)} collective-permute-done((bf16[144,512]{1,0:T(8,128)(2,1)S(1)}, bf16[144,512]{1,0:T(8,128)(2,1)S(1)}, u32[]{:S(2)}, u32[]{:S(2)}) %collective-permute-start.2) | collective-permute-done | bytes 147488 | tf_op jit(solution)/shard_map/ppermute | solution.py:488
  10.6 0.1 row.1
  10.7 1.7 %collective-permute-start.4 = (bf16[144,512]{1,0:T(8,128)(2,1)S(1)}, bf16[144,512]{1,0:T(8,128)(2,1)S(1)}, u32[]{:S(2)}, u32[]{:S(2)}) collective-permute-start(bf16[144,512]{1,0:T(8,128)(2,1)S(1)} %get-tuple-element.56.refs_0_), channel_id=1, source_target_pairs={{0,4},{1,5},{2,6},{3,7},{4,8},{5,9},{6,10},{7,11},{8,12},{9,13},{1... | collective-permute-start | bytes 442376 | tf_op jit(solution)/shard_map/ppermute | solution.py:488
  12.3 0.0 collective-permute-done.1.refs_1_.refs_2_
  12.4 1.5 %collective-permute-start.6 = (bf16[272,512]{1,0:T(8,128)(2,1)S(1)}, bf16[272,512]{1,0:T(8,128)(2,1)S(1)}, u32[]{:S(2)}, u32[]{:S(2)}) collective-permute-start(bf16[272,512]{1,0:T(8,128)(2,1)S(1)} %collective-permute-done.1.refs_1_.refs_2_), channel_id=1, source_target_pairs={{0,1},{1,0},{2,3},{3,2},{4,5},{5,4},{6,7},{7,6},{8,9},{9,8},{10,11... | collective-permute-start | bytes 835592 | tf_op jit(solution)/shard_map/ppermute | solution.py:488
  13.9 1.2 %collective-permute-start.8 = (bf16[272,512]{1,0:T(8,128)(2,1)S(1)}, bf16[272,512]{1,0:T(8,128)(2,1)S(1)}, u32[]{:S(2)}, u32[]{:S(2)}) collective-permute-start(bf16[272,512]{1,0:T(8,128)(2,1)S(1)} %pick.1), channel_id=1, source_target_pairs={{0,2},{1,3},{2,0},{3,1},{4,6},{5,7},{6,4},{7,5},{8,10},{9,11},{10,... | collective-permute-start | bytes 835592 | tf_op jit(solution)/shard_map/ppermute | solution.py:488
  15.2 0.0 collective-permute-start.10
  15.2 1.1 %local.1.refs_0_ = f32[2,128,1024]{2,1,0:T(8,128)S(1)} custom-call(bf16[2,128,1408]{2,1,0:T(8,128)(2,1)S(1)} %get-tuple-element.58.refs_0_.refs_2_, bf16[128,1024]{1,0:T(8,128)(2,1)S(1)} %get-tuple-element.59.refs_1_, f32[2,128,128]{2,1,0:T(8,128)S(1)} %get-tuple-element.60.refs_2_.refs_1_, f32[2,128,128]{2,1,0:T(8,128)S(1)} %get-tuple-element.61.refs_3_), custom_call_target="tpu_custom_call" | custom-call | flops 3449999872 | tf_op jit(solution)/shard_map/local/pallas_call | solution.py:45
  16.3 0.0 collective-permute-done.4.refs_1_
  16.3 0.1 hop1.1
  16.4 1.3 %collective-permute-start.5 = (bf16[144,512]{1,0:T(8,128)(2,1)S(1)}, bf16[144,512]{1,0:T(8,128)(2,1)S(1)}, u32[]{:S(2)}, u32[]{:S(2)}) collective-permute-start(bf16[144,512]{1,0:T(8,128)(2,1)S(1)} %get-tuple-element.63.refs_0_), channel_id=1, source_target_pairs={{0,8},{1,9},{2,10},{3,11},{4,12},{5,13},{6,14},{7,15},{16,24},{17,... | collective-permute-start | bytes 442376 | tf_op jit(solution)/shard_map/ppermute | solution.py:492
  17.7 0.0 collective-permute-done.6.refs_3_
  17.7 1.8 %attend2.1 = (f32[2,128,2048]{2,1,0:T(8,128)S(1)}, f32[2,128,2048]{2,1,0:T(8,128)S(1)}, f32[2,128,2048]{2,1,0:T(8,128)S(1)}) custom-call(bf16[2,128,2048]{2,1,0:T(8,128)(2,1)S(1)} %copy-done, f32[128,128]{1,0:T(8,128)S(1)} %get-tuple-element.53.refs_1_, bf16[272,512]{1,0:T(8,128)(2,1)S(1)} %collective-permute-done.1.refs_1_.refs_2_, ...), custom_call_target="tpu_custom_call" | custom-call | flops 2990000128 | tf_op jit(solution)/shard_map/attend2/pallas_call | solution.py:45
  19.5 2.7 %collective-permute-done.8.refs_2_ = bf16[272,512]{1,0:T(8,128)(2,1)S(1)} collective-permute-done((bf16[272,512]{1,0:T(8,128)(2,1)S(1)}, bf16[272,512]{1,0:T(8,128)(2,1)S(1)}, u32[]{:S(2)}, u32[]{:S(2)}) %collective-permute-start.8) | collective-permute-done | bytes 278560 | tf_op jit(solution)/shard_map/ppermute | solution.py:488
  22.2 0.8 %collective-permute-start.9 = (bf16[272,512]{1,0:T(8,128)(2,1)S(1)}, bf16[272,512]{1,0:T(8,128)(2,1)S(1)}, u32[]{:S(2)}, u32[]{:S(2)}) collective-permute-start(bf16[272,512]{1,0:T(8,128)(2,1)S(1)} %collective-permute-done.8.refs_2_), channel_id=1, source_target_pairs={{0,1},{1,0},{2,3},{3,2},{4,5},{5,4},{6,7},{7,6},{8,9},{9,8},{10,11... | collective-permute-start | bytes 835592 | tf_op jit(solution)/shard_map/ppermute | solution.py:488
  23.0 1.9 %collective-permute-start.13 = (bf16[272,512]{1,0:T(8,128)(2,1)S(1)}, bf16[272,512]{1,0:T(8,128)(2,1)S(1)}, u32[]{:S(2)}, u32[]{:S(2)}) collective-permute-start(bf16[272,512]{1,0:T(8,128)(2,1)S(1)} %collective-permute-done.8.refs_2_), channel_id=1, source_target_pairs={{0,4},{1,5},{2,6},{3,7},{4,8},{5,9},{6,10},{7,11},{8,12},{9,13},{1... | collective-permute-start | bytes 835592 | tf_op jit(solution)/shard_map/ppermute | solution.py:492
  24.9 0.0 collective-permute-done.10.refs_4_
  24.9 3.2 %collective-permute-start.11 = (bf16[272,512]{1,0:T(8,128)(2,1)S(1)}, bf16[272,512]{1,0:T(8,128)(2,1)S(1)}, u32[]{:S(2)}, u32[]{:S(2)}) collective-permute-start(bf16[272,512]{1,0:T(8,128)(2,1)S(1)} %collective-permute-done.10.refs_4_), channel_id=1, source_target_pairs={{0,1},{1,0},{2,3},{3,2},{4,5},{5,4},{6,7},{7,6},{8,9},{9,8},{10,11... | collective-permute-start | bytes 835592 | tf_op jit(solution)/shard_map/ppermute | solution.py:488
  28.2 0.0 collective-permute-done.5.refs_2_
  28.2 0.1 hop2.1
  28.3 0.3 collective-permute-start.7
  28.6 0.0 collective-permute-done.9.refs_3_
  28.6 0.8 %collective-permute-done.11.refs_5_ = bf16[272,512]{1,0:T(8,128)(2,1)S(1)} collective-permute-done((bf16[272,512]{1,0:T(8,128)(2,1)S(1)}, bf16[272,512]{1,0:T(8,128)(2,1)S(1)}, u32[]{:S(2)}, u32[]{:S(2)}) %collective-permute-start.11) | collective-permute-done | bytes 278560 | tf_op jit(solution)/shard_map/ppermute | solution.py:488
  29.4 3.2 %attend4.1 = (f32[2,128,2048]{2,1,0:T(8,128)S(1)}, f32[2,128,2048]{2,1,0:T(8,128)S(1)}, f32[2,128,2048]{2,1,0:T(8,128)S(1)}) custom-call(bf16[2,128,2048]{2,1,0:T(8,128)(2,1)S(1)} %copy-done, f32[128,128]{1,0:T(8,128)S(1)} %get-tuple-element.53.refs_1_, bf16[272,512]{1,0:T(8,128)(2,1)S(1)} %collective-permute-done.8.refs_2_, ...), custom_call_target="tpu_custom_call" | custom-call | flops 5405000192 | tf_op jit(solution)/shard_map/attend4/pallas_call | solution.py:45
  32.5 2.9 %collective-permute-done.13.refs_2_ = bf16[272,512]{1,0:T(8,128)(2,1)S(1)} collective-permute-done((bf16[272,512]{1,0:T(8,128)(2,1)S(1)}, bf16[272,512]{1,0:T(8,128)(2,1)S(1)}, u32[]{:S(2)}, u32[]{:S(2)}) %collective-permute-start.13) | collective-permute-done | bytes 278560 | tf_op jit(solution)/shard_map/ppermute | solution.py:492
  35.4 1.2 %collective-permute-start.14 = (bf16[272,512]{1,0:T(8,128)(2,1)S(1)}, bf16[272,512]{1,0:T(8,128)(2,1)S(1)}, u32[]{:S(2)}, u32[]{:S(2)}) collective-permute-start(bf16[272,512]{1,0:T(8,128)(2,1)S(1)} %collective-permute-done.13.refs_2_), channel_id=1, source_target_pairs={{0,1},{1,0},{2,3},{3,2},{4,5},{5,4},{6,7},{7,6},{8,9},{9,8},{10,11... | collective-permute-start | bytes 835592 | tf_op jit(solution)/shard_map/ppermute | solution.py:488
  36.6 0.0 collective-permute-done.7.refs_4_
  36.6 0.9 %finish.1 = (bf16[128,1024]{1,0:T(8,128)(2,1)S(1)}, bf16[128,1024]{1,0:T(8,128)(2,1)S(1)}) custom-call(f32[2,128,1024]{2,1,0:T(8,128)S(1)} %local.1.refs_0_, f32[2,128,128]{2,1,0:T(8,128)S(1)} %get-tuple-element.60.refs_2_.refs_1_, bf16[2,128,1408]{2,1,0:T(8,128)(2,1)S(1)} %get-tuple-element.58.refs_0_.refs_2_, ...), custom_call_target="tpu_custom_call" | custom-call | flops 1955000064 | tf_op jit(solution)/shard_map/finish/pallas_call | solution.py:45
  37.5 0.1 collective-permute-start.12
  37.6 0.2 collective-permute-done.14.refs_3_
  37.8 2.6 %attend3.1 = bf16[2,128,2048]{2,1,0:T(8,128)(2,1)} custom-call(bf16[2,128,2048]{2,1,0:T(8,128)(2,1)S(1)} %copy-done, f32[128,128]{1,0:T(8,128)S(1)} %get-tuple-element.53.refs_1_, bf16[272,512]{1,0:T(8,128)(2,1)S(1)} %collective-permute-done.13.refs_2_, bf16[272,512]{1,0:T(8,128)(2,1)S(1)} %collective-permute-done.14.refs_3_, ...), custom_call_target="tpu_custom_call" | custom-call | flops 2990000128 | tf_op jit(solution)/shard_map/attend3/pallas_call | solution.py:45
  40.3 0.0 collective-permute-done.12.refs_1_
  40.3 0.8 %collect.1 = bf16[128,2048]{1,0:T(8,128)(2,1)} custom-call(bf16[128,1024]{1,0:T(8,128)(2,1)S(1)} %get-tuple-element.81.refs_0_, bf16[128,1024]{1,0:T(8,128)(2,1)S(1)} %collective-permute-done.12.refs_1_), custom_call_target="tpu_custom_call" | custom-call | flops 920000000 | tf_op jit(solution)/shard_map/collect/pallas_call | solution.py:45
  (1 shorter events, 0.0 us)
Async XLA Ops:
  2.1 2.1 %collective-permute-start = (bf16[128,1408]{1,0:T(8,128)(2,1)S(1)}, bf16[128,1408]{1,0:T(8,128)(2,1)S(1)}, u32[]{:S(2)}, u32[]{:S(2)}) collective-permute-start(bf16[128,1408]{1,0:T(8,128)(2,1)S(1)} %get-tuple-element.46), channel_id=1, source_target_pairs={{0,1},{1,0},{2,3},{3,2},{4,5},{5,4},{6,7},{7,6},{8,9},{9,8},{10,11... | collective-permute-start | bytes 1081352 | tf_op jit(solution)/shard_map/ppermute | solution.py:488
  2.8 4.3 %collective-permute-start.3 = (bf16[272,512]{1,0:T(8,128)(2,1)S(1)}, bf16[272,512]{1,0:T(8,128)(2,1)S(1)}, u32[]{:S(2)}, u32[]{:S(2)}) collective-permute-start(bf16[272,512]{1,0:T(8,128)(2,1)S(1)} %get-tuple-element.49.refs_2_.refs_0_), channel_id=1, source_target_pairs={{0,1},{1,0},{2,3},{3,2},{4,5},{5,4},{6,7},{7,6},{8,9},{9,8},{10,11... | collective-permute-start | bytes 835592 | tf_op jit(solution)/shard_map/ppermute | solution.py:488
  2.9 9.4 %collective-permute-start.1 = (bf16[272,512]{1,0:T(8,128)(2,1)S(1)}, bf16[272,512]{1,0:T(8,128)(2,1)S(1)}, u32[]{:S(2)}, u32[]{:S(2)}) collective-permute-start(bf16[272,512]{1,0:T(8,128)(2,1)S(1)} %get-tuple-element.49.refs_2_.refs_0_), channel_id=1, source_target_pairs={{0,4},{1,5},{2,6},{3,7},{4,8},{5,9},{6,10},{7,11},{8,12},{9,13},{1... | collective-permute-start | bytes 835592 | tf_op jit(solution)/shard_map/ppermute | solution.py:488
  4.2 2.9 %copy-start = (bf16[2,128,2048]{2,1,0:T(8,128)(2,1)S(1)}, bf16[2,128,2048]{2,1,0:T(8,128)(2,1)}, u32[]{:S(2)}) copy-start(bf16[2,128,2048]{2,1,0:T(8,128)(2,1)} %refs_0_.5) | copy-start | bytes 3145732
  5.8 4.7 %collective-permute-start.2 = (bf16[144,512]{1,0:T(8,128)(2,1)S(1)}, bf16[144,512]{1,0:T(8,128)(2,1)S(1)}, u32[]{:S(2)}, u32[]{:S(2)}) collective-permute-start(bf16[144,512]{1,0:T(8,128)(2,1)S(1)} %get-tuple-element.51), channel_id=1, source_target_pairs={{0,2},{1,3},{2,0},{3,1},{4,6},{5,7},{6,4},{7,5},{8,10},{9,11},{10,... | collective-permute-start | bytes 442376 | tf_op jit(solution)/shard_map/ppermute | solution.py:488
  10.7 5.6 %collective-permute-start.4 = (bf16[144,512]{1,0:T(8,128)(2,1)S(1)}, bf16[144,512]{1,0:T(8,128)(2,1)S(1)}, u32[]{:S(2)}, u32[]{:S(2)}) collective-permute-start(bf16[144,512]{1,0:T(8,128)(2,1)S(1)} %get-tuple-element.56.refs_0_), channel_id=1, source_target_pairs={{0,4},{1,5},{2,6},{3,7},{4,8},{5,9},{6,10},{7,11},{8,12},{9,13},{1... | collective-permute-start | bytes 442376 | tf_op jit(solution)/shard_map/ppermute | solution.py:488
  12.4 5.3 %collective-permute-start.6 = (bf16[272,512]{1,0:T(8,128)(2,1)S(1)}, bf16[272,512]{1,0:T(8,128)(2,1)S(1)}, u32[]{:S(2)}, u32[]{:S(2)}) collective-permute-start(bf16[272,512]{1,0:T(8,128)(2,1)S(1)} %collective-permute-done.1.refs_1_.refs_2_), channel_id=1, source_target_pairs={{0,1},{1,0},{2,3},{3,2},{4,5},{5,4},{6,7},{7,6},{8,9},{9,8},{10,11... | collective-permute-start | bytes 835592 | tf_op jit(solution)/shard_map/ppermute | solution.py:488
  13.9 8.2 %collective-permute-start.8 = (bf16[272,512]{1,0:T(8,128)(2,1)S(1)}, bf16[272,512]{1,0:T(8,128)(2,1)S(1)}, u32[]{:S(2)}, u32[]{:S(2)}) collective-permute-start(bf16[272,512]{1,0:T(8,128)(2,1)S(1)} %pick.1), channel_id=1, source_target_pairs={{0,2},{1,3},{2,0},{3,1},{4,6},{5,7},{6,4},{7,5},{8,10},{9,11},{10,... | collective-permute-start | bytes 835592 | tf_op jit(solution)/shard_map/ppermute | solution.py:488
  15.2 9.8 %collective-permute-start.10 = (bf16[272,512]{1,0:T(8,128)(2,1)S(1)}, bf16[272,512]{1,0:T(8,128)(2,1)S(1)}, u32[]{:S(2)}, u32[]{:S(2)}) collective-permute-start(bf16[272,512]{1,0:T(8,128)(2,1)S(1)} %collective-permute-done.1.refs_1_.refs_2_), channel_id=1, source_target_pairs={{0,4},{1,5},{2,6},{3,7},{4,8},{5,9},{6,10},{7,11},{8,12},{9,13},{1... | collective-permute-start | bytes 835592 | tf_op jit(solution)/shard_map/ppermute | solution.py:488
  16.4 11.8 %collective-permute-start.5 = (bf16[144,512]{1,0:T(8,128)(2,1)S(1)}, bf16[144,512]{1,0:T(8,128)(2,1)S(1)}, u32[]{:S(2)}, u32[]{:S(2)}) collective-permute-start(bf16[144,512]{1,0:T(8,128)(2,1)S(1)} %get-tuple-element.63.refs_0_), channel_id=1, source_target_pairs={{0,8},{1,9},{2,10},{3,11},{4,12},{5,13},{6,14},{7,15},{16,24},{17,... | collective-permute-start | bytes 442376 | tf_op jit(solution)/shard_map/ppermute | solution.py:492
  22.2 6.4 %collective-permute-start.9 = (bf16[272,512]{1,0:T(8,128)(2,1)S(1)}, bf16[272,512]{1,0:T(8,128)(2,1)S(1)}, u32[]{:S(2)}, u32[]{:S(2)}) collective-permute-start(bf16[272,512]{1,0:T(8,128)(2,1)S(1)} %collective-permute-done.8.refs_2_), channel_id=1, source_target_pairs={{0,1},{1,0},{2,3},{3,2},{4,5},{5,4},{6,7},{7,6},{8,9},{9,8},{10,11... | collective-permute-start | bytes 835592 | tf_op jit(solution)/shard_map/ppermute | solution.py:488
  23.0 12.4 %collective-permute-start.13 = (bf16[272,512]{1,0:T(8,128)(2,1)S(1)}, bf16[272,512]{1,0:T(8,128)(2,1)S(1)}, u32[]{:S(2)}, u32[]{:S(2)}) collective-permute-start(bf16[272,512]{1,0:T(8,128)(2,1)S(1)} %collective-permute-done.8.refs_2_), channel_id=1, source_target_pairs={{0,4},{1,5},{2,6},{3,7},{4,8},{5,9},{6,10},{7,11},{8,12},{9,13},{1... | collective-permute-start | bytes 835592 | tf_op jit(solution)/shard_map/ppermute | solution.py:492
  24.9 4.4 %collective-permute-start.11 = (bf16[272,512]{1,0:T(8,128)(2,1)S(1)}, bf16[272,512]{1,0:T(8,128)(2,1)S(1)}, u32[]{:S(2)}, u32[]{:S(2)}) collective-permute-start(bf16[272,512]{1,0:T(8,128)(2,1)S(1)} %collective-permute-done.10.refs_4_), channel_id=1, source_target_pairs={{0,1},{1,0},{2,3},{3,2},{4,5},{5,4},{6,7},{7,6},{8,9},{9,8},{10,11... | collective-permute-start | bytes 835592 | tf_op jit(solution)/shard_map/ppermute | solution.py:488
  28.3 8.3 %collective-permute-start.7 = (bf16[128,512]{1,0:T(8,128)(2,1)S(1)}, bf16[128,512]{1,0:T(8,128)(2,1)S(1)}, u32[]{:S(2)}, u32[]{:S(2)}) collective-permute-start(bf16[128,512]{1,0:T(8,128)(2,1)S(1)} %get-tuple-element.72), channel_id=1, source_target_pairs={{0,2},{1,3},{2,0},{3,1},{4,6},{5,7},{6,4},{7,5},{8,10},{9,11},{10,... | collective-permute-start | bytes 393224 | tf_op jit(solution)/shard_map/ppermute | solution.py:488
  35.4 2.4 %collective-permute-start.14 = (bf16[272,512]{1,0:T(8,128)(2,1)S(1)}, bf16[272,512]{1,0:T(8,128)(2,1)S(1)}, u32[]{:S(2)}, u32[]{:S(2)}) collective-permute-start(bf16[272,512]{1,0:T(8,128)(2,1)S(1)} %collective-permute-done.13.refs_2_), channel_id=1, source_target_pairs={{0,1},{1,0},{2,3},{3,2},{4,5},{5,4},{6,7},{7,6},{8,9},{9,8},{10,11... | collective-permute-start | bytes 835592 | tf_op jit(solution)/shard_map/ppermute | solution.py:488
  37.5 2.8 %collective-permute-start.12 = (bf16[128,1024]{1,0:T(8,128)(2,1)S(1)}, bf16[128,1024]{1,0:T(8,128)(2,1)S(1)}, u32[]{:S(2)}, u32[]{:S(2)}) collective-permute-start(bf16[128,1024]{1,0:T(8,128)(2,1)S(1)} %get-tuple-element.82), channel_id=1, source_target_pairs={{0,1},{1,0},{2,3},{3,2},{4,5},{5,4},{6,7},{7,6},{8,9},{9,8},{10,11... | collective-permute-start | bytes 786440 | tf_op jit(solution)/shard_map/ppermute | solution.py:488

commit v7 on v6

--- a/solution.py
+++ b/solution.py
@@ -546,7 +546,14 @@
     carry = attend(
         after(queries, tail), docs, [own, partner], ((0, False), (0, True)), None, False
     )
-    tail_y = after(tail_y, carry[1])
+    mixed = call(
+        functools.partial(local_kernel, heads // 2, state),
+        "local",
+        0.01,
+        [after(blocks, carry[1]), early, run, run_t],
+        shaped(2, tokens, cols, dtype=F32),
+    )
+    tail_y = after(tail_y, mixed)
     span, first = call(
         functools.partial(row_kernel, state),
         "row",
@@ -560,14 +567,6 @@
     behind1 = send(to_y, swap_y)
     behind4 = send(after(behind2, to_y), up(1))
     behind2c = send(behind2, swap_c)
-    mixed = call(
-        functools.partial(local_kernel, heads // 2, state),
-        "local",
-        3.0,
-        [after(blocks, to_y), early, run, run_t],
-        shaped(2, tokens, cols, dtype=F32),
-    )
-    new = after(new, mixed)
     before = None
     distance = 1
     while distance < rows:
@@ -595,7 +594,7 @@
             )
             behind4, behind1 = after(behind4, carry[1]), after(behind1, carry[1])
             behind1c = send(behind1, swap_c)
-            behind3 = climb(behind1)
+            behind3 = send(behind1, up(1))
             behind4c = send(behind4, swap_c)
             new = after(new, carry[1])
         distance *= 2

time: 41.4 us -> 41.3 us (level)
  the two profiles are of different devices: /device:TPU:19 before, /device:TPU:17 now
where the time goes in v7:
time: 41.3 us; the launch traced here: 41.2 us
  starting transfers between devices  16.4 us (40%)
  Pallas kernels  15.4 us (37%)
  waiting for transfers between devices  8.67 us (21%)
  between operations  0.75 us (2%)
    pallas_call x13, Pallas kernels, call(): pl.pallas_call(placed, name=name, out_shape=outs, in_specs=[spec] * len(a...  15.4 us
    ppermute x14, starting transfers between devices, shards(): lax.ppermute(x, 'seq', [(i, route(i)) for i in range(devices)])  15.1 us
    ppermute x14, waiting for transfers between devices, shards(): lax.ppermute(x, 'seq', [(i, route(i)) for i in range(devices)])  8.67 us
    ppermute x1, starting transfers between devices, shards(): lax.ppermute(x, 'seq', [(i, i + n * ROW) for i in range(devices - n * ROW)])  1.29 us
  transfers between devices with their start and end apart: 15, of which 6 were waited for; matrix products, arithmetic and copies ran while one was open for 0% of the time, Pallas kernels for 32%

profile of v7, /device:TPU:17, one launch (start us, length us, event | category | flops | bytes accessed | tf_op | source)
XLA Modules:
  0.0 41.2 jit_solution(18363847748639229938)
XLA Ops:
  0.6 1.5 %pack.1 = (bf16[272,512]{1,0:T(8,128)(2,1)S(1)}, f32[128,128]{1,0:T(8,128)S(1)}, bf16[128,1408]{1,0:T(8,128)(2,1)S(1)}, bf16[128,1408]{1,0:T(8,128)(2,1)S(1)}, f32[1,128]{1,0:T(1,128)S(1)}) custom-call(bf16[128,2048]{1,0:T(8,128)(2,1)} %refs_0_.1, bf16[128,128]{1,0:T(8,128)(2,1)} %refs_1_.1, bf16[128,128]{1,0:T(8,128)(2,1)} %refs_2_.1, s32[32,128]{1,0:T(8,128)} %bitcast.3, ...), custom_call_target="tpu_custom_call" | custom-call | flops 1724999936 | tf_op jit(solution)/shard_map/pack/pallas_call | solution.py:45
  2.1 0.7 %collective-permute-start = (bf16[128,1408]{1,0:T(8,128)(2,1)S(1)}, bf16[128,1408]{1,0:T(8,128)(2,1)S(1)}, u32[]{:S(2)}, u32[]{:S(2)}) collective-permute-start(bf16[128,1408]{1,0:T(8,128)(2,1)S(1)} %get-tuple-element.45), channel_id=1, source_target_pairs={{0,1},{1,0},{2,3},{3,2},{4,5},{5,4},{6,7},{7,6},{8,9},{9,8},{10,11... | collective-permute-start | bytes 1081352 | tf_op jit(solution)/shard_map/ppermute | solution.py:488
  2.8 0.1 collective-permute-start.1
  2.9 1.3 %collective-permute-start.5 = (bf16[272,512]{1,0:T(8,128)(2,1)S(1)}, bf16[272,512]{1,0:T(8,128)(2,1)S(1)}, u32[]{:S(2)}, u32[]{:S(2)}) collective-permute-start(bf16[272,512]{1,0:T(8,128)(2,1)S(1)} %get-tuple-element.51.refs_2_.refs_0_), channel_id=1, source_target_pairs={{0,4},{1,5},{2,6},{3,7},{4,8},{5,9},{6,10},{7,11},{8,12},{9,13},{1... | collective-permute-start | bytes 835592 | tf_op jit(solution)/shard_map/ppermute | solution.py:488
  4.2 0.0 collective-permute-done.refs_1_
  4.2 0.0 copy-start
  4.2 1.6 %states.1 = (bf16[144,512]{1,0:T(8,128)(2,1)S(1)}, bf16[144,512]{1,0:T(8,128)(2,1)S(1)}, bf16[128,1024]{1,0:T(8,128)(2,1)S(1)}, f32[2,128,128]{2,1,0:T(8,128)S(1...) custom-call(bf16[128,1408]{1,0:T(8,128)(2,1)S(1)} %get-tuple-element.44.refs_0_, ...), custom_call_target="tpu_custom_call" | custom-call | flops 2300000000 | tf_op jit(solution)/shard_map/states/pallas_call | solution.py:45
  5.8 1.3 %collective-permute-start.2 = (bf16[144,512]{1,0:T(8,128)(2,1)S(1)}, bf16[144,512]{1,0:T(8,128)(2,1)S(1)}, u32[]{:S(2)}, u32[]{:S(2)}) collective-permute-start(bf16[144,512]{1,0:T(8,128)(2,1)S(1)} %get-tuple-element.57), channel_id=1, source_target_pairs={{0,2},{1,3},{2,0},{3,1},{4,6},{5,7},{6,4},{7,5},{8,10},{9,11},{10,... | collective-permute-start | bytes 442376 | tf_op jit(solution)/shard_map/ppermute | solution.py:488
  7.1 0.0 collective-permute-done.1.refs_3_
  7.1 0.0 copy-done
  7.2 1.5 %attend0.1 = (f32[2,128,2048]{2,1,0:T(8,128)S(1)}, f32[2,128,2048]{2,1,0:T(8,128)S(1)}, f32[2,128,2048]{2,1,0:T(8,128)S(1)}) custom-call(bf16[2,128,2048]{2,1,0:T(8,128)(2,1)S(1)} %copy-done, f32[128,128]{1,0:T(8,128)S(1)} %get-tuple-element.50.refs_1_, bf16[272,512]{1,0:T(8,128)(2,1)S(1)} %get-tuple-element.51.refs_2_.refs_0_, ...), custom_call_target="tpu_custom_call" | custom-call | flops 2990000128 | tf_op jit(solution)/shard_map/attend0/pallas_call | solution.py:45
  8.7 1.1 %local.1.refs_0_ = f32[2,128,1024]{2,1,0:T(8,128)S(1)} custom-call(bf16[2,128,1408]{2,1,0:T(8,128)(2,1)S(1)} %get-tuple-element.53.refs_0_.refs_2_, bf16[128,1024]{1,0:T(8,128)(2,1)S(1)} %get-tuple-element.54.refs_1_, f32[2,128,128]{2,1,0:T(8,128)S(1)} %get-tuple-element.55.refs_2_.refs_1_, f32[2,128,128]{2,1,0:T(8,128)S(1)} %get-tuple-element.56.refs_3_), custom_call_target="tpu_custom_call" | custom-call | flops 11500000 | tf_op jit(solution)/shard_map/local/pallas_call | solution.py:45
  9.7 0.8 %collective-permute-done.2.refs_1_ = bf16[144,512]{1,0:T(8,128)(2,1)S(1)} collective-permute-done((bf16[144,512]{1,0:T(8,128)(2,1)S(1)}, bf16[144,512]{1,0:T(8,128)(2,1)S(1)}, u32[]{:S(2)}, u32[]{:S(2)}) %collective-permute-start.2) | collective-permute-done | bytes 147488 | tf_op jit(solution)/shard_map/ppermute | solution.py:488
  10.6 0.1 row.1
  10.7 1.7 %collective-permute-start.3 = (bf16[144,512]{1,0:T(8,128)(2,1)S(1)}, bf16[144,512]{1,0:T(8,128)(2,1)S(1)}, u32[]{:S(2)}, u32[]{:S(2)}) collective-permute-start(bf16[144,512]{1,0:T(8,128)(2,1)S(1)} %get-tuple-element.59.refs_0_), channel_id=1, source_target_pairs={{0,4},{1,5},{2,6},{3,7},{4,8},{5,9},{6,10},{7,11},{8,12},{9,13},{1... | collective-permute-start | bytes 442376 | tf_op jit(solution)/shard_map/ppermute | solution.py:488
  12.3 0.0 collective-permute-done.5.refs_2_.refs_1_
  12.3 1.5 %collective-permute-start.6 = (bf16[272,512]{1,0:T(8,128)(2,1)S(1)}, bf16[272,512]{1,0:T(8,128)(2,1)S(1)}, u32[]{:S(2)}, u32[]{:S(2)}) collective-permute-start(bf16[272,512]{1,0:T(8,128)(2,1)S(1)} %collective-permute-done.5.refs_2_.refs_1_), channel_id=1, source_target_pairs={{0,1},{1,0},{2,3},{3,2},{4,5},{5,4},{6,7},{7,6},{8,9},{9,8},{10,11... | collective-permute-start | bytes 835592 | tf_op jit(solution)/shard_map/ppermute | solution.py:488
  13.9 1.3 %collective-permute-start.8 = (bf16[272,512]{1,0:T(8,128)(2,1)S(1)}, bf16[272,512]{1,0:T(8,128)(2,1)S(1)}, u32[]{:S(2)}, u32[]{:S(2)}) collective-permute-start(bf16[272,512]{1,0:T(8,128)(2,1)S(1)} %pick.1), channel_id=1, source_target_pairs={{0,2},{1,3},{2,0},{3,1},{4,6},{5,7},{6,4},{7,5},{8,10},{9,11},{10,... | collective-permute-start | bytes 835592 | tf_op jit(solution)/shard_map/ppermute | solution.py:488
  15.2 0.0 collective-permute-start.10
  15.2 0.0 collective-permute-done.3.refs_1_
  15.2 0.1 hop1.1
  15.3 1.3 %collective-permute-start.4 = (bf16[144,512]{1,0:T(8,128)(2,1)S(1)}, bf16[144,512]{1,0:T(8,128)(2,1)S(1)}, u32[]{:S(2)}, u32[]{:S(2)}) collective-permute-start(bf16[144,512]{1,0:T(8,128)(2,1)S(1)} %get-tuple-element.60.refs_0_), channel_id=1, source_target_pairs={{0,8},{1,9},{2,10},{3,11},{4,12},{5,13},{6,14},{7,15},{16,24},{17,... | collective-permute-start | bytes 442376 | tf_op jit(solution)/shard_map/ppermute | solution.py:492
  16.6 0.0 collective-permute-done.6.refs_3_
  16.6 1.9 %attend2.1 = (f32[2,128,2048]{2,1,0:T(8,128)S(1)}, f32[2,128,2048]{2,1,0:T(8,128)S(1)}, f32[2,128,2048]{2,1,0:T(8,128)S(1)}) custom-call(bf16[2,128,2048]{2,1,0:T(8,128)(2,1)S(1)} %copy-done, f32[128,128]{1,0:T(8,128)S(1)} %get-tuple-element.50.refs_1_, bf16[272,512]{1,0:T(8,128)(2,1)S(1)} %collective-permute-done.5.refs_2_.refs_1_, ...), custom_call_target="tpu_custom_call" | custom-call | flops 2990000128 | tf_op jit(solution)/shard_map/attend2/pallas_call | solution.py:45
  18.5 3.7 %collective-permute-done.8.refs_2_ = bf16[272,512]{1,0:T(8,128)(2,1)S(1)} collective-permute-done((bf16[272,512]{1,0:T(8,128)(2,1)S(1)}, bf16[272,512]{1,0:T(8,128)(2,1)S(1)}, u32[]{:S(2)}, u32[]{:S(2)}) %collective-permute-start.8) | collective-permute-done | bytes 278560 | tf_op jit(solution)/shard_map/ppermute | solution.py:488
  22.2 0.8 %collective-permute-start.9 = (bf16[272,512]{1,0:T(8,128)(2,1)S(1)}, bf16[272,512]{1,0:T(8,128)(2,1)S(1)}, u32[]{:S(2)}, u32[]{:S(2)}) collective-permute-start(bf16[272,512]{1,0:T(8,128)(2,1)S(1)} %collective-permute-done.8.refs_2_), channel_id=1, source_target_pairs={{0,1},{1,0},{2,3},{3,2},{4,5},{5,4},{6,7},{7,6},{8,9},{9,8},{10,11... | collective-permute-start | bytes 835592 | tf_op jit(solution)/shard_map/ppermute | solution.py:488
  23.0 0.0 collective-permute-start.13
  23.0 0.1 collective-permute-done.10.refs_4_
  23.2 4.9 %collective-permute-start.11 = (bf16[272,512]{1,0:T(8,128)(2,1)S(1)}, bf16[272,512]{1,0:T(8,128)(2,1)S(1)}, u32[]{:S(2)}, u32[]{:S(2)}) collective-permute-start(bf16[272,512]{1,0:T(8,128)(2,1)S(1)} %collective-permute-done.10.refs_4_), channel_id=1, source_target_pairs={{0,1},{1,0},{2,3},{3,2},{4,5},{5,4},{6,7},{7,6},{8,9},{9,8},{10,11... | collective-permute-start | bytes 835592 | tf_op jit(solution)/shard_map/ppermute | solution.py:488
  28.1 0.0 collective-permute-done.4.refs_2_
  28.1 0.1 hop2.1
  28.2 0.3 collective-permute-start.7
  28.5 0.0 collective-permute-done.9.refs_3_
  28.5 0.8 %collective-permute-done.11.refs_5_ = bf16[272,512]{1,0:T(8,128)(2,1)S(1)} collective-permute-done((bf16[272,512]{1,0:T(8,128)(2,1)S(1)}, bf16[272,512]{1,0:T(8,128)(2,1)S(1)}, u32[]{:S(2)}, u32[]{:S(2)}) %collective-permute-start.11) | collective-permute-done | bytes 278560 | tf_op jit(solution)/shard_map/ppermute | solution.py:488
  29.3 3.2 %attend4.1 = (f32[2,128,2048]{2,1,0:T(8,128)S(1)}, f32[2,128,2048]{2,1,0:T(8,128)S(1)}, f32[2,128,2048]{2,1,0:T(8,128)S(1)}) custom-call(bf16[2,128,2048]{2,1,0:T(8,128)(2,1)S(1)} %copy-done, f32[128,128]{1,0:T(8,128)S(1)} %get-tuple-element.50.refs_1_, bf16[272,512]{1,0:T(8,128)(2,1)S(1)} %collective-permute-done.8.refs_2_, ...), custom_call_target="tpu_custom_call" | custom-call | flops 5405000192 | tf_op jit(solution)/shard_map/attend4/pallas_call | solution.py:45
  32.5 3.0 %collective-permute-done.13.refs_2_ = bf16[272,512]{1,0:T(8,128)(2,1)S(1)} collective-permute-done((bf16[272,512]{1,0:T(8,128)(2,1)S(1)}, bf16[272,512]{1,0:T(8,128)(2,1)S(1)}, u32[]{:S(2)}, u32[]{:S(2)}) %collective-permute-start.13) | collective-permute-done | bytes 278560 | tf_op jit(solution)/shard_map/ppermute | solution.py:488
  35.5 1.1 %collective-permute-start.14 = (bf16[272,512]{1,0:T(8,128)(2,1)S(1)}, bf16[272,512]{1,0:T(8,128)(2,1)S(1)}, u32[]{:S(2)}, u32[]{:S(2)}) collective-permute-start(bf16[272,512]{1,0:T(8,128)(2,1)S(1)} %collective-permute-done.13.refs_2_), channel_id=1, source_target_pairs={{0,1},{1,0},{2,3},{3,2},{4,5},{5,4},{6,7},{7,6},{8,9},{9,8},{10,11... | collective-permute-start | bytes 835592 | tf_op jit(solution)/shard_map/ppermute | solution.py:488
  36.6 0.0 collective-permute-done.7.refs_4_
  36.6 0.9 %finish.1 = (bf16[128,1024]{1,0:T(8,128)(2,1)S(1)}, bf16[128,1024]{1,0:T(8,128)(2,1)S(1)}) custom-call(f32[2,128,1024]{2,1,0:T(8,128)S(1)} %local.1.refs_0_, f32[2,128,128]{2,1,0:T(8,128)S(1)} %get-tuple-element.55.refs_2_.refs_1_, bf16[2,128,1408]{2,1,0:T(8,128)(2,1)S(1)} %get-tuple-element.53.refs_0_.refs_2_, ...), custom_call_target="tpu_custom_call" | custom-call | flops 1955000064 | tf_op jit(solution)/shard_map/finish/pallas_call | solution.py:45
  37.5 0.1 collective-permute-start.12
  37.6 0.2 collective-permute-done.14.refs_3_
  37.7 2.6 %attend3.1 = bf16[2,128,2048]{2,1,0:T(8,128)(2,1)} custom-call(bf16[2,128,2048]{2,1,0:T(8,128)(2,1)S(1)} %copy-done, f32[128,128]{1,0:T(8,128)S(1)} %get-tuple-element.50.refs_1_, bf16[272,512]{1,0:T(8,128)(2,1)S(1)} %collective-permute-done.13.refs_2_, bf16[272,512]{1,0:T(8,128)(2,1)S(1)} %collective-permute-done.14.refs_3_, ...), custom_call_target="tpu_custom_call" | custom-call | flops 2990000128 | tf_op jit(solution)/shard_map/attend3/pallas_call | solution.py:45
  40.3 0.0 collective-permute-done.12.refs_1_
  40.3 0.8 %collect.1 = bf16[128,2048]{1,0:T(8,128)(2,1)} custom-call(bf16[128,1024]{1,0:T(8,128)(2,1)S(1)} %get-tuple-element.79.refs_0_, bf16[128,1024]{1,0:T(8,128)(2,1)S(1)} %collective-permute-done.12.refs_1_), custom_call_target="tpu_custom_call" | custom-call | flops 920000000 | tf_op jit(solution)/shard_map/collect/pallas_call | solution.py:45
  (1 shorter events, 0.0 us)
Async XLA Ops:
  2.1 2.1 %collective-permute-start = (bf16[128,1408]{1,0:T(8,128)(2,1)S(1)}, bf16[128,1408]{1,0:T(8,128)(2,1)S(1)}, u32[]{:S(2)}, u32[]{:S(2)}) collective-permute-start(bf16[128,1408]{1,0:T(8,128)(2,1)S(1)} %get-tuple-element.45), channel_id=1, source_target_pairs={{0,1},{1,0},{2,3},{3,2},{4,5},{5,4},{6,7},{7,6},{8,9},{9,8},{10,11... | collective-permute-start | bytes 1081352 | tf_op jit(solution)/shard_map/ppermute | solution.py:488
  2.8 4.3 %collective-permute-start.1 = (bf16[272,512]{1,0:T(8,128)(2,1)S(1)}, bf16[272,512]{1,0:T(8,128)(2,1)S(1)}, u32[]{:S(2)}, u32[]{:S(2)}) collective-permute-start(bf16[272,512]{1,0:T(8,128)(2,1)S(1)} %get-tuple-element.51.refs_2_.refs_0_), channel_id=1, source_target_pairs={{0,1},{1,0},{2,3},{3,2},{4,5},{5,4},{6,7},{7,6},{8,9},{9,8},{10,11... | collective-permute-start | bytes 835592 | tf_op jit(solution)/shard_map/ppermute | solution.py:488
  2.9 9.4 %collective-permute-start.5 = (bf16[272,512]{1,0:T(8,128)(2,1)S(1)}, bf16[272,512]{1,0:T(8,128)(2,1)S(1)}, u32[]{:S(2)}, u32[]{:S(2)}) collective-permute-start(bf16[272,512]{1,0:T(8,128)(2,1)S(1)} %get-tuple-element.51.refs_2_.refs_0_), channel_id=1, source_target_pairs={{0,4},{1,5},{2,6},{3,7},{4,8},{5,9},{6,10},{7,11},{8,12},{9,13},{1... | collective-permute-start | bytes 835592 | tf_op jit(solution)/shard_map/ppermute | solution.py:488
  4.2 2.9 %copy-start = (bf16[2,128,2048]{2,1,0:T(8,128)(2,1)S(1)}, bf16[2,128,2048]{2,1,0:T(8,128)(2,1)}, u32[]{:S(2)}) copy-start(bf16[2,128,2048]{2,1,0:T(8,128)(2,1)} %refs_0_.5) | copy-start | bytes 3145732
  5.8 4.7 %collective-permute-start.2 = (bf16[144,512]{1,0:T(8,128)(2,1)S(1)}, bf16[144,512]{1,0:T(8,128)(2,1)S(1)}, u32[]{:S(2)}, u32[]{:S(2)}) collective-permute-start(bf16[144,512]{1,0:T(8,128)(2,1)S(1)} %get-tuple-element.57), channel_id=1, source_target_pairs={{0,2},{1,3},{2,0},{3,1},{4,6},{5,7},{6,4},{7,5},{8,10},{9,11},{10,... | collective-permute-start | bytes 442376 | tf_op jit(solution)/shard_map/ppermute | solution.py:488
  10.7 4.5 %collective-permute-start.3 = (bf16[144,512]{1,0:T(8,128)(2,1)S(1)}, bf16[144,512]{1,0:T(8,128)(2,1)S(1)}, u32[]{:S(2)}, u32[]{:S(2)}) collective-permute-start(bf16[144,512]{1,0:T(8,128)(2,1)S(1)} %get-tuple-element.59.refs_0_), channel_id=1, source_target_pairs={{0,4},{1,5},{2,6},{3,7},{4,8},{5,9},{6,10},{7,11},{8,12},{9,13},{1... | collective-permute-start | bytes 442376 | tf_op jit(solution)/shard_map/ppermute | solution.py:488
  12.3 4.2 %collective-permute-start.6 = (bf16[272,512]{1,0:T(8,128)(2,1)S(1)}, bf16[272,512]{1,0:T(8,128)(2,1)S(1)}, u32[]{:S(2)}, u32[]{:S(2)}) collective-permute-start(bf16[272,512]{1,0:T(8,128)(2,1)S(1)} %collective-permute-done.5.refs_2_.refs_1_), channel_id=1, source_target_pairs={{0,1},{1,0},{2,3},{3,2},{4,5},{5,4},{6,7},{7,6},{8,9},{9,8},{10,11... | collective-permute-start | bytes 835592 | tf_op jit(solution)/shard_map/ppermute | solution.py:488
  13.9 8.4 %collective-permute-start.8 = (bf16[272,512]{1,0:T(8,128)(2,1)S(1)}, bf16[272,512]{1,0:T(8,128)(2,1)S(1)}, u32[]{:S(2)}, u32[]{:S(2)}) collective-permute-start(bf16[272,512]{1,0:T(8,128)(2,1)S(1)} %pick.1), channel_id=1, source_target_pairs={{0,2},{1,3},{2,0},{3,1},{4,6},{5,7},{6,4},{7,5},{8,10},{9,11},{10,... | collective-permute-start | bytes 835592 | tf_op jit(solution)/shard_map/ppermute | solution.py:488
  15.2 8.0 %collective-permute-start.10 = (bf16[272,512]{1,0:T(8,128)(2,1)S(1)}, bf16[272,512]{1,0:T(8,128)(2,1)S(1)}, u32[]{:S(2)}, u32[]{:S(2)}) collective-permute-start(bf16[272,512]{1,0:T(8,128)(2,1)S(1)} %collective-permute-done.5.refs_2_.refs_1_), channel_id=1, source_target_pairs={{0,4},{1,5},{2,6},{3,7},{4,8},{5,9},{6,10},{7,11},{8,12},{9,13},{1... | collective-permute-start | bytes 835592 | tf_op jit(solution)/shard_map/ppermute | solution.py:488
  15.3 12.8 %collective-permute-start.4 = (bf16[144,512]{1,0:T(8,128)(2,1)S(1)}, bf16[144,512]{1,0:T(8,128)(2,1)S(1)}, u32[]{:S(2)}, u32[]{:S(2)}) collective-permute-start(bf16[144,512]{1,0:T(8,128)(2,1)S(1)} %get-tuple-element.60.refs_0_), channel_id=1, source_target_pairs={{0,8},{1,9},{2,10},{3,11},{4,12},{5,13},{6,14},{7,15},{16,24},{17,... | collective-permute-start | bytes 442376 | tf_op jit(solution)/shard_map/ppermute | solution.py:492
  22.2 6.3 %collective-permute-start.9 = (bf16[272,512]{1,0:T(8,128)(2,1)S(1)}, bf16[272,512]{1,0:T(8,128)(2,1)S(1)}, u32[]{:S(2)}, u32[]{:S(2)}) collective-permute-start(bf16[272,512]{1,0:T(8,128)(2,1)S(1)} %collective-permute-done.8.refs_2_), channel_id=1, source_target_pairs={{0,1},{1,0},{2,3},{3,2},{4,5},{5,4},{6,7},{7,6},{8,9},{9,8},{10,11... | collective-permute-start | bytes 835592 | tf_op jit(solution)/shard_map/ppermute | solution.py:488
  23.0 12.5 %collective-permute-start.13 = (bf16[272,512]{1,0:T(8,128)(2,1)S(1)}, bf16[272,512]{1,0:T(8,128)(2,1)S(1)}, u32[]{:S(2)}, u32[]{:S(2)}) collective-permute-start(bf16[272,512]{1,0:T(8,128)(2,1)S(1)} %collective-permute-done.8.refs_2_), channel_id=1, source_target_pairs={{0,4},{1,5},{2,6},{3,7},{4,8},{5,9},{6,10},{7,11},{8,12},{9,13},{1... | collective-permute-start | bytes 835592 | tf_op jit(solution)/shard_map/ppermute | solution.py:488
  23.2 6.1 %collective-permute-start.11 = (bf16[272,512]{1,0:T(8,128)(2,1)S(1)}, bf16[272,512]{1,0:T(8,128)(2,1)S(1)}, u32[]{:S(2)}, u32[]{:S(2)}) collective-permute-start(bf16[272,512]{1,0:T(8,128)(2,1)S(1)} %collective-permute-done.10.refs_4_), channel_id=1, source_target_pairs={{0,1},{1,0},{2,3},{3,2},{4,5},{5,4},{6,7},{7,6},{8,9},{9,8},{10,11... | collective-permute-start | bytes 835592 | tf_op jit(solution)/shard_map/ppermute | solution.py:488
  28.2 8.4 %collective-permute-start.7 = (bf16[128,512]{1,0:T(8,128)(2,1)S(1)}, bf16[128,512]{1,0:T(8,128)(2,1)S(1)}, u32[]{:S(2)}, u32[]{:S(2)}) collective-permute-start(bf16[128,512]{1,0:T(8,128)(2,1)S(1)} %get-tuple-element.70), channel_id=1, source_target_pairs={{0,2},{1,3},{2,0},{3,1},{4,6},{5,7},{6,4},{7,5},{8,10},{9,11},{10,... | collective-permute-start | bytes 393224 | tf_op jit(solution)/shard_map/ppermute | solution.py:488
  35.5 2.3 %collective-permute-start.14 = (bf16[272,512]{1,0:T(8,128)(2,1)S(1)}, bf16[272,512]{1,0:T(8,128)(2,1)S(1)}, u32[]{:S(2)}, u32[]{:S(2)}) collective-permute-start(bf16[272,512]{1,0:T(8,128)(2,1)S(1)} %collective-permute-done.13.refs_2_), channel_id=1, source_target_pairs={{0,1},{1,0},{2,3},{3,2},{4,5},{5,4},{6,7},{7,6},{8,9},{9,8},{10,11... | collective-permute-start | bytes 835592 | tf_op jit(solution)/shard_map/ppermute | solution.py:488
  37.5 2.8 %collective-permute-start.12 = (bf16[128,1024]{1,0:T(8,128)(2,1)S(1)}, bf16[128,1024]{1,0:T(8,128)(2,1)S(1)}, u32[]{:S(2)}, u32[]{:S(2)}) collective-permute-start(bf16[128,1024]{1,0:T(8,128)(2,1)S(1)} %get-tuple-element.80), channel_id=1, source_target_pairs={{0,1},{1,0},{2,3},{3,2},{4,5},{5,4},{6,7},{7,6},{8,9},{9,8},{10,11... | collective-permute-start | bytes 786440 | tf_op jit(solution)/shard_map/ppermute | solution.py:488

commit v8 on v7

--- a/solution.py
+++ b/solution.py
@@ -69,14 +69,14 @@
     heads = codes.shape[0]
     half = x.shape[1] // 2
     copies = [
+        (codes, code_buf),
+        (seg, seg_buf),
+        (rate, rate_buf),
         (kv.at[0], own.at[0:tokens]),
         (kv.at[1], own.at[tokens : 2 * tokens]),
         (x.at[:, lanes(1 - core, half)], to_c.at[:, 0:half]),
         (write, to_c.at[:, half : half + state]),
         (read, to_c.at[:, half + state : half + 2 * state]),
-        (codes, code_buf),
-        (seg, seg_buf),
-        (rate, rate_buf),
         (x.at[:, lanes(core, half)], mine.at[:, 0:half]),
         (write, mine.at[:, half : half + state]),
         (read, mine.at[:, half + state : half + 2 * state]),
@@ -88,7 +88,7 @@
     for copy in copies:
         copy.start()
     own[2 * tokens :, tokens:] = jnp.zeros((16, own.shape[1] - tokens), BF16)
-    for copy in copies:
+    for copy in copies[:3]:
         copy.wait()
     codes_of = (seg_buf[...] + 1).astype(F32).astype(BF16)
     own[2 * tokens :, 0:tokens] = jnp.broadcast_to(codes_of, (16, tokens))
@@ -101,6 +101,8 @@
     mine[:, half + 2 * state :] = both
     to_c[:, half + 2 * state :] = both
     rates[...] = jnp.concatenate([rate_buf[...], jnp.zeros((1, 128 - heads), F32)], axis=1)
+    for copy in copies[3:]:
+        copy.wait()
 
 
 def attend_kernel(kinds, first, last, place, q_ref, doc_ref, *refs):
@@ -465,11 +467,17 @@
             out_ref[:, part] = (tile * lax.rsqrt(mean + 1e-05)).astype(BF16)
 
 
-def collect_kernel(place, self_ref, c_ref, out_ref):
+def collect_kernel(place, self_ref, c_ref, out_ref, sems):
     core = place[0]
     cols = self_ref.shape[1]
-    out_ref[:, lanes(core, cols)] = self_ref[...]
-    out_ref[:, lanes(1 - core, cols)] = c_ref[...]
+    copies = [
+        pltpu.make_async_copy(self_ref, out_ref.at[:, lanes(core, cols)], sems.at[0]),
+        pltpu.make_async_copy(c_ref, out_ref.at[:, lanes(1 - core, cols)], sems.at[1]),
+    ]
+    for copy in copies:
+        copy.start()
+    for copy in copies:
+        copy.wait()
 
 
 def after(value, *others):
@@ -565,7 +573,7 @@
     behind2 = after(behind2, span)
     to_y = call(pick, "pick", 20.0, [own, behind2], shaped(2 * tokens + 16, kv_width))
     behind1 = send(to_y, swap_y)
-    behind4 = send(after(behind2, to_y), up(1))
+    behind4 = send(behind2, up(1))
     behind2c = send(behind2, swap_c)
     before = None
     distance = 1
@@ -631,6 +639,8 @@
         0.8,
         [done, after(back_c, attn_output)],
         shaped(tokens, channels),
+        [pltpu.SemaphoreType.DMA((2,))],
+        leaves=True,
     )
     return (ssm_output, attn_output)
 

time: 41.3 us -> 40.7 us (0.985)
  the two profiles are of different devices: /device:TPU:17 before, /device:TPU:23 now
where the time goes in v8:
time: 40.7 us; the launch traced here: 40.4 us
  Pallas kernels  15.2 us (37%)
  starting transfers between devices  13.7 us (34%)
  waiting for transfers between devices  10.6 us (26%)
  between operations  0.9 us (2%)
    pallas_call x13, Pallas kernels, call(): pl.pallas_call(placed, name=name, out_shape=outs, in_specs=[spec] * len(a...  15.2 us
    ppermute x14, starting transfers between devices, shards(): lax.ppermute(x, 'seq', [(i, route(i)) for i in range(devices)])  12.4 us
    ppermute x14, waiting for transfers between devices, shards(): lax.ppermute(x, 'seq', [(i, route(i)) for i in range(devices)])  10.6 us
    ppermute x1, starting transfers between devices, shards(): lax.ppermute(x, 'seq', [(i, i + n * ROW) for i in range(devices - n * ROW)])  1.29 us
  transfers between devices with their start and end apart: 15, of which 6 were waited for; matrix products, arithmetic and copies ran while one was open for 0% of the time, Pallas kernels for 32%

profile of v8, /device:TPU:23, one launch (start us, length us, event | category | flops | bytes accessed | tf_op | source)
XLA Modules:
  0.0 40.4 jit_solution(17868084088858112213)
XLA Ops:
  0.6 1.3 %pack.1 = (bf16[272,512]{1,0:T(8,128)(2,1)S(1)}, f32[128,128]{1,0:T(8,128)S(1)}, bf16[128,1408]{1,0:T(8,128)(2,1)S(1)}, bf16[128,1408]{1,0:T(8,128)(2,1)S(1)}, f32[1,128]{1,0:T(1,128)S(1)}) custom-call(bf16[128,2048]{1,0:T(8,128)(2,1)} %refs_0_.1, bf16[128,128]{1,0:T(8,128)(2,1)} %refs_1_.1, bf16[128,128]{1,0:T(8,128)(2,1)} %refs_2_.1, s32[32,128]{1,0:T(8,128)} %bitcast.3, ...), custom_call_target="tpu_custom_call" | custom-call | flops 1724999936 | tf_op jit(solution)/shard_map/pack/pallas_call | solution.py:45
  2.0 0.7 %collective-permute-start = (bf16[128,1408]{1,0:T(8,128)(2,1)S(1)}, bf16[128,1408]{1,0:T(8,128)(2,1)S(1)}, u32[]{:S(2)}, u32[]{:S(2)}) collective-permute-start(bf16[128,1408]{1,0:T(8,128)(2,1)S(1)} %get-tuple-element.44), channel_id=1, source_target_pairs={{0,1},{1,0},{2,3},{3,2},{4,5},{5,4},{6,7},{7,6},{8,9},{9,8},{10,11... | collective-permute-start | bytes 1081352 | tf_op jit(solution)/shard_map/ppermute | solution.py:496
  2.7 0.1 collective-permute-start.1
  2.8 1.3 %collective-permute-start.5 = (bf16[272,512]{1,0:T(8,128)(2,1)S(1)}, bf16[272,512]{1,0:T(8,128)(2,1)S(1)}, u32[]{:S(2)}, u32[]{:S(2)}) collective-permute-start(bf16[272,512]{1,0:T(8,128)(2,1)S(1)} %get-tuple-element.50.refs_2_.refs_0_), channel_id=1, source_target_pairs={{0,4},{1,5},{2,6},{3,7},{4,8},{5,9},{6,10},{7,11},{8,12},{9,13},{1... | collective-permute-start | bytes 835592 | tf_op jit(solution)/shard_map/ppermute | solution.py:496
  4.1 0.0 collective-permute-done.refs_1_
  4.1 0.0 copy-start
  4.1 1.6 %states.1 = (bf16[144,512]{1,0:T(8,128)(2,1)S(1)}, bf16[144,512]{1,0:T(8,128)(2,1)S(1)}, bf16[128,1024]{1,0:T(8,128)(2,1)S(1)}, f32[2,128,128]{2,1,0:T(8,128)S(1...) custom-call(bf16[128,1408]{1,0:T(8,128)(2,1)S(1)} %get-tuple-element.43.refs_0_, ...), custom_call_target="tpu_custom_call" | custom-call | flops 2300000000 | tf_op jit(solution)/shard_map/states/pallas_call | solution.py:45
  5.7 0.3 collective-permute-start.2
  6.0 0.0 collective-permute-done.1.refs_3_
  6.0 0.0 copy-done
  6.0 1.5 %attend0.1 = (f32[2,128,2048]{2,1,0:T(8,128)S(1)}, f32[2,128,2048]{2,1,0:T(8,128)S(1)}, f32[2,128,2048]{2,1,0:T(8,128)S(1)}) custom-call(bf16[2,128,2048]{2,1,0:T(8,128)(2,1)S(1)} %copy-done, f32[128,128]{1,0:T(8,128)S(1)} %get-tuple-element.49.refs_1_, bf16[272,512]{1,0:T(8,128)(2,1)S(1)} %get-tuple-element.50.refs_2_.refs_0_, ...), custom_call_target="tpu_custom_call" | custom-call | flops 2990000128 | tf_op jit(solution)/shard_map/attend0/pallas_call | solution.py:45
  7.5 1.1 %local.1.refs_0_ = f32[2,128,1024]{2,1,0:T(8,128)S(1)} custom-call(bf16[2,128,1408]{2,1,0:T(8,128)(2,1)S(1)} %get-tuple-element.52.refs_0_.refs_2_, bf16[128,1024]{1,0:T(8,128)(2,1)S(1)} %get-tuple-element.53.refs_1_, f32[2,128,128]{2,1,0:T(8,128)S(1)} %get-tuple-element.54.refs_2_.refs_1_, f32[2,128,128]{2,1,0:T(8,128)S(1)} %get-tuple-element.55.refs_3_), custom_call_target="tpu_custom_call" | custom-call | flops 11500000 | tf_op jit(solution)/shard_map/local/pallas_call | solution.py:45
  8.6 1.9 %collective-permute-done.2.refs_1_ = bf16[144,512]{1,0:T(8,128)(2,1)S(1)} collective-permute-done((bf16[144,512]{1,0:T(8,128)(2,1)S(1)}, bf16[144,512]{1,0:T(8,128)(2,1)S(1)}, u32[]{:S(2)}, u32[]{:S(2)}) %collective-permute-start.2) | collective-permute-done | bytes 147488 | tf_op jit(solution)/shard_map/ppermute | solution.py:496
  10.5 0.1 row.1
  10.6 1.7 %collective-permute-start.3 = (bf16[144,512]{1,0:T(8,128)(2,1)S(1)}, bf16[144,512]{1,0:T(8,128)(2,1)S(1)}, u32[]{:S(2)}, u32[]{:S(2)}) collective-permute-start(bf16[144,512]{1,0:T(8,128)(2,1)S(1)} %get-tuple-element.58.refs_0_), channel_id=1, source_target_pairs={{0,4},{1,5},{2,6},{3,7},{4,8},{5,9},{6,10},{7,11},{8,12},{9,13},{1... | collective-permute-start | bytes 442376 | tf_op jit(solution)/shard_map/ppermute | solution.py:496
  12.2 0.0 collective-permute-done.5.refs_2_.refs_1_
  12.2 1.5 %collective-permute-start.6 = (bf16[272,512]{1,0:T(8,128)(2,1)S(1)}, bf16[272,512]{1,0:T(8,128)(2,1)S(1)}, u32[]{:S(2)}, u32[]{:S(2)}) collective-permute-start(bf16[272,512]{1,0:T(8,128)(2,1)S(1)} %collective-permute-done.5.refs_2_.refs_1_), channel_id=1, source_target_pairs={{0,1},{1,0},{2,3},{3,2},{4,5},{5,4},{6,7},{7,6},{8,9},{9,8},{10,11... | collective-permute-start | bytes 835592 | tf_op jit(solution)/shard_map/ppermute | solution.py:496
  13.7 0.0 collective-permute-start.10
  13.8 0.3 collective-permute-start.8
  14.1 0.6 %collective-permute-done.3.refs_1_ = bf16[144,512]{1,0:T(8,128)(2,1)S(1)} collective-permute-done((bf16[144,512]{1,0:T(8,128)(2,1)S(1)}, bf16[144,512]{1,0:T(8,128)(2,1)S(1)}, u32[]{:S(2)}, u32[]{:S(2)}) %collective-permute-start.3) | collective-permute-done | bytes 147488 | tf_op jit(solution)/shard_map/ppermute | solution.py:496
  14.6 0.1 hop1.1
  14.7 1.3 %collective-permute-start.4 = (bf16[144,512]{1,0:T(8,128)(2,1)S(1)}, bf16[144,512]{1,0:T(8,128)(2,1)S(1)}, u32[]{:S(2)}, u32[]{:S(2)}) collective-permute-start(bf16[144,512]{1,0:T(8,128)(2,1)S(1)} %get-tuple-element.59.refs_0_), channel_id=1, source_target_pairs={{0,8},{1,9},{2,10},{3,11},{4,12},{5,13},{6,14},{7,15},{16,24},{17,... | collective-permute-start | bytes 442376 | tf_op jit(solution)/shard_map/ppermute | solution.py:500
  16.0 0.0 collective-permute-done.6.refs_3_
  16.0 1.9 %attend2.1 = (f32[2,128,2048]{2,1,0:T(8,128)S(1)}, f32[2,128,2048]{2,1,0:T(8,128)S(1)}, f32[2,128,2048]{2,1,0:T(8,128)S(1)}) custom-call(bf16[2,128,2048]{2,1,0:T(8,128)(2,1)S(1)} %copy-done, f32[128,128]{1,0:T(8,128)S(1)} %get-tuple-element.49.refs_1_, bf16[272,512]{1,0:T(8,128)(2,1)S(1)} %collective-permute-done.5.refs_2_.refs_1_, ...), custom_call_target="tpu_custom_call" | custom-call | flops 2990000128 | tf_op jit(solution)/shard_map/attend2/pallas_call | solution.py:45
  17.9 3.9 %collective-permute-done.8.refs_2_ = bf16[272,512]{1,0:T(8,128)(2,1)S(1)} collective-permute-done((bf16[272,512]{1,0:T(8,128)(2,1)S(1)}, bf16[272,512]{1,0:T(8,128)(2,1)S(1)}, u32[]{:S(2)}, u32[]{:S(2)}) %collective-permute-start.8) | collective-permute-done | bytes 278560 | tf_op jit(solution)/shard_map/ppermute | solution.py:496
  21.8 1.1 %collective-permute-start.9 = (bf16[272,512]{1,0:T(8,128)(2,1)S(1)}, bf16[272,512]{1,0:T(8,128)(2,1)S(1)}, u32[]{:S(2)}, u32[]{:S(2)}) collective-permute-start(bf16[272,512]{1,0:T(8,128)(2,1)S(1)} %collective-permute-done.8.refs_2_), channel_id=1, source_target_pairs={{0,1},{1,0},{2,3},{3,2},{4,5},{5,4},{6,7},{7,6},{8,9},{9,8},{10,11... | collective-permute-start | bytes 835592 | tf_op jit(solution)/shard_map/ppermute | solution.py:496
  22.9 1.3 %collective-permute-start.13 = (bf16[272,512]{1,0:T(8,128)(2,1)S(1)}, bf16[272,512]{1,0:T(8,128)(2,1)S(1)}, u32[]{:S(2)}, u32[]{:S(2)}) collective-permute-start(bf16[272,512]{1,0:T(8,128)(2,1)S(1)} %collective-permute-done.8.refs_2_), channel_id=1, source_target_pairs={{0,4},{1,5},{2,6},{3,7},{4,8},{5,9},{6,10},{7,11},{8,12},{9,13},{1... | collective-permute-start | bytes 835592 | tf_op jit(solution)/shard_map/ppermute | solution.py:496
  24.2 0.0 collective-permute-done.10.refs_4_
  24.2 2.8 %collective-permute-start.11 = (bf16[272,512]{1,0:T(8,128)(2,1)S(1)}, bf16[272,512]{1,0:T(8,128)(2,1)S(1)}, u32[]{:S(2)}, u32[]{:S(2)}) collective-permute-start(bf16[272,512]{1,0:T(8,128)(2,1)S(1)} %collective-permute-done.10.refs_4_), channel_id=1, source_target_pairs={{0,1},{1,0},{2,3},{3,2},{4,5},{5,4},{6,7},{7,6},{8,9},{9,8},{10,11... | collective-permute-start | bytes 835592 | tf_op jit(solution)/shard_map/ppermute | solution.py:496
  27.0 0.0 collective-permute-done.4.refs_2_
  27.0 0.1 hop2.1
  27.1 0.3 collective-permute-start.7
  27.4 0.8 %collective-permute-done.11.refs_5_ = bf16[272,512]{1,0:T(8,128)(2,1)S(1)} collective-permute-done((bf16[272,512]{1,0:T(8,128)(2,1)S(1)}, bf16[272,512]{1,0:T(8,128)(2,1)S(1)}, u32[]{:S(2)}, u32[]{:S(2)}) %collective-permute-start.11) | collective-permute-done | bytes 278560 | tf_op jit(solution)/shard_map/ppermute | solution.py:496
  28.2 0.0 collective-permute-done.9.refs_3_
  28.2 3.2 %attend4.1 = (f32[2,128,2048]{2,1,0:T(8,128)S(1)}, f32[2,128,2048]{2,1,0:T(8,128)S(1)}, f32[2,128,2048]{2,1,0:T(8,128)S(1)}) custom-call(bf16[2,128,2048]{2,1,0:T(8,128)(2,1)S(1)} %copy-done, f32[128,128]{1,0:T(8,128)S(1)} %get-tuple-element.49.refs_1_, bf16[272,512]{1,0:T(8,128)(2,1)S(1)} %collective-permute-done.8.refs_2_, ...), custom_call_target="tpu_custom_call" | custom-call | flops 5405000192 | tf_op jit(solution)/shard_map/attend4/pallas_call | solution.py:45
  31.4 3.4 %collective-permute-done.13.refs_2_ = bf16[272,512]{1,0:T(8,128)(2,1)S(1)} collective-permute-done((bf16[272,512]{1,0:T(8,128)(2,1)S(1)}, bf16[272,512]{1,0:T(8,128)(2,1)S(1)}, u32[]{:S(2)}, u32[]{:S(2)}) %collective-permute-start.13) | collective-permute-done | bytes 278560 | tf_op jit(solution)/shard_map/ppermute | solution.py:496
  34.7 0.9 %collective-permute-start.14 = (bf16[272,512]{1,0:T(8,128)(2,1)S(1)}, bf16[272,512]{1,0:T(8,128)(2,1)S(1)}, u32[]{:S(2)}, u32[]{:S(2)}) collective-permute-start(bf16[272,512]{1,0:T(8,128)(2,1)S(1)} %collective-permute-done.13.refs_2_), channel_id=1, source_target_pairs={{0,1},{1,0},{2,3},{3,2},{4,5},{5,4},{6,7},{7,6},{8,9},{9,8},{10,11... | collective-permute-start | bytes 835592 | tf_op jit(solution)/shard_map/ppermute | solution.py:496
  35.7 0.0 collective-permute-done.7.refs_4_
  35.7 0.9 %finish.1 = (bf16[128,1024]{1,0:T(8,128)(2,1)S(1)}, bf16[128,1024]{1,0:T(8,128)(2,1)S(1)}) custom-call(f32[2,128,1024]{2,1,0:T(8,128)S(1)} %local.1.refs_0_, f32[2,128,128]{2,1,0:T(8,128)S(1)} %get-tuple-element.54.refs_2_.refs_1_, bf16[2,128,1408]{2,1,0:T(8,128)(2,1)S(1)} %get-tuple-element.52.refs_0_.refs_2_, ...), custom_call_target="tpu_custom_call" | custom-call | flops 1955000064 | tf_op jit(solution)/shard_map/finish/pallas_call | solution.py:45
  36.6 0.1 collective-permute-start.12
  36.7 0.2 collective-permute-done.14.refs_3_
  36.8 2.6 %attend3.1 = bf16[2,128,2048]{2,1,0:T(8,128)(2,1)} custom-call(bf16[2,128,2048]{2,1,0:T(8,128)(2,1)S(1)} %copy-done, f32[128,128]{1,0:T(8,128)S(1)} %get-tuple-element.49.refs_1_, bf16[272,512]{1,0:T(8,128)(2,1)S(1)} %collective-permute-done.13.refs_2_, bf16[272,512]{1,0:T(8,128)(2,1)S(1)} %collective-permute-done.14.refs_3_, ...), custom_call_target="tpu_custom_call" | custom-call | flops 2990000128 | tf_op jit(solution)/shard_map/attend3/pallas_call | solution.py:45
  39.4 0.0 collective-permute-done.12.refs_1_
  39.4 0.8 %collect.1 = bf16[128,2048]{1,0:T(8,128)(2,1)} custom-call(bf16[128,1024]{1,0:T(8,128)(2,1)S(1)} %get-tuple-element.77.refs_0_, bf16[128,1024]{1,0:T(8,128)(2,1)S(1)} %collective-permute-done.12.refs_1_), custom_call_target="tpu_custom_call" | custom-call | flops 920000000 | tf_op jit(solution)/shard_map/collect/pallas_call | solution.py:45
  (1 shorter events, 0.0 us)
Async XLA Ops:
  2.0 2.1 %collective-permute-start = (bf16[128,1408]{1,0:T(8,128)(2,1)S(1)}, bf16[128,1408]{1,0:T(8,128)(2,1)S(1)}, u32[]{:S(2)}, u32[]{:S(2)}) collective-permute-start(bf16[128,1408]{1,0:T(8,128)(2,1)S(1)} %get-tuple-element.44), channel_id=1, source_target_pairs={{0,1},{1,0},{2,3},{3,2},{4,5},{5,4},{6,7},{7,6},{8,9},{9,8},{10,11... | collective-permute-start | bytes 1081352 | tf_op jit(solution)/shard_map/ppermute | solution.py:496
  2.7 3.3 %collective-permute-start.1 = (bf16[272,512]{1,0:T(8,128)(2,1)S(1)}, bf16[272,512]{1,0:T(8,128)(2,1)S(1)}, u32[]{:S(2)}, u32[]{:S(2)}) collective-permute-start(bf16[272,512]{1,0:T(8,128)(2,1)S(1)} %get-tuple-element.50.refs_2_.refs_0_), channel_id=1, source_target_pairs={{0,1},{1,0},{2,3},{3,2},{4,5},{5,4},{6,7},{7,6},{8,9},{9,8},{10,11... | collective-permute-start | bytes 835592 | tf_op jit(solution)/shard_map/ppermute | solution.py:496
  2.8 9.4 %collective-permute-start.5 = (bf16[272,512]{1,0:T(8,128)(2,1)S(1)}, bf16[272,512]{1,0:T(8,128)(2,1)S(1)}, u32[]{:S(2)}, u32[]{:S(2)}) collective-permute-start(bf16[272,512]{1,0:T(8,128)(2,1)S(1)} %get-tuple-element.50.refs_2_.refs_0_), channel_id=1, source_target_pairs={{0,4},{1,5},{2,6},{3,7},{4,8},{5,9},{6,10},{7,11},{8,12},{9,13},{1... | collective-permute-start | bytes 835592 | tf_op jit(solution)/shard_map/ppermute | solution.py:496
  4.1 1.9 %copy-start = (bf16[2,128,2048]{2,1,0:T(8,128)(2,1)S(1)}, bf16[2,128,2048]{2,1,0:T(8,128)(2,1)}, u32[]{:S(2)}) copy-start(bf16[2,128,2048]{2,1,0:T(8,128)(2,1)} %refs_0_.5) | copy-start | bytes 3145732
  5.7 4.7 %collective-permute-start.2 = (bf16[144,512]{1,0:T(8,128)(2,1)S(1)}, bf16[144,512]{1,0:T(8,128)(2,1)S(1)}, u32[]{:S(2)}, u32[]{:S(2)}) collective-permute-start(bf16[144,512]{1,0:T(8,128)(2,1)S(1)} %get-tuple-element.56), channel_id=1, source_target_pairs={{0,2},{1,3},{2,0},{3,1},{4,6},{5,7},{6,4},{7,5},{8,10},{9,11},{10,... | collective-permute-start | bytes 442376 | tf_op jit(solution)/shard_map/ppermute | solution.py:496
  10.6 4.0 %collective-permute-start.3 = (bf16[144,512]{1,0:T(8,128)(2,1)S(1)}, bf16[144,512]{1,0:T(8,128)(2,1)S(1)}, u32[]{:S(2)}, u32[]{:S(2)}) collective-permute-start(bf16[144,512]{1,0:T(8,128)(2,1)S(1)} %get-tuple-element.58.refs_0_), channel_id=1, source_target_pairs={{0,4},{1,5},{2,6},{3,7},{4,8},{5,9},{6,10},{7,11},{8,12},{9,13},{1... | collective-permute-start | bytes 442376 | tf_op jit(solution)/shard_map/ppermute | solution.py:496
  12.2 3.8 %collective-permute-start.6 = (bf16[272,512]{1,0:T(8,128)(2,1)S(1)}, bf16[272,512]{1,0:T(8,128)(2,1)S(1)}, u32[]{:S(2)}, u32[]{:S(2)}) collective-permute-start(bf16[272,512]{1,0:T(8,128)(2,1)S(1)} %collective-permute-done.5.refs_2_.refs_1_), channel_id=1, source_target_pairs={{0,1},{1,0},{2,3},{3,2},{4,5},{5,4},{6,7},{7,6},{8,9},{9,8},{10,11... | collective-permute-start | bytes 835592 | tf_op jit(solution)/shard_map/ppermute | solution.py:496
  13.7 10.5 %collective-permute-start.10 = (bf16[272,512]{1,0:T(8,128)(2,1)S(1)}, bf16[272,512]{1,0:T(8,128)(2,1)S(1)}, u32[]{:S(2)}, u32[]{:S(2)}) collective-permute-start(bf16[272,512]{1,0:T(8,128)(2,1)S(1)} %collective-permute-done.5.refs_2_.refs_1_), channel_id=1, source_target_pairs={{0,4},{1,5},{2,6},{3,7},{4,8},{5,9},{6,10},{7,11},{8,12},{9,13},{1... | collective-permute-start | bytes 835592 | tf_op jit(solution)/shard_map/ppermute | solution.py:496
  13.8 8.0 %collective-permute-start.8 = (bf16[272,512]{1,0:T(8,128)(2,1)S(1)}, bf16[272,512]{1,0:T(8,128)(2,1)S(1)}, u32[]{:S(2)}, u32[]{:S(2)}) collective-permute-start(bf16[272,512]{1,0:T(8,128)(2,1)S(1)} %pick.1), channel_id=1, source_target_pairs={{0,2},{1,3},{2,0},{3,1},{4,6},{5,7},{6,4},{7,5},{8,10},{9,11},{10,... | collective-permute-start | bytes 835592 | tf_op jit(solution)/shard_map/ppermute | solution.py:496
  14.7 12.3 %collective-permute-start.4 = (bf16[144,512]{1,0:T(8,128)(2,1)S(1)}, bf16[144,512]{1,0:T(8,128)(2,1)S(1)}, u32[]{:S(2)}, u32[]{:S(2)}) collective-permute-start(bf16[144,512]{1,0:T(8,128)(2,1)S(1)} %get-tuple-element.59.refs_0_), channel_id=1, source_target_pairs={{0,8},{1,9},{2,10},{3,11},{4,12},{5,13},{6,14},{7,15},{16,24},{17,... | collective-permute-start | bytes 442376 | tf_op jit(solution)/shard_map/ppermute | solution.py:500
  21.8 6.4 %collective-permute-start.9 = (bf16[272,512]{1,0:T(8,128)(2,1)S(1)}, bf16[272,512]{1,0:T(8,128)(2,1)S(1)}, u32[]{:S(2)}, u32[]{:S(2)}) collective-permute-start(bf16[272,512]{1,0:T(8,128)(2,1)S(1)} %collective-permute-done.8.refs_2_), channel_id=1, source_target_pairs={{0,1},{1,0},{2,3},{3,2},{4,5},{5,4},{6,7},{7,6},{8,9},{9,8},{10,11... | collective-permute-start | bytes 835592 | tf_op jit(solution)/shard_map/ppermute | solution.py:496
  22.9 11.8 %collective-permute-start.13 = (bf16[272,512]{1,0:T(8,128)(2,1)S(1)}, bf16[272,512]{1,0:T(8,128)(2,1)S(1)}, u32[]{:S(2)}, u32[]{:S(2)}) collective-permute-start(bf16[272,512]{1,0:T(8,128)(2,1)S(1)} %collective-permute-done.8.refs_2_), channel_id=1, source_target_pairs={{0,4},{1,5},{2,6},{3,7},{4,8},{5,9},{6,10},{7,11},{8,12},{9,13},{1... | collective-permute-start | bytes 835592 | tf_op jit(solution)/shard_map/ppermute | solution.py:496
  24.2 4.0 %collective-permute-start.11 = (bf16[272,512]{1,0:T(8,128)(2,1)S(1)}, bf16[272,512]{1,0:T(8,128)(2,1)S(1)}, u32[]{:S(2)}, u32[]{:S(2)}) collective-permute-start(bf16[272,512]{1,0:T(8,128)(2,1)S(1)} %collective-permute-done.10.refs_4_), channel_id=1, source_target_pairs={{0,1},{1,0},{2,3},{3,2},{4,5},{5,4},{6,7},{7,6},{8,9},{9,8},{10,11... | collective-permute-start | bytes 835592 | tf_op jit(solution)/shard_map/ppermute | solution.py:496
  27.1 8.5 %collective-permute-start.7 = (bf16[128,512]{1,0:T(8,128)(2,1)S(1)}, bf16[128,512]{1,0:T(8,128)(2,1)S(1)}, u32[]{:S(2)}, u32[]{:S(2)}) collective-permute-start(bf16[128,512]{1,0:T(8,128)(2,1)S(1)} %get-tuple-element.69), channel_id=1, source_target_pairs={{0,2},{1,3},{2,0},{3,1},{4,6},{5,7},{6,4},{7,5},{8,10},{9,11},{10,... | collective-permute-start | bytes 393224 | tf_op jit(solution)/shard_map/ppermute | solution.py:496
  34.7 2.1 %collective-permute-start.14 = (bf16[272,512]{1,0:T(8,128)(2,1)S(1)}, bf16[272,512]{1,0:T(8,128)(2,1)S(1)}, u32[]{:S(2)}, u32[]{:S(2)}) collective-permute-start(bf16[272,512]{1,0:T(8,128)(2,1)S(1)} %collective-permute-done.13.refs_2_), channel_id=1, source_target_pairs={{0,1},{1,0},{2,3},{3,2},{4,5},{5,4},{6,7},{7,6},{8,9},{9,8},{10,11... | collective-permute-start | bytes 835592 | tf_op jit(solution)/shard_map/ppermute | solution.py:496
  36.6 2.8 %collective-permute-start.12 = (bf16[128,1024]{1,0:T(8,128)(2,1)S(1)}, bf16[128,1024]{1,0:T(8,128)(2,1)S(1)}, u32[]{:S(2)}, u32[]{:S(2)}) collective-permute-start(bf16[128,1024]{1,0:T(8,128)(2,1)S(1)} %get-tuple-element.78), channel_id=1, source_target_pairs={{0,1},{1,0},{2,3},{3,2},{4,5},{5,4},{6,7},{7,6},{8,9},{9,8},{10,11... | collective-permute-start | bytes 786440 | tf_op jit(solution)/shard_map/ppermute | solution.py:496
